TPU v7x, 256 devices: a whole 4x4x8 slice. The times are simulated.
256 devices in a mesh: patch: 128 (over y, z, x_hi, core), lat: 2 (over x_lo).
Axes of the slice: x: 4 (x_hi: 2, x_lo: 2; x = x_hi * 2 + x_lo), y: 4, z: 8, core: 2. Of those that a mesh axis runs over, the one named last changes fastest.
Arguments:
- node_latents: bfloat16 [24576, 512], P('patch', 'lat'), may hold values from -6 to 6
- edge_latents: bfloat16 [196608, 512], P('patch', 'lat'), may hold values from -6 to 6
- senders: int32 [1536, 128], P('patch'), may hold values from 0 to 24575, as said below
- receivers: int32 [1536, 128], P('patch'), may hold values from 0 to 24575, as said below
- long_count: int32 [128], P('patch'), may hold values from 1 to 384, 24576 in all
- edge_inner: bfloat16 [3, 512, 512], P(None, 'lat'), may hold values from -0.15625 to 0.15625
- edge_outer: bfloat16 [512, 512], P('lat'), may hold values from -0.25 to 0.25
- node_inner: bfloat16 [2, 512, 512], P(None, 'lat'), may hold values from -0.1875 to 0.1875
- node_outer: bfloat16 [512, 512], P('lat'), may hold values from -0.25 to 0.25
- node_cotangent: bfloat16 [24576, 512], P('patch', 'lat'), may hold values from -3 to 3
- edge_cotangent: bfloat16 [196608, 512], P('patch', 'lat'), may hold values from -3 to 3
Outputs:
- edge_output: bfloat16 [196608, 512], P('patch', 'lat')
- node_output: bfloat16 [24576, 512], P('patch', 'lat')
- edge_grads: bfloat16 [196608, 512], P('patch', 'lat')
- node_grads: bfloat16 [24576, 512], P('patch', 'lat')
- edgeinner_grad: float32 [3, 512, 512], P(None, 'lat')
- edgeouter_grad: float32 [512, 512], P('lat')
- nodeinner_grad: float32 [2, 512, 512], P(None, 'lat')
- nodeouter_grad: float32 [512, 512], P('lat')
Inputs may be any that keep to these rules, and one draw needn't show every extreme that they name: `senders`: patch p holds nodes p*192 to (p+1)*192 - 1. The sender of each of a patch's first 1152 slots is 1 to 32 nodes away from its receiver, counted cyclically over all 24576 nodes; the sender of each long slot is a coarse node, a node whose index within its patch is below 8. Every slot's receiver is a node of the slot's own patch; long slots' receivers are coarse nodes of that patch. The first long_count[p] of patch p's 384 long slots are live.
All inputs are finite; a program needn't handle non-finite values. No bound on the sum of `long_count` on one device may be relied on, other than what follows from the above.
Results may differ from a plain program's by a relative error of at most 0.014.
Values may be sent and summed in bfloat16 or wider, within the bound.
No kernel may reach another device: no remote copies, remote signals or barrier semaphores. Data moves between devices by JAX's collectives and lax.ppermute only.
A program may use at most 128 MiB of HBM per device.

v0:
```python
import jax
import jax.numpy as jnp
from jax import lax
from jax.sharding import PartitionSpec as P

HALO = 32
COARSE_DEV = 8
FINE_DEV = 1152


EPSILON = 1e-05


def with_halo(block, sides, width):
    for axis, dim in sides:
        count = lax.axis_size(axis)
        forward = [(i, i + 1) for i in range(count - 1)]
        forward.append((count - 1, 0))
        backward = [(target, source) for source, target in forward]
        low = lax.ppermute(
            lax.slice_in_dim(block, block.shape[dim] - width, None, axis=dim), axis, forward
        )
        high = lax.ppermute(lax.slice_in_dim(block, 0, width, axis=dim), axis, backward)
        block = jnp.concatenate([low, block, high], axis=dim)
    return block


def shifted(value, axis, steps):
    count = lax.axis_size(axis)
    pairs = [(source, (source + steps) % count) for source in range(count)]
    return lax.ppermute(value, axis, pairs)


def swish_slope(values):
    sigmoid = jax.nn.sigmoid(values)
    return sigmoid * (1.0 + values * (1.0 - sigmoid))


def contract_rows(left, right):
    return lax.dot_general(
        left, right, (((0,), (0,)), ((), ())), preferred_element_type=jnp.float32
    )


def contract_cols(left, right):
    return lax.dot_general(
        left, right, (((1,), (1,)), ((), ())), preferred_element_type=jnp.float32
    )


def inner_layer(operands, weights):
    partial_value = jnp.zeros((operands[0].shape[0], weights.shape[2]), jnp.float32)
    for position in range(len(operands)):
        partial_value = partial_value + jnp.dot(
            operands[position], weights[position], preferred_element_type=jnp.float32
        )
    return lax.psum_scatter(partial_value, "lat", scatter_dimension=1, tiled=True)


def outer_layer(hidden, weights):
    partial_value = jnp.dot(hidden, weights, preferred_element_type=jnp.float32)
    width = weights.shape[1]
    summed = lax.psum_scatter(partial_value, "lat", scatter_dimension=1, tiled=True)
    totals, squares = lax.psum((jnp.sum(summed, axis=1), jnp.sum(summed * summed, axis=1)), "lat")
    middle = (totals / width)[:, None]
    inverse = lax.rsqrt(squares[:, None] / width - middle * middle + EPSILON)
    normed = (summed - middle) * inverse
    return (normed, inverse)


def norm_backward(cotangent, normed, inverse):
    width = normed.shape[1] * lax.axis_size("lat")
    totals, crossed = lax.psum(
        (jnp.sum(cotangent, axis=1), jnp.sum(cotangent * normed, axis=1)), "lat"
    )
    return (cotangent - (totals / width)[:, None] - normed * (crossed / width)[:, None]) * inverse


def layer_backward(cotangent, operands, weights):
    gathered = lax.all_gather(cotangent, "lat", axis=1, tiled=True)
    weight_grads = [contract_rows(operand, gathered) for operand in operands]
    operand_grads = [contract_cols(gathered, weight) for weight in weights]
    return (weight_grads, operand_grads)


def body(
    node_latents,
    edge_latents,
    senders,
    receivers,
    long_count,
    edge_inner,
    edge_outer,
    node_inner,
    node_outer,
    node_cotangent,
    edge_cotangent,
):
    node_count = node_latents.shape[0]
    edge_count = edge_latents.shape[0]
    fine_count = FINE_DEV
    patch_count = lax.axis_size("patch")
    first_node = lax.axis_index("patch") * node_count
    sender_ids = senders.reshape(edge_count)
    receiver_ids = receivers.reshape(edge_count) - first_node
    extended = with_halo(node_latents, (("patch", 0),), HALO)
    coarse_rows = lax.all_gather(node_latents[:COARSE_DEV], "patch", axis=0, tiled=True)
    near_index = (sender_ids[:fine_count] - first_node + HALO) % (node_count * patch_count)
    far_ids = sender_ids[fine_count:]
    far_index = far_ids // node_count * COARSE_DEV + far_ids % node_count
    near_table = (
        near_index[:, None] == jnp.arange(extended.shape[0], dtype=jnp.int32)[None, :]
    ).astype(jnp.bfloat16)
    far_table = (
        far_index[:, None] == jnp.arange(coarse_rows.shape[0], dtype=jnp.int32)[None, :]
    ).astype(jnp.bfloat16)
    recv_table = (receiver_ids[:, None] == jnp.arange(node_count, dtype=jnp.int32)[None, :]).astype(
        jnp.bfloat16
    )
    near_rows = jnp.dot(near_table, extended, preferred_element_type=jnp.float32)
    far_rows = jnp.dot(far_table, coarse_rows, preferred_element_type=jnp.float32)
    sender_rows = jnp.concatenate([near_rows, far_rows], 0).astype(jnp.bfloat16)
    receiver_rows = jnp.dot(recv_table, node_latents, preferred_element_type=jnp.float32).astype(
        jnp.bfloat16
    )
    slot_index = jnp.arange(edge_count - fine_count, dtype=jnp.int32)
    live_mask = jnp.concatenate(
        [jnp.ones((fine_count,), jnp.float32), (slot_index < long_count[0]).astype(jnp.float32)]
    )[:, None]
    operands = (edge_latents, sender_rows, receiver_rows)
    hidden_pre = inner_layer(operands, edge_inner)
    hidden_act = jax.nn.silu(hidden_pre).astype(jnp.bfloat16)
    normed, inverse = outer_layer(hidden_act, edge_outer)
    update = live_mask * normed
    edge_output = (edge_latents.astype(jnp.float32) + update).astype(jnp.bfloat16)
    aggregate = contract_rows(recv_table, update.astype(jnp.bfloat16)).astype(jnp.bfloat16)
    node_pre = inner_layer((node_latents, aggregate), node_inner)
    node_act = jax.nn.silu(node_pre).astype(jnp.bfloat16)
    node_normed, node_inverse = outer_layer(node_act, node_outer)
    node_output = (node_latents.astype(jnp.float32) + node_normed).astype(jnp.bfloat16)
    node_dy = norm_backward(node_cotangent.astype(jnp.float32), node_normed, node_inverse).astype(
        jnp.bfloat16
    )
    outer_grads, outer_inputs = layer_backward(node_dy, [node_act], [node_outer])
    node_dpre = (outer_inputs[0] * swish_slope(node_pre)).astype(jnp.bfloat16)
    inner_grads, inner_inputs = layer_backward(
        node_dpre, [node_latents, aggregate], [node_inner[0], node_inner[1]]
    )
    node_weights = (jnp.stack(inner_grads), outer_grads[0])
    aggregate_grad = inner_inputs[1].astype(jnp.bfloat16)
    node_self = node_cotangent.astype(jnp.float32) + inner_inputs[0]
    update_grad = edge_cotangent.astype(jnp.float32) + jnp.dot(
        recv_table, aggregate_grad, preferred_element_type=jnp.float32
    )
    edge_dy = norm_backward(live_mask * update_grad, normed, inverse).astype(jnp.bfloat16)
    edge_outer_grads, edge_outer_inputs = layer_backward(edge_dy, [hidden_act], [edge_outer])
    edge_dpre = (edge_outer_inputs[0] * swish_slope(hidden_pre)).astype(jnp.bfloat16)
    edge_inner_grads, edge_inner_inputs = layer_backward(
        edge_dpre, list(operands), [edge_inner[0], edge_inner[1], edge_inner[2]]
    )
    edge_weights = (jnp.stack(edge_inner_grads), edge_outer_grads[0])
    edge_grads = (edge_cotangent.astype(jnp.float32) + edge_inner_inputs[0]).astype(jnp.bfloat16)
    sender_grads = edge_inner_inputs[1].astype(jnp.bfloat16)
    receiver_grads = edge_inner_inputs[2].astype(jnp.bfloat16)
    all_weights = lax.psum(
        (edge_weights[0], edge_weights[1], node_weights[0], node_weights[1]), "patch"
    )
    near_grads = contract_rows(near_table, sender_grads[:fine_count])
    far_grads = contract_rows(far_table, sender_grads[fine_count:])
    coarse_share = lax.psum_scatter(far_grads, "patch", scatter_dimension=0, tiled=True)
    own_grads = (
        node_self + contract_rows(recv_table, receiver_grads) + near_grads[HALO : HALO + node_count]
    )
    returned = []
    for offset, rim_part in ((-1, near_grads[:HALO]), (1, near_grads[HALO + node_count :])):
        returned.append(
            shifted(rim_part.astype(jnp.bfloat16), "patch", offset).astype(rim_part.dtype)
        )
    own_grads = own_grads.at[node_count - HALO :].add(returned[0])
    own_grads = own_grads.at[:HALO].add(returned[1])
    own_grads = own_grads.at[:COARSE_DEV].add(coarse_share)
    node_grads = own_grads.astype(jnp.bfloat16)
    return (
        edge_output,
        node_output,
        edge_grads,
        node_grads,
        all_weights[0] / patch_count,
        all_weights[1] / patch_count,
        all_weights[2] / patch_count,
        all_weights[3] / patch_count,
    )


def solution(mesh):
    placed = (
        P("patch", "lat"),
        P("patch", "lat"),
        P("patch", None),
        P("patch", None),
        P("patch"),
        P(None, "lat", None),
        P("lat", None),
        P(None, "lat", None),
        P("lat", None),
        P("patch", "lat"),
        P("patch", "lat"),
    )
    return jax.shard_map(
        body,
        mesh=mesh,
        in_specs=placed,
        out_specs=(
            P("patch", "lat"),
            P("patch", "lat"),
            P("patch", "lat"),
            P("patch", "lat"),
            P(None, "lat", None),
            P("lat", None),
            P(None, "lat", None),
            P("lat", None),
        ),
        check_vma=False,
    )
```

profile of v0, /device:TPU:1, one launch (start us, length us, event | category | flops | bytes accessed | tf_op | source)
XLA Modules:
  0.0 2394.9 jit_solution(835558063851591119)
XLA Ops:
  8.1 4.1 collective-permute-start
  13.7 187.4 %all_gather.15 = bf16[1024,256]{1,0:T(8,128)(2,1)S(1)} all-gather(bf16[8,256]{1,0:T(8,128)(2,1)S(1)} %slice.117), channel_id=1, replica_groups=mesh['patch'=128,'lat'=2] {'patch'}, dimensions={0}, use_global_device_ids=true | all-gather | bytes 528384 | tf_op jit(solution)/shard_map/all_gather | solution.py:107
  205.8 2.2 convolution_add_fusion
  208.1 39.3 %reduce-scatter.6.cloned.1.call-done = f32[1536,256]{1,0:T(8,128)} async-done(((f32[1536,512]{1,0:T(8,128)}), f32[1536,256]{1,0:T(8,128)}) %reduce-scatter.6.cloned.1.call-update) | async-done | bytes 1572880 | tf_op jit(solution)/shard_map/reduce_scatter | solution.py:57
  247.4 3.6 fusion.75
  252.3 48.4 %reduce-scatter.8.cloned.1.call-done = f32[1536,256]{1,0:T(8,128)} async-done(((f32[1536,512]{1,0:T(8,128)}), f32[1536,256]{1,0:T(8,128)}) %reduce-scatter.8.cloned.1.call-update) | async-done | bytes 1572880 | tf_op jit(solution)/shard_map/reduce_scatter | solution.py:63
  300.7 2.0 fusion.77
  302.7 5.3 all-reduce.5
  310.5 21.5 reduce-scatter.10.cloned.1.call-done
  332.0 2.0 fusion.73
  334.0 20.2 reduce-scatter.12.cloned.1.call-done
  355.3 3.8 all-reduce.4
  360.3 3.8 all-reduce.3
  364.1 1.7 fusion.53
  365.8 4.1 all_gather.16
  370.6 4.2 all_gather.17
  374.9 2.7 fusion.76
  377.6 5.6 all-reduce.2
  384.5 3.8 multiply_convert_fusion
  388.6 40.2 %all-gather.3.cloned.1.call-done = bf16[1536,512]{1,0:T(8,128)(2,1)} async-done(((bf16[1536,256]{1,0:T(8,128)(2,1)}), bf16[1536,512]{1,0:T(8,128)(2,1)}) %all-gather.3.cloned.1.call-update) | async-done | bytes 1572880 | tf_op jit(solution)/shard_map/all_gather | solution.py:80
  428.8 3.5 fusion.1
  432.4 33.4 %all-gather.5.cloned.1.call-done = bf16[1536,512]{1,0:T(8,128)(2,1)} async-done(((bf16[1536,256]{1,0:T(8,128)(2,1)}), bf16[1536,512]{1,0:T(8,128)(2,1)}) %all-gather.5.cloned.1.call-update) | async-done | bytes 1572880 | tf_op jit(solution)/shard_map/all_gather | solution.py:80
  465.7 2.0 convolution_convert_fusion
  467.8 1.7 fusion.5
  480.1 1.7 fusion.83
  481.9 3.0 collective-permute-start.3
  484.9 1.5 fusion.2
  487.4 2.8 collective-permute-done.2
  490.2 633.2 %reduce-scatter.14.cloned.1.call-done = f32[8,256]{1,0:T(8,128)} async-done(((f32[1024,256]{1,0:T(8,128)}), f32[8,256]{1,0:T(8,128)}) %reduce-scatter.14.cloned.1.call-update) | async-done | bytes 8208 | tf_op jit(solution)/shard_map/reduce_scatter | solution.py:170
  1124.8 1257.1 %all-reduce.8.cloned.1.call-done = (f32[3,256,512]{1,2,0:T(8,128)}, f32[256,512]{1,0:T(8,128)}, f32[2,256,512]{1,2,0:T(8,128)}, f32[256,512]{1,0:T(8,128)}) async-done(((f32[3,256,512]{1,2,0:T(8,128)}, f32[256,512]{1,0:T(8,128)}, f32[2,256,512]{1,2,0:T(8,128)}, f32[256,512]{1,0:T(8,128)}), (f32[3,256,512]{1,2,0:T(8,128)}, f32[256,512]{1,0:T(8,128)}, f32[2,256,512]{1,2,0:T(8,128)}, ...) | async-done | bytes 3670032 | tf_op jit(solution)/shard_map/psum | solution.py:165
  2381.9 1.5 broadcast_multiply_fusion
  2383.4 1.6 copy.23
  (144 shorter events, 30.6 us)
Async XLA Ops:
  7.2 240.2 %copy-start = (bf16[256,512]{1,0:T(8,128)(2,1)S(1)}, bf16[256,512]{1,0:T(8,128)(2,1)}, u32[]{:S(2)}) copy-start(bf16[256,512]{1,0:T(8,128)(2,1)} %param.23) | copy-start | bytes 786436
  7.2 196.4 %copy-start.14 = (bf16[3,256,512]{2,1,0:T(8,128)(2,1)S(1)}, bf16[3,256,512]{2,1,0:T(8,128)(2,1)}, u32[]{:S(2)}) copy-start(bf16[3,256,512]{2,1,0:T(8,128)(2,1)} %param.22) | copy-start | bytes 2359300
  7.2 196.4 %copy-start.5 = (bf16[1536,256]{1,0:T(8,128)(2,1)S(1)}, bf16[1536,256]{1,0:T(8,128)(2,1)}, u32[]{:S(2)}) copy-start(bf16[1536,256]{1,0:T(8,128)(2,1)} %param.18) | copy-start | bytes 2359300
  7.2 240.2 %reduce-scatter.6.cloned.1.call-start = ((), (), s32[]{:S(2)}) async-start(), calls=%async_computation.5 | async-start | bytes 4718592 | tf_op jit(solution)/shard_map/reduce_scatter | solution.py:57
  8.1 196.3 %collective-permute-start = (bf16[32,256]{1,0:T(8,128)(2,1)S(1)}, bf16[32,256]{1,0:T(8,128)(2,1)S(1)}, u32[]{:S(2)}, u32[]{:S(2)}) collective-permute-start(bf16[32,256]{1,0:T(8,128)(2,1)S(1)} %get-tuple-element.80), channel_id=1, source_target_pairs={{0,2},{2,4},{4,6},{6,8},{8,10},{10,12},{12,14},{14,16},{16,18},{18... | collective-permute-start | bytes 49160 | tf_op jit(solution)/shard_map/ppermute | solution.py:20
  12.2 192.1 %collective-permute-start.1 = (bf16[32,256]{1,0:T(8,128)(2,1)S(1)}, bf16[32,256]{1,0:T(8,128)(2,1)S(1)}, u32[]{:S(2)}, u32[]{:S(2)}) collective-permute-start(bf16[32,256]{1,0:T(8,128)(2,1)S(1)} %get-tuple-element.81), channel_id=1, source_target_pairs={{2,0},{4,2},{6,4},{8,6},{10,8},{12,10},{14,12},{16,14},{18,16},{20... | collective-permute-start | bytes 49160 | tf_op jit(solution)/shard_map/ppermute | solution.py:23
  13.6 189.5 %copy-start.30 = (s32[384]{0:T(512)}, s32[384]{0:T(512)S(1)}, u32[]{:S(2)}) copy-start(s32[384]{0:T(512)S(1)} %fusion.65) | copy-start | bytes 4612
  203.2 2.4 copy-start.3
  208.0 92.6 %reduce-scatter.8.cloned.1.call-start = ((), (), s32[]{:S(2)}) async-start(), calls=%async_computation.6 | async-start | bytes 4718592 | tf_op jit(solution)/shard_map/reduce_scatter | solution.py:63
  251.1 80.9 %reduce-scatter.10.cloned.1.call-start = ((), (), s32[]{:S(2)}) async-start(), calls=%async_computation.7 | async-start | bytes 589824 | tf_op jit(solution)/shard_map/reduce_scatter | solution.py:57
  300.7 7.3 copy-start.1
  308.0 24.0 %copy-start.36 = (bf16[256,512]{1,0:T(8,128)(2,1)S(1)}, bf16[256,512]{1,0:T(8,128)(2,1)}, u32[]{:S(2)}) copy-start(bf16[256,512]{1,0:T(8,128)(2,1)} %param.25) | copy-start | bytes 786436
  309.5 45.9 %copy-start.21 = (bf16[192,256]{1,0:T(8,128)(2,1)}, bf16[192,256]{1,0:T(8,128)(2,1)S(1)}, u32[]{:S(2)}) copy-start(bf16[192,256]{1,0:T(8,128)(2,1)S(1)} %fusion.12) | copy-start | bytes 294916
  309.5 49.7 %copy-start.12 = (bf16[192,256]{1,0:T(8,128)(2,1)S(1)}, bf16[192,256]{1,0:T(8,128)(2,1)}, u32[]{:S(2)}) copy-start(bf16[192,256]{1,0:T(8,128)(2,1)} %param.26) | copy-start | bytes 294916
  310.4 59.5 %copy-start.37 = (bf16[256,512]{1,0:T(8,128)(2,1)S(1)}, bf16[256,512]{1,0:T(8,128)(2,1)}, u32[]{:S(2)}) copy-start(bf16[256,512]{1,0:T(8,128)(2,1)} %param.25) | copy-start | bytes 786436
  310.5 43.8 %reduce-scatter.12.cloned.1.call-start = ((), (), s32[]{:S(2)}) async-start(), calls=%async_computation.8 | async-start | bytes 589824 | tf_op jit(solution)/shard_map/reduce_scatter | solution.py:63
  332.0 38.0 %copy-start.38 = (f32[192,256]{1,0:T(8,128)S(1)}, f32[192,256]{1,0:T(8,128)}, u32[]{:S(2)}) copy-start(f32[192,256]{1,0:T(8,128)} %reduce-scatter.10.cloned.1.call-done) | copy-start | bytes 589828
  334.0 94.8 %all-gather.3.cloned.1.call-start = ((), (), s32[]{:S(2)}) async-start(), calls=%async_computation.9 | async-start | bytes 2359296 | tf_op jit(solution)/shard_map/all_gather | solution.py:80
  388.3 77.4 %all-gather.5.cloned.1.call-start = ((), (), s32[]{:S(2)}) async-start(), calls=%async_computation.10 | async-start | bytes 2359296 | tf_op jit(solution)/shard_map/all_gather | solution.py:80
  432.3 35.5 %copy-start.31 = (s32[384]{0:T(512)S(1)}, s32[384]{0:T(512)}, u32[]{:S(2)}) copy-start(s32[384]{0:T(512)} %copy-done.30) | copy-start | bytes 4612
  432.3 691.1 %reduce-scatter.14.cloned.1.call-start = ((), (), s32[]{:S(2)}) async-start(), calls=%async_computation.11 | async-start | bytes 1056768 | tf_op jit(solution)/shard_map/reduce_scatter | solution.py:170
  467.8 1.8 copy-start.28
  467.8 1.8 copy-start.2
  469.5 1912.4 %all-reduce.8.cloned.1.call-start = ((), (), s32[]{:S(2)}) async-start(), calls=%async_computation.12 | async-start | bytes 7340032 | tf_op jit(solution)/shard_map/psum | solution.py:165
  470.1 2.2 copy-start.34
  470.1 2.3 copy-start.35
  478.2 2.0 copy-start.33
  479.2 5.7 copy-start.15
  479.2 5.7 copy-start.16
  481.9 8.3 collective-permute-start.3
  484.9 5.2 collective-permute-start.2
  2383.4 2.5 copy-start.19
  (20 other events, 25.2 us)
Sparse Core Ops, SparseCore 0:
  208.2 39.1 reduce-scatter.5
  251.2 49.4 reduce-scatter.7
  310.6 21.3 reduce-scatter.9
  335.1 19.1 reduce-scatter.11
  388.5 40.3 all-gather.2
  432.4 33.2 all-gather.4
  469.6 653.7 reduce-scatter.13
  1127.1 1254.7 all-reduce.7
where the time goes:
time: 2400 us; the launch traced here: 2390 us
  waiting for transfers between devices  2100 us (88%)
  blocking collectives  214 us (9%)
  matrix products  34 us (1%)
    psum x1, waiting for transfers between devices, body(): lax.psum((edge_weights[0], edge_weights[1], node_weights[0], node_weights...  1260 us
    reduce_scatter x1, waiting for transfers between devices, body(): lax.psum_scatter(far_grads, 'patch', scatter_dimension=0, tiled=True)  633 us
    all_gather x1, blocking collectives, body(): lax.all_gather(node_latents[:COARSE_DEV], 'patch', axis=0, tiled=True)  187 us
    all_gather x2, waiting for transfers between devices, layer_backward(): gathered = lax.all_gather(cotangent, 'lat', axis=1, tiled=True)  73.6 us
    reduce_scatter x2, waiting for transfers between devices, outer_layer(): lax.psum_scatter(partial_value, 'lat', scatter_dimension=1, tiled=True)  68.6 us
    reduce_scatter x2, waiting for transfers between devices, inner_layer(): lax.psum_scatter(partial_value, 'lat', scatter_dimension=1, tiled=True)  60.8 us
  transfers between devices with their start and end apart: 12, of which 9 were waited for; matrix products, arithmetic and copies ran while one was open for 1% of the time, Pallas kernels for 0%

commit v1 on v0

v1 whole, which is shorter than its diff:
```python
import jax
import jax.numpy as jnp
from jax import lax
from jax.sharding import PartitionSpec as P

HALO = 32
COARSE = 8
FINE = 1152
EPSILON = 1e-05
F32 = jnp.float32
BF16 = jnp.bfloat16


def dot(left, right):
    return jnp.dot(left, right, preferred_element_type=F32)


def contract_rows(left, right):
    return lax.dot_general(left, right, (((0,), (0,)), ((), ())), preferred_element_type=F32)


def contract_cols(left, right):
    return lax.dot_general(left, right, (((1,), (1,)), ((), ())), preferred_element_type=F32)


def swish_slope(values):
    sigmoid = jax.nn.sigmoid(values)
    return sigmoid * (1.0 + values * (1.0 - sigmoid))


def layer_norm(values):
    middle = jnp.mean(values, axis=1, keepdims=True)
    centered = values - middle
    inverse = lax.rsqrt(jnp.mean(centered * centered, axis=1, keepdims=True) + EPSILON)
    return centered * inverse, inverse


def norm_backward(cotangent, normed, inverse):
    mean = jnp.mean(cotangent, axis=1, keepdims=True)
    crossed = jnp.mean(cotangent * normed, axis=1, keepdims=True)
    return (cotangent - mean - normed * crossed) * inverse


def swap_lat(value):
    return lax.ppermute(value, "lat", [(0, 1), (1, 0)])


def swap_core(value):
    count = lax.axis_size("patch")
    return lax.ppermute(value, "patch", [(i, i ^ 1) for i in range(count)])


def shifted(value, steps):
    count = lax.axis_size("patch")
    return lax.ppermute(value, "patch", [(i, (i + steps) % count) for i in range(count)])


def other_neighbour(value):
    count = lax.axis_size("patch")
    pairs = []
    for patch in range(count):
        for lat in range(2):
            across = patch ^ 2
            pairs.append((patch * 2 + lat, across * 2 + (1 - lat)))
    return lax.ppermute(value, ("patch", "lat"), pairs)


def same_core_groups():
    count = lax.axis_size("patch")
    return [list(range(core, count, 2)) for core in range(2)]


def chips_all_to_all(value):
    return lax.all_to_all(value, "patch", 0, 0, tiled=True, axis_index_groups=same_core_groups())


def take(value, start, size, axis):
    return lax.dynamic_slice_in_dim(value, start, size, axis)


def one_hot(index, width):
    return (index[:, None] == jnp.arange(width, dtype=jnp.int32)[None, :]).astype(BF16)


def body(
    node_latents,
    edge_latents,
    senders,
    receivers,
    long_count,
    edge_inner,
    edge_outer,
    node_inner,
    node_outer,
    node_cotangent,
    edge_cotangent,
):
    nodes, half = node_latents.shape
    edges = edge_latents.shape[0]
    fine, longs = FINE // 2, (edges - FINE) // 2
    patches = lax.axis_size("patch")
    chips = patches // 2
    lat = lax.axis_index("lat")
    patch = lax.axis_index("patch")
    core = patch % 2
    first_node = patch * nodes

    def rows_of(value, side):
        return jnp.concatenate(
            [take(value, side * fine, fine, 0), take(value, FINE + side * longs, longs, 0)], 0
        )

    def ordered(mine, other, axis):
        return jnp.where(
            lat == 0,
            jnp.concatenate([mine, other], axis),
            jnp.concatenate([other, mine], axis),
        )

    def own_cols(value):
        return take(value, lat * half, half, 1)

    def other_cols(value):
        return take(value, (1 - lat) * half, half, 1)

    def whole_rows(value):
        return ordered(rows_of(value, lat), swap_lat(rows_of(value, 1 - lat)), 1)

    def back_to_columns(value):
        mine, got = own_cols(value), swap_lat(other_cols(value))
        fine_rows = ordered(mine[:fine], got[:fine], 0)
        long_rows = ordered(mine[fine:], got[fine:], 0)
        return jnp.concatenate([fine_rows, long_rows], 0)

    pair = swap_lat(jnp.concatenate([node_latents, node_cotangent], 0))
    node_x = ordered(node_latents, pair[:nodes], 1)
    node_g = ordered(node_cotangent, pair[nodes:], 1)
    low = shifted(node_x[nodes - HALO :], 1)
    high = shifted(node_x[:HALO], -1)
    extended = jnp.concatenate([low, node_x, high], 0)
    coarse_mine = chips_all_to_all(
        jnp.broadcast_to(node_x[None, :COARSE], (chips, COARSE, 2 * half))
    )
    coarse_other = swap_core(coarse_mine)
    coarse = jnp.where(
        core == 0,
        jnp.stack([coarse_mine, coarse_other], 1),
        jnp.stack([coarse_other, coarse_mine], 1),
    ).reshape(patches * COARSE, 2 * half)

    def whole_weight(weight):
        rows = weight.shape[-2] // 2
        axis = weight.ndim - 2
        got = other_neighbour(take(weight, core * rows, rows, axis))
        again = swap_core(got)
        missing = jnp.where(
            core == 0,
            jnp.concatenate([got, again], axis),
            jnp.concatenate([again, got], axis),
        )
        return ordered(weight, missing, axis)

    edge_in, edge_out = whole_weight(edge_inner), whole_weight(edge_outer)
    node_in, node_out = whole_weight(node_inner), whole_weight(node_outer)

    edge_x = whole_rows(edge_latents)
    edge_g = whole_rows(edge_cotangent)
    sender_ids = rows_of(senders.reshape(edges), lat)
    receiver_ids = rows_of(receivers.reshape(edges), lat) - first_node
    near_index = (sender_ids[:fine] - first_node + HALO) % (nodes * patches)
    far_ids = sender_ids[fine:]
    far_index = far_ids // nodes * COARSE + far_ids % nodes
    near_table = one_hot(near_index, extended.shape[0])
    far_table = one_hot(far_index, coarse.shape[0])
    recv_table = one_hot(receiver_ids, nodes)
    slot_index = jnp.arange(longs, dtype=jnp.int32) + lat * longs
    live_mask = jnp.concatenate(
        [jnp.ones((fine,), F32), (slot_index < long_count[0]).astype(F32)]
    )[:, None]

    sender_rows = jnp.concatenate(
        [dot(near_table, extended), dot(far_table, coarse)], 0
    ).astype(BF16)
    receiver_rows = dot(recv_table, node_x).astype(BF16)
    hidden_pre = (
        dot(edge_x, edge_in[0]) + dot(sender_rows, edge_in[1]) + dot(receiver_rows, edge_in[2])
    )
    hidden_act = jax.nn.silu(hidden_pre).astype(BF16)
    normed, inverse = layer_norm(dot(hidden_act, edge_out))
    update = live_mask * normed
    edge_output = back_to_columns((edge_x.astype(F32) + update).astype(BF16))
    partial = contract_rows(recv_table, update.astype(BF16))
    aggregate = (partial + swap_lat(partial.astype(BF16)).astype(F32)).astype(BF16)

    node_pre = dot(node_x, node_in[0]) + dot(aggregate, node_in[1])
    node_act = jax.nn.silu(node_pre).astype(BF16)
    node_normed, node_inverse = layer_norm(dot(node_act, node_out))
    node_output = (node_latents.astype(F32) + own_cols(node_normed)).astype(BF16)
    node_dy = norm_backward(node_g.astype(F32), node_normed, node_inverse).astype(BF16)
    node_dpre = (contract_cols(node_dy, node_out) * swish_slope(node_pre)).astype(BF16)
    node_grad_parts = jnp.concatenate(
        [
            contract_rows(node_latents, node_dpre),
            contract_rows(own_cols(aggregate), node_dpre),
            contract_rows(own_cols(node_act), node_dy),
        ],
        0,
    ).astype(BF16)
    aggregate_grad = contract_cols(node_dpre, node_in[1]).astype(BF16)
    node_self = node_cotangent.astype(F32) + contract_cols(
        node_dpre, node_inner[0]
    )

    update_grad = edge_g.astype(F32) + dot(recv_table, aggregate_grad)
    edge_dy = norm_backward(live_mask * update_grad, normed, inverse).astype(BF16)
    edge_dpre = (contract_cols(edge_dy, edge_out) * swish_slope(hidden_pre)).astype(BF16)
    edge_grad_parts = jnp.stack(
        [
            contract_rows(edge_x, edge_dpre),
            contract_rows(sender_rows, edge_dpre),
            contract_rows(receiver_rows, edge_dpre),
            contract_rows(hidden_act, edge_dy),
        ]
    ).astype(BF16)
    edge_grads = back_to_columns(
        (edge_g.astype(F32) + contract_cols(edge_dpre, edge_in[0])).astype(BF16)
    )
    sender_grads = contract_cols(edge_dpre, edge_in[1]).astype(BF16)
    receiver_grads = contract_cols(edge_dpre, edge_in[2]).astype(BF16)
    near_grads = contract_rows(near_table, sender_grads[:fine])
    far_grads = contract_rows(far_table, sender_grads[fine:]).astype(BF16)
    recv_grads = contract_rows(recv_table, receiver_grads)
    near_grads = near_grads + jnp.pad(recv_grads, ((HALO, HALO), (0, 0)))

    summed = own_cols(near_grads) + swap_lat(other_cols(near_grads).astype(BF16)).astype(F32)
    to_low = shifted(summed[:HALO].astype(BF16), -1).astype(F32)
    to_high = shifted(summed[HALO + nodes :].astype(BF16), 1).astype(F32)

    lanes = 128
    blocks = 2 * half // 2 // lanes

    def core_cols(value, which):
        return take(value, which * half, half, value.ndim - 1)

    def over_cores_cols(value):
        got = swap_core(core_cols(value, 1 - core))
        return core_cols(value, core).astype(F32) + got.astype(F32)

    edge_parts = over_cores_cols(edge_grad_parts).astype(BF16)
    edge_parts = take(edge_parts, lat * half, half, 1).astype(F32) + swap_lat(
        take(edge_parts, (1 - lat) * half, half, 1)
    ).astype(F32)
    node_parts = over_cores_cols(node_grad_parts)
    weight_parts = jnp.concatenate(
        [edge_parts.reshape(4 * half, half), node_parts], 0
    ).astype(BF16)
    total_rows = weight_parts.shape[0] * blocks
    share = total_rows // chips
    weight_parts = jnp.concatenate(
        [weight_parts[:, i * lanes : (i + 1) * lanes] for i in range(blocks)], 0
    ).reshape(chips, share, lanes)

    far_parts = far_grads.reshape(chips, 2, COARSE, 2 * half)
    far_own = jnp.where(core == 0, far_parts[:, 0], far_parts[:, 1])
    far_sent = jnp.where(core == 0, far_parts[:, 1], far_parts[:, 0])
    far_own = far_own.astype(F32) + swap_core(far_sent).astype(F32)
    far_own = take(far_own, lat * half, half, 2) + swap_lat(
        take(far_own, (1 - lat) * half, half, 2).astype(BF16)
    ).astype(F32)
    far_own = far_own.astype(BF16)
    far_own = jnp.concatenate(
        [far_own[:, :, i * lanes : (i + 1) * lanes] for i in range(blocks)], 1
    )
    arrived = chips_all_to_all(jnp.concatenate([weight_parts, far_own], 1))
    total = jnp.sum(arrived.astype(F32), 0)
    coarse_share = jnp.concatenate(
        [total[share + i * COARSE : share + (i + 1) * COARSE] for i in range(blocks)], 1
    )
    weight_share = (total[:share] / patches).astype(BF16)
    mine = chips_all_to_all(jnp.broadcast_to(weight_share[None], (chips, share, lanes)))
    mine = mine.reshape(blocks, total_rows // blocks, lanes)
    mine = jnp.concatenate([mine[i] for i in range(blocks)], 1)
    other = swap_core(mine)
    weights = jnp.where(
        core == 0, jnp.concatenate([mine, other], 1), jnp.concatenate([other, mine], 1)
    ).astype(F32)

    own_grads = node_self + summed[HALO : HALO + nodes]
    own_grads = own_grads.at[nodes - HALO :].add(to_low)
    own_grads = own_grads.at[:HALO].add(to_high)
    own_grads = own_grads.at[:COARSE].add(coarse_share)
    node_grads = own_grads.astype(BF16)
    return (
        edge_output,
        node_output,
        edge_grads,
        node_grads,
        weights[: 3 * half].reshape(3, half, 2 * half),
        weights[3 * half : 4 * half],
        weights[4 * half : 6 * half].reshape(2, half, 2 * half),
        weights[6 * half :],
    )


def solution(mesh):
    placed = (
        P("patch", "lat"),
        P("patch", "lat"),
        P("patch", None),
        P("patch", None),
        P("patch"),
        P(None, "lat", None),
        P("lat", None),
        P(None, "lat", None),
        P("lat", None),
        P("patch", "lat"),
        P("patch", "lat"),
    )
    return jax.shard_map(
        body,
        mesh=mesh,
        in_specs=placed,
        out_specs=(
            P("patch", "lat"),
            P("patch", "lat"),
            P("patch", "lat"),
            P("patch", "lat"),
            P(None, "lat", None),
            P("lat", None),
            P(None, "lat", None),
            P("lat", None),
        ),
        check_vma=False,
    )
```

time: 2400 us -> 211 us (0.09)
  waiting for transfers between devices: 2100 us -> 52.7 us
  blocking collectives: 214 us -> 0 us
  starting transfers between devices: 7.68 us -> 78.8 us
    psum x1 -> x0, waiting for transfers between devices: 1260 us -> none  [body(): lax.psum((edge_weights[0], edge_weights[1], node_weights[0], node_weights...]
    reduce_scatter x5 -> x0, waiting for transfers between devices: 763 us -> none  [the longest x1 633 us: body(): lax.psum_scatter(far_grads, 'patch', scatter_dimension=0, tiled=True)]
    all_gather x3 -> x0, blocking collectives: 196 us -> none  [the longest x1 187 us: body(): lax.all_gather(node_latents[:COARSE_DEV], 'patch', axis=0, tiled=True)]
    all_gather x2 -> x0, waiting for transfers between devices: 73.6 us -> none  [layer_backward(): gathered = lax.all_gather(cotangent, 'lat', axis=1, tiled=True)]
    ppermute x4 -> x26, starting transfers between devices: 7.17 us -> 47.9 us  [the longest x9 26.8 us: swap_core(): return lax.ppermute(value, 'patch', [(i, i ^ 1) for i in range(count)])]
    all_to_all x0 -> x3, starting transfers between devices: none -> 31 us  [chips_all_to_all(): lax.all_to_all(value, 'patch', 0, 0, tiled=True, axis_index_groups=same_c...]
    all_to_all x0 -> x3, waiting for transfers between devices: none -> 28.6 us  [chips_all_to_all(): lax.all_to_all(value, 'patch', 0, 0, tiled=True, axis_index_groups=same_c...]
  transfers between devices with their start and end apart: 12 -> 29, of which waited for: 9 -> 9; matrix products, arithmetic and copies ran while one was open for 1% -> 24% of each run, Pallas kernels for 0% -> 0%
where the time goes in v1:
time: 211 us; the launch traced here: 208 us
  starting transfers between devices  78.8 us (37%)
  waiting for transfers between devices  52.7 us (25%)
  local copies, waits for them, and re-layouts  29 us (14%)
  matrix products  22.5 us (11%)
  other arithmetic  22 us (10%)
  between operations  2.58 us (1%)
    all_to_all x3, starting transfers between devices, chips_all_to_all(): lax.all_to_all(value, 'patch', 0, 0, tiled=True, axis_index_groups=same_c...  31 us
    all_to_all x3, waiting for transfers between devices, chips_all_to_all(): lax.all_to_all(value, 'patch', 0, 0, tiled=True, axis_index_groups=same_c...  28.6 us
    ppermute x9, starting transfers between devices, swap_core(): return lax.ppermute(value, 'patch', [(i, i ^ 1) for i in range(count)])  26.8 us
    ppermute x9, waiting for transfers between devices, swap_lat(): return lax.ppermute(value, 'lat', [(0, 1), (1, 0)])  20 us
    dynamic_slice x15, local copies, waits for them, and re-layouts, take(): return lax.dynamic_slice_in_dim(value, start, size, axis)  11.2 us
    ppermute x4, starting transfers between devices, shifted(): lax.ppermute(value, 'patch', [(i, (i + steps) % count) for i in range(cou...  9.72 us
    dot_general x11, matrix products, dot(): return jnp.dot(left, right, preferred_element_type=F32)  8.81 us
    dot_general x11, matrix products, contract_rows(): lax.dot_general(left, right, (((0,), (0,)), ((), ())), preferred_element_...  8.42 us
  transfers between devices with their start and end apart: 29, of which 9 were waited for; matrix products, arithmetic and copies ran while one was open for 24% of the time, Pallas kernels for 0%

profile of v1, /device:TPU:1, one launch (start us, length us, event | category | flops | bytes accessed | tf_op | source)
XLA Modules:
  0.0 207.7 jit_solution(10675320233886333973)
XLA Ops:
  0.7 1.7 constant_dynamic-slice_fusion.10
  2.4 3.3 %collective-permute-start.13 = (bf16[128,512]{1,0:T(8,128)(2,1)}, bf16[128,512]{1,0:T(8,128)(2,1)}, u32[]{:S(2)}, u32[]{:S(2)}) collective-permute-start(bf16[128,512]{1,0:T(8,128)(2,1)} %constant_dynamic-slice_fusion.10), channel_id=1, source_target_pairs={{0,5},{1,4},{2,7},{3,6},{4,1},{5,0},{6,3},{7,2},{8,13},{9,12},{10,... | collective-permute-start | bytes 393224 | tf_op jit(solution)/shard_map/ppermute | solution.py:65
  5.7 1.6 constant_dynamic-slice_fusion.13
  8.5 1.7 constant_dynamic-slice_fusion.11
  10.2 2.5 %collective-permute-start.10 = (bf16[2,128,512]{2,1,0:T(8,128)(2,1)}, bf16[2,128,512]{2,1,0:T(8,128)(2,1)}, u32[]{:S(2)}, u32[]{:S(2)}) collective-permute-start(bf16[2,128,512]{2,1,0:T(8,128)(2,1)} %constant_dynamic-slice_fusion.11), channel_id=1, source_target_pairs={{0,5},{1,4},{2,7},{3,6},{4,1},{5,0},{6,3},{7,2},{8,13},{9,12},{10,... | collective-permute-start | bytes 786440 | tf_op jit(solution)/shard_map/ppermute | solution.py:65
  13.8 1.6 constant_dynamic-slice_fusion.6
  15.5 2.0 constant_dynamic-slice_fusion.7
  20.8 14.0 %all-to-all-start = ((bf16[64,8,512]{2,1,0:T(8,128)(2,1)}), bf16[64,8,512]{2,1,0:T(8,128)(2,1)S(1)}, u32[]{:S(2)}, u32[]{:S(2)}) async-start(bf16[64,8,512]{2,1,0:T(8,128)(2,1)} %broadcast_in_dim.4), calls=%async_computation | async-start | bytes 1048576 | tf_op jit(solution)/shard_map/all_to_all | solution.py:74
  34.9 5.1 %collective-permute-start.4 = (bf16[32,512]{1,0:T(8,128)(2,1)S(1)}, bf16[32,512]{1,0:T(8,128)(2,1)S(1)}, u32[]{:S(2)}, u32[]{:S(2)}) collective-permute-start(bf16[32,512]{1,0:T(8,128)(2,1)S(1)} %get-tuple-element.71), channel_id=1, source_target_pairs={{0,2},{2,4},{4,6},{6,8},{8,10},{10,12},{12,14},{14,16},{16,18},{18... | collective-permute-start | bytes 98312 | tf_op jit(solution)/shard_map/ppermute | solution.py:55
  41.1 9.9 %collective-permute-start.14 = (bf16[128,512]{1,0:T(8,128)(2,1)}, bf16[128,512]{1,0:T(8,128)(2,1)S(1)}, u32[]{:S(2)}, u32[]{:S(2)}) collective-permute-start(bf16[128,512]{1,0:T(8,128)(2,1)} %collective-permute-done.13), channel_id=1, source_target_pairs={{0,2},{2,0},{4,6},{6,4},{8,10},{10,8},{12,14},{14,12},{16,18},{18,... | collective-permute-start | bytes 393224 | tf_op jit(solution)/shard_map/ppermute | solution.py:50
  53.8 1.8 maximum_select_fusion.13
  55.6 1.8 maximum_select_fusion.12
  57.7 1.6 maximum_select_fusion.5
  69.0 3.5 %collective-permute-done.12 = bf16[192,512]{1,0:T(8,128)(2,1)S(1)} collective-permute-done((bf16[192,512]{1,0:T(8,128)(2,1)S(1)}, bf16[192,512]{1,0:T(8,128)(2,1)S(1)}, u32[]{:S(2)}, u32[]{:S(2)}) %collective-permute-start.12) | collective-permute-done | bytes 196640 | tf_op jit(solution)/shard_map/ppermute | solution.py:45
  76.1 3.4 %fusion.61 = (f32[768]{0:T(1024)S(1)}, f32[768]{0:T(1024)S(1)}, f32[768,512]{1,0:T(8,128)}) fusion(f32[768]{0:T(1024)S(1)} %add_rsqrt_fusion, f32[768,512]{1,0:T(8,128)S(1)} %get-tuple-element.78, f32[768]{0:T(1024)S(1)} %broadcast_multiply_fusion.2, bf16[192,512]{1,0:T(8,128)(2,1)S(1)} %fusion.8, bf16[2,512,512]{2,1,0:T(8,128)(2,1)} %copy-done.1, ...), kind=kOutput, calls=%fused_computation.188 | convolution fusion | flops 260160000 | bytes 4671489 | tf_op jit(solution)/shard_map/dot_general | solution.py:15
  79.5 3.0 %multiply_convert_fusion.1 = (bf16[768,512]{1,0:T(8,128)(2,1)S(1)}, bf16[768,512]{1,0:T(8,128)(2,1)S(1)}) fusion(f32[768,512]{1,0:T(8,128)} %get-tuple-element.85, f32[768,512]{1,0:T(8,128)S(1)} %get-tuple-element.78, f32[768]{0:T(1024)S(1)} %broadcast_multiply_fusion, f32[768]{0:T(1024)S(1)} %broadcast_multiply_fusion.1, f32[768]{0:T(1024)S(1)} %add_rsqrt_fusion, ...), kind=kLoop, calls=%fused_computation.11 | loop fusion | flops 9437184 | bytes 5520385 | tf_op jit(solution)/shard_map/convert_element_type | solution.py:215
  85.8 1.7 convolution_convert_fusion.2
  88.5 11.4 %collective-permute-start.23 = (bf16[64,8,512]{2,1,0:T(8,128)(2,1)S(1)}, bf16[64,8,512]{2,1,0:T(8,128)(2,1)S(1)}, u32[]{:S(2)}, u32[]{:S(2)}) collective-permute-start(bf16[64,8,512]{2,1,0:T(8,128)(2,1)S(1)} %fusion.16), channel_id=1, source_target_pairs={{0,2},{2,0},{4,6},{6,4},{8,10},{10,8},{12,14},{14,12},{16,18},{18,... | collective-permute-start | bytes 1572872 | tf_op jit(solution)/shard_map/ppermute | solution.py:50
  104.9 5.3 %collective-permute-done.24 = bf16[64,8,256]{2,1,0:T(8,128)(2,1)S(1)} collective-permute-done((bf16[64,8,256]{2,1,0:T(8,128)(2,1)S(1)}, bf16[64,8,256]{2,1,0:T(8,128)(2,1)S(1)}, u32[]{:S(2)}, u32[]{:S(2)}) %collective-permute-start.24) | collective-permute-done | bytes 262176 | tf_op jit(solution)/shard_map/ppermute | solution.py:45
  110.4 11.1 %collective-permute-done.21 = bf16[4,256,256]{2,1,0:T(8,128)(2,1)S(1)} collective-permute-done((bf16[4,256,256]{2,1,0:T(8,128)(2,1)S(1)}, bf16[4,256,256]{2,1,0:T(8,128)(2,1)S(1)}, u32[]{:S(2)}, u32[]{:S(2)}) %collective-permute-start.21) | collective-permute-done | bytes 524320 | tf_op jit(solution)/shard_map/ppermute | solution.py:45
  122.9 9.5 %all-to-all-start.1 = ((bf16[64,72,128]{2,1,0:T(8,128)(2,1)}), bf16[64,72,128]{2,1,0:T(8,128)(2,1)S(1)}, u32[]{:S(2)}, u32[]{:S(2)}) async-start(bf16[64,72,128]{2,1,0:T(8,128)(2,1)} %pad_maximum_fusion.1), calls=%async_computation.1 | async-start | bytes 2359296 | tf_op jit(solution)/shard_map/all_to_all | solution.py:74
  133.2 2.1 %fusion.2 = bf16[768,512]{1,0:T(8,128)(2,1)S(1)} fusion(bf16[768,512]{1,0:T(8,128)(2,1)} %copy-done.54, bf16[3,512,512]{2,1,0:T(8,128)(2,1)} %copy-done, bf16[192,256]{1,0:T(8,128)(2,1)S(1)} %copy-done.38, bf16[576,256]{1,0:T(8,128)(2,1)S(1)} %copy-done.33, bf16[768,256]{1,0:T(8,128)(2,1)} %collective-permute-done.15, pred[]{:T(512)S(6)} %eq.28), kind=kOutput, calls=%fused_computation.8 | convolution fusion | flops 408944640 | bytes 2883585 | tf_op jit(solution)/shard_map/dot_general | solution.py:23
  136.2 2.1 fusion.3
  138.3 1.6 convolution_add_fusion
  140.7 1.5 collective-permute-start.17
  145.1 18.5 %all-to-all-done.1 = bf16[64,72,128]{2,1,0:T(8,128)(2,1)S(1)} async-done(((bf16[64,72,128]{2,1,0:T(8,128)(2,1)}), bf16[64,72,128]{2,1,0:T(8,128)(2,1)S(1)}, u32[]{:S(2)}, u32[]{:S(2)}) %all-to-all-start.1) | async-done | bytes 1179680 | tf_op jit(solution)/shard_map/all_to_all | solution.py:74
  164.8 7.5 %all-to-all-start.2 = ((bf16[64,56,128]{2,1,0:T(8,128)(2,1)}), bf16[64,56,128]{2,1,0:T(8,128)(2,1)S(1)}, u32[]{:S(2)}, u32[]{:S(2)}) async-start(bf16[64,56,128]{2,1,0:T(8,128)(2,1)} %broadcast_in_dim.5), calls=%async_computation.2 | async-start | bytes 1835008 | tf_op jit(solution)/shard_map/all_to_all | solution.py:74
  173.3 1.8 collective-permute-start.18
  175.4 2.8 %collective-permute-start.19 = (bf16[32,256]{1,0:T(8,128)(2,1)S(1)}, bf16[32,256]{1,0:T(8,128)(2,1)S(1)}, u32[]{:S(2)}, u32[]{:S(2)}) collective-permute-start(bf16[32,256]{1,0:T(8,128)(2,1)S(1)} %get-tuple-element.73), channel_id=1, source_target_pairs={{0,2},{2,4},{4,6},{6,8},{8,10},{10,12},{12,14},{14,16},{16,18},{18... | collective-permute-start | bytes 49160 | tf_op jit(solution)/shard_map/ppermute | solution.py:55
  179.2 2.6 %collective-permute-done.19 = bf16[32,256]{1,0:T(8,128)(2,1)S(1)} collective-permute-done((bf16[32,256]{1,0:T(8,128)(2,1)S(1)}, bf16[32,256]{1,0:T(8,128)(2,1)S(1)}, u32[]{:S(2)}, u32[]{:S(2)}) %collective-permute-start.19) | collective-permute-done | bytes 16416 | tf_op jit(solution)/shard_map/ppermute | solution.py:55
  187.0 10.2 %all-to-all-done.2 = bf16[64,56,128]{2,1,0:T(8,128)(2,1)S(1)} async-done(((bf16[64,56,128]{2,1,0:T(8,128)(2,1)}), bf16[64,56,128]{2,1,0:T(8,128)(2,1)S(1)}, u32[]{:S(2)}, u32[]{:S(2)}) %all-to-all-start.2) | async-done | bytes 917536 | tf_op jit(solution)/shard_map/all_to_all | solution.py:74
  197.4 3.9 %collective-permute-start.25 = (bf16[1792,256]{1,0:T(8,128)(2,1)S(1)}, bf16[1792,256]{1,0:T(8,128)(2,1)S(1)}, u32[]{:S(2)}, u32[]{:S(2)}) collective-permute-start(bf16[1792,256]{1,0:T(8,128)(2,1)S(1)} %pad_maximum_fusion.3), channel_id=1, source_target_pairs={{0,2},{2,0},{4,6},{6,4},{8,10},{10,8},{12,14},{14,12},{16,18},{18,... | collective-permute-start | bytes 2752520 | tf_op jit(solution)/shard_map/ppermute | solution.py:50
  (261 shorter events, 53.3 us)
Async XLA Ops:
  2.4 37.7 %collective-permute-start.13 = (bf16[128,512]{1,0:T(8,128)(2,1)}, bf16[128,512]{1,0:T(8,128)(2,1)}, u32[]{:S(2)}, u32[]{:S(2)}) collective-permute-start(bf16[128,512]{1,0:T(8,128)(2,1)} %constant_dynamic-slice_fusion.10), channel_id=1, source_target_pairs={{0,5},{1,4},{2,7},{3,6},{4,1},{5,0},{6,3},{7,2},{8,13},{9,12},{10,... | collective-permute-start | bytes 393224 | tf_op jit(solution)/shard_map/ppermute | solution.py:65
  7.2 33.2 %collective-permute-start.7 = (bf16[128,512]{1,0:T(8,128)(2,1)}, bf16[128,512]{1,0:T(8,128)(2,1)}, u32[]{:S(2)}, u32[]{:S(2)}) collective-permute-start(bf16[128,512]{1,0:T(8,128)(2,1)} %constant_dynamic-slice_fusion.13), channel_id=1, source_target_pairs={{0,5},{1,4},{2,7},{3,6},{4,1},{5,0},{6,3},{7,2},{8,13},{9,12},{10,... | collective-permute-start | bytes 393224 | tf_op jit(solution)/shard_map/ppermute | solution.py:65
  8.2 11.0 %collective-permute-start.3 = (bf16[384,256]{1,0:T(8,128)(2,1)S(1)}, bf16[384,256]{1,0:T(8,128)(2,1)S(1)}, u32[]{:S(2)}, u32[]{:S(2)}) collective-permute-start(bf16[384,256]{1,0:T(8,128)(2,1)S(1)} %pad_maximum_fusion.12), channel_id=1, source_target_pairs={{0,1},{1,0},{2,3},{3,2},{4,5},{5,4},{6,7},{7,6},{8,9},{9,8},{10,11... | collective-permute-start | bytes 589832 | tf_op jit(solution)/shard_map/ppermute | solution.py:45
  10.2 43.3 %collective-permute-start.10 = (bf16[2,128,512]{2,1,0:T(8,128)(2,1)}, bf16[2,128,512]{2,1,0:T(8,128)(2,1)}, u32[]{:S(2)}, u32[]{:S(2)}) collective-permute-start(bf16[2,128,512]{2,1,0:T(8,128)(2,1)} %constant_dynamic-slice_fusion.11), channel_id=1, source_target_pairs={{0,5},{1,4},{2,7},{3,6},{4,1},{5,0},{6,3},{7,2},{8,13},{9,12},{10,... | collective-permute-start | bytes 786440 | tf_op jit(solution)/shard_map/ppermute | solution.py:65
  13.4 37.6 %collective-permute-start.1 = (bf16[3,128,512]{2,1,0:T(8,128)(2,1)}, bf16[3,128,512]{2,1,0:T(8,128)(2,1)}, u32[]{:S(2)}, u32[]{:S(2)}) collective-permute-start(bf16[3,128,512]{2,1,0:T(8,128)(2,1)} %constant_dynamic-slice_fusion.14), channel_id=1, source_target_pairs={{0,5},{1,4},{2,7},{3,6},{4,1},{5,0},{6,3},{7,2},{8,13},{9,12},{10,... | collective-permute-start | bytes 1179656 | tf_op jit(solution)/shard_map/ppermute | solution.py:65
  13.8 48.4 %copy-start.30 = (bf16[192,256]{1,0:T(8,128)(2,1)}, bf16[192,256]{1,0:T(8,128)(2,1)S(1)}, u32[]{:S(2)}) copy-start(bf16[192,256]{1,0:T(8,128)(2,1)S(1)} %get-tuple-element.65) | copy-start | bytes 294916
  15.5 46.7 %copy-start.15 = (bf16[576,256]{1,0:T(8,128)(2,1)}, bf16[576,256]{1,0:T(8,128)(2,1)S(1)}, u32[]{:S(2)}) copy-start(bf16[576,256]{1,0:T(8,128)(2,1)S(1)} %get-tuple-element.63) | copy-start | bytes 884740
  18.3 33.2 %copy-start.44 = (s32[576]{0:T(1024)}, s32[576]{0:T(1024)S(1)}, u32[]{:S(2)}) copy-start(s32[576]{0:T(1024)S(1)} %add_select_fusion) | copy-start | bytes 6916
  20.8 36.6 %all-to-all-start = ((bf16[64,8,512]{2,1,0:T(8,128)(2,1)}), bf16[64,8,512]{2,1,0:T(8,128)(2,1)S(1)}, u32[]{:S(2)}, u32[]{:S(2)}) async-start(bf16[64,8,512]{2,1,0:T(8,128)(2,1)} %broadcast_in_dim.4), calls=%async_computation | async-start | bytes 1048576 | tf_op jit(solution)/shard_map/all_to_all | solution.py:74
  34.9 6.2 %collective-permute-start.4 = (bf16[32,512]{1,0:T(8,128)(2,1)S(1)}, bf16[32,512]{1,0:T(8,128)(2,1)S(1)}, u32[]{:S(2)}, u32[]{:S(2)}) collective-permute-start(bf16[32,512]{1,0:T(8,128)(2,1)S(1)} %get-tuple-element.71), channel_id=1, source_target_pairs={{0,2},{2,4},{4,6},{6,8},{8,10},{10,12},{12,14},{14,16},{16,18},{18... | collective-permute-start | bytes 98312 | tf_op jit(solution)/shard_map/ppermute | solution.py:55
  40.0 11.0 %collective-permute-start.5 = (bf16[32,512]{1,0:T(8,128)(2,1)S(1)}, bf16[32,512]{1,0:T(8,128)(2,1)S(1)}, u32[]{:S(2)}, u32[]{:S(2)}) collective-permute-start(bf16[32,512]{1,0:T(8,128)(2,1)S(1)} %get-tuple-element.72), channel_id=1, source_target_pairs={{0,254},{2,0},{4,2},{6,4},{8,6},{10,8},{12,10},{14,12},{16,14},{18... | collective-permute-start | bytes 98312 | tf_op jit(solution)/shard_map/ppermute | solution.py:55
  40.5 21.7 %collective-permute-start = (bf16[768,256]{1,0:T(8,128)(2,1)S(1)}, bf16[768,256]{1,0:T(8,128)(2,1)S(1)}, u32[]{:S(2)}, u32[]{:S(2)}) collective-permute-start(bf16[768,256]{1,0:T(8,128)(2,1)S(1)} %pad_maximum_fusion.10), channel_id=1, source_target_pairs={{0,1},{1,0},{2,3},{3,2},{4,5},{5,4},{6,7},{7,6},{8,9},{9,8},{10,11... | collective-permute-start | bytes 1179656 | tf_op jit(solution)/shard_map/ppermute | solution.py:45
  41.1 11.7 %collective-permute-start.14 = (bf16[128,512]{1,0:T(8,128)(2,1)}, bf16[128,512]{1,0:T(8,128)(2,1)S(1)}, u32[]{:S(2)}, u32[]{:S(2)}) collective-permute-start(bf16[128,512]{1,0:T(8,128)(2,1)} %collective-permute-done.13), channel_id=1, source_target_pairs={{0,2},{2,0},{4,6},{6,4},{8,10},{10,8},{12,14},{14,12},{16,18},{18,... | collective-permute-start | bytes 393224 | tf_op jit(solution)/shard_map/ppermute | solution.py:50
  51.0 4.6 %collective-permute-start.8 = (bf16[128,512]{1,0:T(8,128)(2,1)}, bf16[128,512]{1,0:T(8,128)(2,1)S(1)}, u32[]{:S(2)}, u32[]{:S(2)}) collective-permute-start(bf16[128,512]{1,0:T(8,128)(2,1)} %collective-permute-done.7), channel_id=1, source_target_pairs={{0,2},{2,0},{4,6},{6,4},{8,10},{10,8},{12,14},{14,12},{16,18},{18,... | collective-permute-start | bytes 393224 | tf_op jit(solution)/shard_map/ppermute | solution.py:50
  51.0 6.7 %collective-permute-start.2 = (bf16[3,128,512]{2,1,0:T(8,128)(2,1)}, bf16[3,128,512]{2,1,0:T(8,128)(2,1)}, u32[]{:S(2)}, u32[]{:S(2)}) collective-permute-start(bf16[3,128,512]{2,1,0:T(8,128)(2,1)} %collective-permute-done.1), channel_id=1, source_target_pairs={{0,2},{2,0},{4,6},{6,4},{8,10},{10,8},{12,14},{14,12},{16,18},{18,... | collective-permute-start | bytes 1179656 | tf_op jit(solution)/shard_map/ppermute | solution.py:50
  52.7 22.9 %collective-permute-start.15 = (bf16[768,256]{1,0:T(8,128)(2,1)}, bf16[768,256]{1,0:T(8,128)(2,1)}, u32[]{:S(2)}, u32[]{:S(2)}) collective-permute-start(bf16[768,256]{1,0:T(8,128)(2,1)} %pad_maximum_fusion.11), channel_id=1, source_target_pairs={{0,1},{1,0},{2,3},{3,2},{4,5},{5,4},{6,7},{7,6},{8,9},{9,8},{10,11... | collective-permute-start | bytes 1179656 | tf_op jit(solution)/shard_map/ppermute | solution.py:45
  53.5 13.7 %collective-permute-start.11 = (bf16[2,128,512]{2,1,0:T(8,128)(2,1)}, bf16[2,128,512]{2,1,0:T(8,128)(2,1)}, u32[]{:S(2)}, u32[]{:S(2)}) collective-permute-start(bf16[2,128,512]{2,1,0:T(8,128)(2,1)} %collective-permute-done.10), channel_id=1, source_target_pairs={{0,2},{2,0},{4,6},{6,4},{8,10},{10,8},{12,14},{14,12},{16,18},{18,... | collective-permute-start | bytes 786440 | tf_op jit(solution)/shard_map/ppermute | solution.py:50
  57.3 3.2 %collective-permute-start.6 = (bf16[64,8,512]{2,1,0:T(8,128)(2,1)S(1)}, bf16[64,8,512]{2,1,0:T(8,128)(2,1)S(1)}, u32[]{:S(2)}, u32[]{:S(2)}) collective-permute-start(bf16[64,8,512]{2,1,0:T(8,128)(2,1)S(1)} %all-to-all-done), channel_id=1, source_target_pairs={{0,2},{2,0},{4,6},{6,4},{8,10},{10,8},{12,14},{14,12},{16,18},{18,... | collective-permute-start | bytes 1572872 | tf_op jit(solution)/shard_map/ppermute | solution.py:50
  66.3 6.2 %collective-permute-start.12 = (bf16[192,512]{1,0:T(8,128)(2,1)S(1)}, bf16[192,512]{1,0:T(8,128)(2,1)S(1)}, u32[]{:S(2)}, u32[]{:S(2)}) collective-permute-start(bf16[192,512]{1,0:T(8,128)(2,1)S(1)} %get-tuple-element.79), channel_id=1, source_target_pairs={{0,1},{1,0},{2,3},{3,2},{4,5},{5,4},{6,7},{7,6},{8,9},{9,8},{10,11... | collective-permute-start | bytes 589832 | tf_op jit(solution)/shard_map/ppermute | solution.py:45
  88.5 14.1 %collective-permute-start.23 = (bf16[64,8,512]{2,1,0:T(8,128)(2,1)S(1)}, bf16[64,8,512]{2,1,0:T(8,128)(2,1)S(1)}, u32[]{:S(2)}, u32[]{:S(2)}) collective-permute-start(bf16[64,8,512]{2,1,0:T(8,128)(2,1)S(1)} %fusion.16), channel_id=1, source_target_pairs={{0,2},{2,0},{4,6},{6,4},{8,10},{10,8},{12,14},{14,12},{16,18},{18,... | collective-permute-start | bytes 1572872 | tf_op jit(solution)/shard_map/ppermute | solution.py:50
  100.8 2.8 %collective-permute-start.20 = (bf16[4,512,256]{2,1,0:T(8,128)(2,1)S(1)}, bf16[4,512,256]{2,1,0:T(8,128)(2,1)S(1)}, u32[]{:S(2)}, u32[]{:S(2)}) collective-permute-start(bf16[4,512,256]{2,1,0:T(8,128)(2,1)S(1)} %constant_dynamic-slice_fusion.3), channel_id=1, source_target_pairs={{0,2},{2,0},{4,6},{6,4},{8,10},{10,8},{12,14},{14,12},{16,18},{18,... | collective-permute-start | bytes 3145736 | tf_op jit(solution)/shard_map/ppermute | solution.py:50
  102.4 2.4 %collective-permute-start.22 = (bf16[768,256]{1,0:T(8,128)(2,1)S(1)}, bf16[768,256]{1,0:T(8,128)(2,1)S(1)}, u32[]{:S(2)}, u32[]{:S(2)}) collective-permute-start(bf16[768,256]{1,0:T(8,128)(2,1)S(1)} %constant_dynamic-slice_fusion.1), channel_id=1, source_target_pairs={{0,2},{2,0},{4,6},{6,4},{8,10},{10,8},{12,14},{14,12},{16,18},{18,... | collective-permute-start | bytes 1179656 | tf_op jit(solution)/shard_map/ppermute | solution.py:50
  102.8 7.5 %collective-permute-start.24 = (bf16[64,8,256]{2,1,0:T(8,128)(2,1)S(1)}, bf16[64,8,256]{2,1,0:T(8,128)(2,1)S(1)}, u32[]{:S(2)}, u32[]{:S(2)}) collective-permute-start(bf16[64,8,256]{2,1,0:T(8,128)(2,1)S(1)} %dynamic-slice_convert_fusion), channel_id=1, source_target_pairs={{0,1},{1,0},{2,3},{3,2},{4,5},{5,4},{6,7},{7,6},{8,9},{9,8},{10,11... | collective-permute-start | bytes 786440 | tf_op jit(solution)/shard_map/ppermute | solution.py:45
  104.0 17.5 %collective-permute-start.21 = (bf16[4,256,256]{2,1,0:T(8,128)(2,1)S(1)}, bf16[4,256,256]{2,1,0:T(8,128)(2,1)S(1)}, u32[]{:S(2)}, u32[]{:S(2)}) collective-permute-start(bf16[4,256,256]{2,1,0:T(8,128)(2,1)S(1)} %constant_dynamic-slice_fusion.2), channel_id=1, source_target_pairs={{0,1},{1,0},{2,3},{3,2},{4,5},{5,4},{6,7},{7,6},{8,9},{9,8},{10,11... | collective-permute-start | bytes 1572872 | tf_op jit(solution)/shard_map/ppermute | solution.py:45
  122.9 40.7 %all-to-all-start.1 = ((bf16[64,72,128]{2,1,0:T(8,128)(2,1)}), bf16[64,72,128]{2,1,0:T(8,128)(2,1)S(1)}, u32[]{:S(2)}, u32[]{:S(2)}) async-start(bf16[64,72,128]{2,1,0:T(8,128)(2,1)} %pad_maximum_fusion.1), calls=%async_computation.1 | async-start | bytes 2359296 | tf_op jit(solution)/shard_map/all_to_all | solution.py:74
  133.2 48.7 %collective-permute-start.9 = (bf16[768,256]{1,0:T(8,128)(2,1)}, bf16[768,256]{1,0:T(8,128)(2,1)}, u32[]{:S(2)}, u32[]{:S(2)}) collective-permute-start(bf16[768,256]{1,0:T(8,128)(2,1)} %constant_dynamic-slice_fusion.12), channel_id=1, source_target_pairs={{0,1},{1,0},{2,3},{3,2},{4,5},{5,4},{6,7},{7,6},{8,9},{9,8},{10,11... | collective-permute-start | bytes 1179656 | tf_op jit(solution)/shard_map/ppermute | solution.py:45
  140.7 31.6 %collective-permute-start.17 = (bf16[256,256]{1,0:T(8,128)(2,1)}, bf16[256,256]{1,0:T(8,128)(2,1)}, u32[]{:S(2)}, u32[]{:S(2)}) collective-permute-start(bf16[256,256]{1,0:T(8,128)(2,1)} %dynamic-slice_convert_fusion.1), channel_id=1, source_target_pairs={{0,1},{1,0},{2,3},{3,2},{4,5},{5,4},{6,7},{7,6},{8,9},{9,8},{10,11... | collective-permute-start | bytes 393224 | tf_op jit(solution)/shard_map/ppermute | solution.py:45
  142.9 40.8 %collective-permute-start.16 = (bf16[768,256]{1,0:T(8,128)(2,1)}, bf16[768,256]{1,0:T(8,128)(2,1)}, u32[]{:S(2)}, u32[]{:S(2)}) collective-permute-start(bf16[768,256]{1,0:T(8,128)(2,1)} %constant_dynamic-slice_fusion.4), channel_id=1, source_target_pairs={{0,1},{1,0},{2,3},{3,2},{4,5},{5,4},{6,7},{7,6},{8,9},{9,8},{10,11... | collective-permute-start | bytes 1179656 | tf_op jit(solution)/shard_map/ppermute | solution.py:45
  164.8 32.3 %all-to-all-start.2 = ((bf16[64,56,128]{2,1,0:T(8,128)(2,1)}), bf16[64,56,128]{2,1,0:T(8,128)(2,1)S(1)}, u32[]{:S(2)}, u32[]{:S(2)}) async-start(bf16[64,56,128]{2,1,0:T(8,128)(2,1)} %broadcast_in_dim.5), calls=%async_computation.2 | async-start | bytes 1835008 | tf_op jit(solution)/shard_map/all_to_all | solution.py:74
  173.3 5.9 %collective-permute-start.18 = (bf16[32,256]{1,0:T(8,128)(2,1)S(1)}, bf16[32,256]{1,0:T(8,128)(2,1)S(1)}, u32[]{:S(2)}, u32[]{:S(2)}) collective-permute-start(bf16[32,256]{1,0:T(8,128)(2,1)S(1)} %get-tuple-element.74), channel_id=1, source_target_pairs={{0,254},{2,0},{4,2},{6,4},{8,6},{10,8},{12,10},{14,12},{16,14},{18... | collective-permute-start | bytes 49160 | tf_op jit(solution)/shard_map/ppermute | solution.py:55
  175.4 6.5 %collective-permute-start.19 = (bf16[32,256]{1,0:T(8,128)(2,1)S(1)}, bf16[32,256]{1,0:T(8,128)(2,1)S(1)}, u32[]{:S(2)}, u32[]{:S(2)}) collective-permute-start(bf16[32,256]{1,0:T(8,128)(2,1)S(1)} %get-tuple-element.73), channel_id=1, source_target_pairs={{0,2},{2,4},{4,6},{6,8},{8,10},{10,12},{12,14},{14,16},{16,18},{18... | collective-permute-start | bytes 49160 | tf_op jit(solution)/shard_map/ppermute | solution.py:55
  197.4 6.0 %collective-permute-start.25 = (bf16[1792,256]{1,0:T(8,128)(2,1)S(1)}, bf16[1792,256]{1,0:T(8,128)(2,1)S(1)}, u32[]{:S(2)}, u32[]{:S(2)}) collective-permute-start(bf16[1792,256]{1,0:T(8,128)(2,1)S(1)} %pad_maximum_fusion.3), channel_id=1, source_target_pairs={{0,2},{2,0},{4,6},{6,4},{8,10},{10,8},{12,14},{14,12},{16,18},{18,... | collective-permute-start | bytes 2752520 | tf_op jit(solution)/shard_map/ppermute | solution.py:50
  (55 other events, 311.1 us)

commit v2 on v1

v2 whole, which is shorter than its diff:
```python
import jax
import jax.numpy as jnp
from jax import lax
from jax.experimental import pallas as pl
from jax.experimental.pallas import tpu as pltpu
from jax.sharding import PartitionSpec as P

HALO = 32
COARSE = 8
FINE = 1152
EPSILON = 1e-05
F32 = jnp.float32
BF16 = jnp.bfloat16
I32 = jnp.int32
LANES = 128
VMEM_LIMIT = 48 * 1024 * 1024


def dot(left, right):
    return jnp.dot(left, right, preferred_element_type=F32)


def contract_rows(left, right):
    return lax.dot_general(left, right, (((0,), (0,)), ((), ())), preferred_element_type=F32)


def contract_cols(left, right):
    return lax.dot_general(left, right, (((1,), (1,)), ((), ())), preferred_element_type=F32)


def layer_norm(values):
    centered = values - jnp.mean(values, axis=1, keepdims=True)
    inverse = lax.rsqrt(jnp.mean(centered * centered, axis=1, keepdims=True) + EPSILON)
    return centered * inverse, inverse


def norm_backward(cotangent, normed, inverse):
    mean = jnp.mean(cotangent, axis=1, keepdims=True)
    crossed = jnp.mean(cotangent * normed, axis=1, keepdims=True)
    return (cotangent - mean - normed * crossed) * inverse


def swish_parts(values):
    sigmoid = jax.nn.sigmoid(values)
    return values * sigmoid, sigmoid * (1.0 + values * (1.0 - sigmoid))


def one_hot(index, width):
    return (index == lax.broadcasted_iota(I32, (index.shape[0], width), 1)).astype(F32).astype(BF16)


def one_hot_t(index, width):
    return (index == lax.broadcasted_iota(I32, (width, index.shape[1]), 0)).astype(F32).astype(BF16)


def swap_lat(value):
    return lax.ppermute(value, "lat", [(0, 1), (1, 0)])


def swap_core(value):
    count = lax.axis_size("patch")
    return lax.ppermute(value, "patch", [(i, i ^ 1) for i in range(count)])


def shifted(value, steps):
    count = lax.axis_size("patch")
    return lax.ppermute(value, "patch", [(i, (i + steps) % count) for i in range(count)])


def other_neighbour(value):
    count = lax.axis_size("patch")
    pairs = []
    for patch in range(count):
        for lat in range(2):
            pairs.append((patch * 2 + lat, (patch ^ 2) * 2 + (1 - lat)))
    return lax.ppermute(value, ("patch", "lat"), pairs)


def chips_all_to_all(value):
    count = lax.axis_size("patch")
    groups = [list(range(core, count, 2)) for core in range(2)]
    return lax.all_to_all(value, "patch", 0, 0, tiled=True, axis_index_groups=groups)


def pairs_all_to_all(value):
    count = lax.axis_size("patch")
    groups = [
        [patch * 2 + lat for patch in range(core, count, 2) for lat in range(2)]
        for core in range(2)
    ]
    return lax.all_to_all(value, ("patch", "lat"), 0, 0, tiled=True, axis_index_groups=groups)


def whole(shape):
    return pl.BlockSpec(shape, lambda i, s: (0,) * len(shape), pipeline_mode=pl.Buffered(1))


def block(shape, index):
    return pl.BlockSpec(shape, index, pipeline_mode=pl.Buffered(1))


def call(kernel, info, operands, in_specs, outs, scratch=(), flops=0, moved=0, name=None):
    return pl.pallas_call(
        kernel,
        grid_spec=pltpu.PrefetchScalarGridSpec(
            num_scalar_prefetch=1,
            grid=(1,),
            in_specs=in_specs,
            out_specs=[whole(shape) for shape, _ in outs],
            scratch_shapes=list(scratch),
        ),
        out_shape=[jax.ShapeDtypeStruct(shape, dtype) for shape, dtype in outs],
        compiler_params=pltpu.CompilerParams(vmem_limit_bytes=VMEM_LIMIT),
        cost_estimate=pl.CostEstimate(flops=flops, bytes_accessed=moved, transcendentals=0),
        name=name,
    )(info, *operands)


def pack_kernel(info, xf, xl, gf, gl, n, ng, wi, wo, ni, no, xs, gs, ns, wes, wns, coarse):
    fine, nodes = xf.shape[0], n.shape[0]
    ns[:nodes] = n[...]
    ns[nodes:] = ng[...]
    xs[:fine] = xf[...]
    xs[fine:] = xl[...]
    gs[:fine] = gf[...]
    gs[fine:] = gl[...]
    wes[:3] = wi[...]
    wes[3] = wo[...]
    wns[:2] = ni[...]
    wns[2] = no[...]
    coarse[...] = jnp.broadcast_to(n[:COARSE][None], coarse.shape)


def results_kernel(info, mine, other, inner, outer, node_inner, node_outer, staged, sems):
    first = info[1] == 0
    blocks, half = mine.shape[0], staged.shape[1]
    targets = [inner.at[0], inner.at[1], inner.at[2], outer, node_inner.at[0], node_inner.at[1], node_outer]
    copies = []
    for k, target in enumerate(targets):
        rows = slice(k * half, (k + 1) * half)
        for i in range(blocks):
            a, b = mine[i, rows].astype(F32), other[i, rows].astype(F32)
            staged[k, :, i * LANES : (i + 1) * LANES] = jnp.where(first, a, b)
            staged[k, :, half + i * LANES : half + (i + 1) * LANES] = jnp.where(first, b, a)
        copies.append(pltpu.make_async_copy(staged.at[k], target, sems.at[k]))
        copies[-1].start()
    for copy in copies:
        copy.wait()


def weights_kernel(info, wi, wo, got, again, full_in, full_out):
    lat, core = info[0], info[1]
    half = wo.shape[0]
    quarter = half // 2
    inner = wi.shape[0]
    first = core == 0
    for k in range(inner):
        full_in[k, :half] = wi[k]
        full_in[k, half : half + quarter] = jnp.where(first, got[k], again[k])
        full_in[k, half + quarter :] = jnp.where(first, again[k], got[k])
    own = wo[...]
    top = jnp.where(first, got[inner], again[inner])
    bottom = jnp.where(first, again[inner], got[inner])
    missing = jnp.concatenate([top, bottom], 0)
    low = lat == 0
    for rows, value in ((slice(0, half), jnp.where(low, own, missing)), (slice(half, 2 * half), jnp.where(low, missing, own))):
        full_out[rows, :half] = jnp.where(low, value[:, :half], value[:, half:])
        full_out[rows, half:] = jnp.where(low, value[:, half:], value[:, :half])


def edge_rows(x, sender, receiver, mask, w_in, w_out, rows, half, slope, act, normed, inverse, out_own, out_sent, update):
    pre = dot(x, w_in[0]) + dot(sender, w_in[1]) + dot(receiver, w_in[2])
    value, derivative = swish_parts(pre)
    value = value.astype(BF16)
    slope[rows] = derivative
    act[rows] = value
    scaled, scale = layer_norm(dot(value, w_out[...]))
    normed[rows] = scaled
    inverse[rows] = scale
    change = scaled if mask is None else scaled * mask
    out = (x.astype(F32) + change).astype(BF16)
    out_own[rows] = out[:, :half]
    out_sent[rows] = out[:, half:]
    update[rows] = change.astype(BF16)


def fine_kernel(info, x_own, x_got, n_own, n_got, low, high, near, recv, recv_t, w_in, w_out,
                slope, act, normed, inverse, out_own, out_sent, partial, ext, update):
    half = x_own.shape[1]
    nodes = n_own.shape[0]
    ext[:HALO] = low[...]
    ext[HALO : HALO + nodes, :half] = n_own[...]
    ext[HALO : HALO + nodes, half:] = n_got[...]
    ext[HALO + nodes :] = high[...]
    node_x = ext[HALO : HALO + nodes]
    chunk = 192
    for start in range(0, x_own.shape[0], chunk):
        rows = pl.ds(start, chunk)
        x = jnp.concatenate([x_own[rows], x_got[rows]], 1)
        sender = dot(one_hot(near[rows], ext.shape[0]), ext[...]).astype(BF16)
        receiver = dot(one_hot(recv[rows], nodes), node_x).astype(BF16)
        edge_rows(x, sender, receiver, None, w_in, w_out, rows, half, slope, act, normed, inverse, out_own, out_sent, update)
    partial[...] = dot(one_hot_t(recv_t[...], nodes), update[...])


def long_kernel(info, x_own, x_got, n_own, n_got, same, other, far_same, far_other, recv, recv_t, mask, w_in, w_out, before,
                slope, act, normed, inverse, out_own, out_sent, partial, sent, sender_rows, update):
    lat = info[0]
    half = x_own.shape[1]
    nodes = n_own.shape[0]
    rows = pl.ds(0, x_own.shape[0])
    count = same.shape[0]
    for side, columns in ((lat, slice(0, half)), (1 - lat, slice(half, 2 * half))):
        value = dot(one_hot(far_same[...] + side * COARSE, count), same[...])
        value = value + dot(one_hot(far_other[...] + side * COARSE, count), other[...])
        sender_rows[:, columns] = value.astype(BF16)
    x = jnp.concatenate([x_own[...], x_got[...]], 1)
    node_x = jnp.concatenate([n_own[...], n_got[...]], 1)
    receiver = dot(one_hot(recv[...], nodes), node_x).astype(BF16)
    edge_rows(x, sender_rows[...], receiver, mask[...], w_in, w_out, rows, half, slope, act, normed, inverse, out_own, out_sent, update)
    total = before[...] + dot(one_hot_t(recv_t[...], nodes), update[...])
    partial[...] = total
    sent[...] = total.astype(BF16)


def back_kernel(info, partial, got, n_own, n_got, ng_own, ng_got, low, high, nin, nout,
                xf_own, xl_own, xf_got, xl_got, gf_own, gl_own, gf_got, gl_got,
                slope_f, slope_l, act_f, act_l, normed_f, normed_l, inverse_f, inverse_l, mask, srow_l,
                recv, recv_t, near_t, far_t, w_in, w_out,
                node_out, node_self, node_keep, node_send, edge_keep, edge_send, far_keep, far_send, dpre, near_sum, recv_sum,
                ndpre, ndy, nact, agg_grad, dy, ext):
    lat, core = info[0], info[1]
    half = n_own.shape[1]
    nodes = n_own.shape[0]
    fine, longs = xf_own.shape[0], xl_own.shape[0]
    mine = pl.ds(pl.multiple_of(core * half, half), half)
    theirs = pl.ds(pl.multiple_of((1 - core) * half, half), half)
    turn = (core + lat) % 2
    mine_own = pl.ds(pl.multiple_of(turn * half, half), half)
    theirs_own = pl.ds(pl.multiple_of((1 - turn) * half, half), half)
    hidden_mine = pl.ds(pl.multiple_of(lat * half, half), half)
    hidden_theirs = pl.ds(pl.multiple_of((1 - lat) * half, half), half)

    ext[:HALO] = low[...]
    ext[HALO : HALO + nodes, :half] = n_own[...]
    ext[HALO : HALO + nodes, half:] = n_got[...]
    ext[HALO + nodes :] = high[...]
    node_x = ext[HALO : HALO + nodes]
    received = got[...].astype(F32)
    agg = (partial[...] + jnp.concatenate([received[:, half:], received[:, :half]], 1)).astype(BF16)
    node_value, node_slope = swish_parts(dot(node_x, nin[0]) + dot(agg, nin[1]))
    nact[...] = node_value.astype(BF16)
    node_normed, node_inverse = layer_norm(dot(nact[...], nout[...]))
    node_out[...] = (n_own[...].astype(F32) + node_normed[:, :half]).astype(BF16)
    node_g = jnp.concatenate([ng_own[...], ng_got[...]], 1).astype(F32)
    ndy[...] = norm_backward(node_g, node_normed, node_inverse).astype(BF16)
    ndpre[...] = (contract_cols(ndy[...], nout[...]) * node_slope).astype(BF16)
    agg_grad[...] = contract_cols(ndpre[...], nin[1]).astype(BF16)
    node_self[...] = ng_own[...].astype(F32) + contract_cols(ndpre[...], nin[0, :half])

    chunk = 192
    for start in range(0, fine + longs, chunk):
        rows = pl.ds(start, chunk)
        if start < fine:
            part = pl.ds(start, chunk)
            g_own, g_got, normed, inverse, slope = gf_own, gf_got, normed_f, inverse_f, slope_f
        else:
            part = pl.ds(start - fine, chunk)
            g_own, g_got, normed, inverse, slope = gl_own, gl_got, normed_l, inverse_l, slope_l
        cotangent = jnp.concatenate([g_own[part], g_got[part]], 1).astype(F32)
        cotangent = cotangent + dot(one_hot(recv[rows], nodes), agg_grad[...])
        if start >= fine:
            cotangent = cotangent * mask[part]
        dy[rows] = norm_backward(cotangent, normed[part], inverse[part]).astype(BF16)
        dpre[rows] = (contract_cols(dy[rows], w_out[...]) * slope[part]).astype(BF16)

    tail = pl.ds(fine, longs)
    head = pl.ds(0, fine)
    srow_grads = contract_cols(dpre[tail], w_in[1]).astype(BF16)
    far = dot(one_hot_t(far_t[...], 2 * far_keep.shape[0]), srow_grads).astype(BF16)
    far_keep[...] = far[: far_keep.shape[0]]
    far_send[...] = far[far_keep.shape[0] :]
    near_sum[...] = dot(one_hot_t(near_t[...], ext.shape[0]), dpre[head]).astype(BF16)
    recv_sum[...] = dot(one_hot_t(recv_t[...], nodes), dpre[...]).astype(BF16)
    for keep, node_keep_ref, columns, columns_own in (
        (edge_send, node_send, theirs, theirs_own),
        (edge_keep, node_keep, mine, mine_own),
    ):
        for side, xf, xl, hidden, cols in (
            (1, xf_got, xl_got, hidden_theirs, slice(half, 2 * half)),
            (0, xf_own, xl_own, hidden_mine, slice(0, half)),
        ):
            grad = contract_rows(xf[...], dpre[head, columns]) + contract_rows(xl[...], dpre[tail, columns])
            keep[side, 0] = grad.astype(BF16)
            grad = contract_rows(ext[:, cols], near_sum[:, columns]) + contract_rows(srow_l[:, cols], dpre[tail, columns])
            keep[side, 1] = grad.astype(BF16)
            keep[side, 2] = contract_rows(ext[HALO : HALO + nodes, cols], recv_sum[:, columns]).astype(BF16)
            grad = contract_rows(act_f[:, hidden], dy[head, columns_own]) + contract_rows(act_l[:, hidden], dy[tail, columns_own])
            keep[side, 3] = grad.astype(BF16)
        node_keep_ref[0] = contract_rows(n_own[...], ndpre[:, columns]).astype(BF16)
        node_keep_ref[1] = contract_rows(agg[:, :half], ndpre[:, columns]).astype(BF16)
        node_keep_ref[2] = contract_rows(nact[:, hidden_mine], ndy[:, columns_own]).astype(BF16)


def inputs_kernel(info, dpre, gf_own, gl_own, g_got, near_sum, recv_sum, w_in,
                  grads_own, grads_sent, rim_own, rim_sent):
    half = g_got.shape[1]
    fine, longs = gf_own.shape[0], gl_own.shape[0]
    nodes = recv_sum.shape[0]
    for start, rows, own in ((0, fine, gf_own), (fine, longs, gl_own)):
        part = pl.ds(start, rows)
        change = contract_cols(dpre[part], w_in[0])
        grads_own[part] = (own[...].astype(F32) + change[:, :half]).astype(BF16)
        grads_sent[part] = (g_got[part].astype(F32) + change[:, half:]).astype(BF16)
    near = contract_cols(near_sum[...], w_in[1])
    received = contract_cols(recv_sum[...], w_in[2])
    for rows, value in (
        (slice(0, HALO), near[:HALO]),
        (slice(HALO, HALO + nodes), near[HALO : HALO + nodes] + received),
        (slice(HALO + nodes, 2 * HALO + nodes), near[HALO + nodes :]),
    ):
        rim_own[rows] = value[:, :half]
        rim_sent[rows] = value[:, half:].astype(BF16)


def body(
    node_latents,
    edge_latents,
    senders,
    receivers,
    long_count,
    edge_inner,
    edge_outer,
    node_inner,
    node_outer,
    node_cotangent,
    edge_cotangent,
):
    nodes, half = node_latents.shape
    full = 2 * half
    edges = edge_latents.shape[0]
    rows = edges // 2
    fine, longs = FINE // 2, (edges - FINE) // 2
    quarter = half // 2
    patches = lax.axis_size("patch")
    chips = patches // 2
    extent = nodes + 2 * HALO
    lat = lax.axis_index("lat")
    patch = lax.axis_index("patch")
    core = patch % 2
    first_node = patch * nodes
    info = jnp.stack([lat, core]).astype(I32)

    fine_other = block((fine, half), lambda i, s: (1 - s[0], 0))
    long_other = block((longs, half), lambda i, s: (FINE // longs + 1 - s[0], 0))
    quarter_rows = block((quarter, full), lambda i, s: (s[1], 0))
    sent_x, sent_g, sent_n, sent_we, sent_wn, sent_coarse = call(
        pack_kernel,
        info,
        (edge_latents, edge_latents, edge_cotangent, edge_cotangent, node_latents, node_cotangent,
         edge_inner, edge_outer, node_inner, node_outer),
        [
            fine_other, long_other, fine_other, long_other, whole((nodes, half)), whole((nodes, half)),
            block((3, quarter, full), lambda i, s: (0, s[1], 0)), quarter_rows,
            block((2, quarter, full), lambda i, s: (0, s[1], 0)), quarter_rows,
        ],
        [
            ((rows, half), BF16),
            ((rows, half), BF16),
            ((2 * nodes, half), BF16),
            ((4, quarter, full), BF16),
            ((3, quarter, full), BF16),
            ((patches, COARSE, half), BF16),
        ],
        moved=5_000_000,
        name="pack",
    )
    node_got = swap_lat(sent_n)
    we_got = other_neighbour(sent_we)
    x_got = swap_lat(sent_x)
    same = pairs_all_to_all(sent_coarse)
    other = swap_core(same)
    same, other = same.reshape(patches * COARSE, half), other.reshape(patches * COARSE, half)
    low = shifted(
        jnp.concatenate([node_latents[nodes - HALO :], node_got[nodes - HALO : nodes]], 1), 1
    )
    high = shifted(jnp.concatenate([node_latents[:HALO], node_got[:HALO]], 1), -1)
    we_again = swap_core(we_got)
    wn_got = other_neighbour(sent_wn)
    wn_again = swap_core(wn_got)
    g_got = swap_lat(sent_g)

    def rows_of(value):
        return jnp.concatenate(
            [
                lax.dynamic_slice_in_dim(value, lat * fine, fine, 0),
                lax.dynamic_slice_in_dim(value, FINE + lat * longs, longs, 0),
            ]
        )

    sender_ids = rows_of(senders.reshape(edges))
    recv = rows_of(receivers.reshape(edges)) - first_node
    near = (sender_ids[:fine] - first_node + HALO) % (nodes * patches)
    far_ids = sender_ids[fine:]
    far_patch, far_row = far_ids // nodes, far_ids % nodes
    is_same = far_patch % 2 == core
    far_base = far_patch // 2 * (2 * COARSE) + far_row
    far_same = jnp.where(is_same, far_base, -4 * patches * COARSE)
    far_other = jnp.where(is_same, -4 * patches * COARSE, far_base)
    far_slot = jnp.where(is_same, 0, chips * COARSE) + far_patch // 2 * COARSE + far_row
    mask = (jnp.arange(longs, dtype=I32) + lat * longs < long_count[0]).astype(F32)[:, None]
    recv_c, recv_r = recv[:, None], recv[None, :]
    recv_fc, recv_fr = recv[:fine, None], recv[None, :fine]
    recv_lc, recv_lr = recv[fine:, None], recv[None, fine:]

    def weights_of(wi, wo, got, again, name):
        count = wi.shape[0]
        return call(
            weights_kernel,
            info,
            (wi, wo, got, again),
            [
                whole((count, half, full)),
                whole((half, full)),
                whole((count + 1, quarter, full)),
                whole((count + 1, quarter, full)),
            ],
            [((count, full, full), BF16), ((full, full), BF16)],
            moved=4 * (count + 1) * full * full,
            name=name,
        )

    w_in, w_out = weights_of(edge_inner, edge_outer, we_got, we_again, "edge_weights")
    nin, nout = weights_of(node_inner, node_outer, wn_got, wn_again, "node_weights")

    def fine_own():
        return block((fine, half), lambda i, s: (s[0], 0))

    def long_own():
        return block((longs, half), lambda i, s: (FINE // longs + s[0], 0))

    def fine_got():
        return whole((fine, half))

    def long_got():
        return block((longs, half), lambda i, s: (fine // longs, 0))

    node_spec = whole((nodes, half))
    second_nodes = block((nodes, half), lambda i, s: (1, 0))
    rim = whole((HALO, full))
    win_spec, wout_spec = whole((3, full, full)), whole((full, full))

    def forward_outs(count):
        return [
            ((count, full), F32),
            ((count, full), BF16),
            ((count, full), F32),
            ((count, 1), F32),
            ((count, half), BF16),
            ((count, half), BF16),
            ((nodes, full), F32),
        ]

    slope_f, act_f, normed_f, inverse_f, fine_out, fine_sent, partial_f = call(
        fine_kernel,
        info,
        (edge_latents, x_got, node_latents, node_got, low, high, near[:, None], recv_fc, recv_fr, w_in, w_out),
        [
            fine_own(), fine_got(), node_spec, whole((nodes, half)), rim, rim,
            whole((fine, 1)), whole((fine, 1)), whole((1, fine)), win_spec, wout_spec,
        ],
        forward_outs(fine),
        [pltpu.VMEM((extent, full), BF16), pltpu.VMEM((fine, full), BF16)],
        flops=2 * fine * full * (4 * full + extent + 2 * nodes),
        moved=8_000_000,
        name="edges_forward_fine",
    )
    slope_l, act_l, normed_l, inverse_l, long_out, long_sent, partial, partial_sent, srow_l = call(
        long_kernel,
        info,
        (edge_latents, x_got, node_latents, node_got, same, other, far_same[:, None], far_other[:, None],
         recv_lc, recv_lr, mask, w_in, w_out, partial_f),
        [
            long_own(), long_got(), node_spec, whole((nodes, half)),
            whole((patches * COARSE, half)), whole((patches * COARSE, half)),
            whole((longs, 1)), whole((longs, 1)), whole((longs, 1)), whole((1, longs)), whole((longs, 1)),
            win_spec, wout_spec, whole((nodes, full)),
        ],
        forward_outs(longs) + [((nodes, full), BF16), ((longs, full), BF16)],
        [pltpu.VMEM((longs, full), BF16)],
        flops=2 * longs * full * (4 * full + 4 * patches * COARSE + 2 * nodes),
        moved=6_000_000,
        name="edges_forward_long",
    )
    partial_got = swap_lat(partial_sent)

    (node_output, node_self, node_keep, node_send, edge_keep, edge_send, far_keep, far_send,
     dpre, near_sum, recv_sum) = call(
        back_kernel,
        info,
        (partial, partial_got, node_latents, node_got, node_cotangent, node_got, low, high, nin, nout,
         edge_latents, edge_latents, x_got, x_got, edge_cotangent, edge_cotangent, g_got, g_got,
         slope_f, slope_l, act_f, act_l, normed_f, normed_l, inverse_f, inverse_l, mask, srow_l,
         recv_c, recv_r, near[None, :], far_slot[None, :], w_in, w_out),
        [
            whole((nodes, full)), whole((nodes, full)), node_spec, whole((nodes, half)), node_spec, second_nodes,
            rim, rim, whole((2, full, full)), wout_spec,
            fine_own(), long_own(), fine_got(), long_got(), fine_own(), long_own(), fine_got(), long_got(),
            whole((fine, full)), whole((longs, full)), whole((fine, full)), whole((longs, full)),
            whole((fine, full)), whole((longs, full)), whole((fine, 1)), whole((longs, 1)), whole((longs, 1)),
            whole((longs, full)),
            whole((rows, 1)), whole((1, rows)), whole((1, fine)), whole((1, longs)), win_spec, wout_spec,
        ],
        [
            ((nodes, half), BF16),
            ((nodes, half), F32),
            ((3, half, half), BF16),
            ((3, half, half), BF16),
            ((2, 4, half, half), BF16),
            ((2, 4, half, half), BF16),
            ((chips * COARSE, full), BF16),
            ((chips * COARSE, full), BF16),
            ((rows, full), BF16),
            ((extent, full), BF16),
            ((nodes, full), BF16),
        ],
        [
            pltpu.VMEM((nodes, full), BF16),
            pltpu.VMEM((nodes, full), BF16),
            pltpu.VMEM((nodes, full), BF16),
            pltpu.VMEM((nodes, full), BF16),
            pltpu.VMEM((rows, full), BF16),
            pltpu.VMEM((extent, full), BF16),
        ],
        flops=8 * rows * full * full,
        moved=14_000_000,
        name="nodes_and_edges_backward",
    )

    core_edge, core_far, core_node = swap_core(edge_send), swap_core(far_send), swap_core(node_send)
    edge_parts = edge_keep.astype(F32) + core_edge.astype(F32)
    far_parts = far_keep.astype(F32) + core_far.astype(F32)
    node_parts = node_keep.astype(F32) + core_node.astype(F32)
    edge_sent, far_sent = edge_parts[1].astype(BF16), far_parts[:, half:].astype(BF16)
    middle = chips * COARSE // 2
    lat_edge = jnp.concatenate([swap_lat(edge_sent[:2]), other_neighbour(edge_sent[2:])], 0)
    lat_far = jnp.concatenate([swap_lat(far_sent[:middle]), other_neighbour(far_sent[middle:])], 0)
    weight_parts = jnp.concatenate(
        [(edge_parts[0] + lat_edge.astype(F32)).reshape(4 * half, half), node_parts.reshape(3 * half, half)], 0
    ).astype(BF16)
    far_own = (far_parts[:, :half] + lat_far.astype(F32)).astype(BF16).reshape(chips, COARSE, half)
    blocks = half // LANES
    total_rows = weight_parts.shape[0] * blocks
    share = total_rows // chips
    weight_parts = jnp.concatenate(
        [weight_parts[:, i * LANES : (i + 1) * LANES] for i in range(blocks)], 0
    ).reshape(chips, share, LANES)
    far_own = jnp.concatenate(
        [far_own[:, :, i * LANES : (i + 1) * LANES] for i in range(blocks)], 1
    )
    arrived = chips_all_to_all(jnp.concatenate([weight_parts, far_own], 1))

    grads_own, grads_sent, rim_own, rim_sent = call(
        inputs_kernel,
        info,
        (dpre, edge_cotangent, edge_cotangent, g_got, near_sum, recv_sum, w_in),
        [
            whole((rows, full)), fine_own(), long_own(), whole((rows, half)),
            whole((extent, full)), whole((nodes, full)), win_spec,
        ],
        [((rows, half), BF16), ((rows, half), BF16), ((extent, half), F32), ((extent, half), BF16)],
        flops=4 * rows * full * full,
        moved=5_000_000,
        name="input_gradients",
    )

    def ordered(mine, other):
        return jnp.where(lat == 0, jnp.concatenate([mine, other], 0), jnp.concatenate([other, mine], 0))

    def back_to_columns(fine_mine, long_mine, got):
        return jnp.concatenate([ordered(fine_mine, got[:fine]), ordered(long_mine, got[fine:])], 0)

    edge_output = back_to_columns(fine_out, long_out, swap_lat(jnp.concatenate([fine_sent, long_sent], 0)))
    edge_grads = back_to_columns(grads_own[:fine], grads_own[fine:], swap_lat(grads_sent))
    summed = rim_own + swap_lat(rim_sent).astype(F32)
    to_low = shifted(summed[:HALO].astype(BF16), -1).astype(F32)
    to_high = shifted(summed[HALO + nodes :].astype(BF16), 1).astype(F32)

    total = jnp.sum(arrived.astype(F32), 0)
    coarse_share = jnp.concatenate(
        [total[share + i * COARSE : share + (i + 1) * COARSE] for i in range(blocks)], 1
    )
    weight_share = (total[:share] / patches).astype(BF16)
    own_grads = node_self + summed[HALO : HALO + nodes]
    own_grads = own_grads.at[nodes - HALO :].add(to_low)
    own_grads = own_grads.at[:HALO].add(to_high)
    own_grads = own_grads.at[:COARSE].add(coarse_share)
    node_grads = own_grads.astype(BF16)
    mine = chips_all_to_all(jnp.broadcast_to(weight_share[None], (chips, share, LANES)))
    mine = mine.reshape(blocks, total_rows // blocks, LANES)
    other = swap_core(mine)
    square = (half, full)
    weights = pl.pallas_call(
        results_kernel,
        grid_spec=pltpu.PrefetchScalarGridSpec(
            num_scalar_prefetch=1,
            grid=(1,),
            in_specs=[whole(mine.shape)] * 2,
            out_specs=[pl.BlockSpec(memory_space=pl.ANY)] * 4,
            scratch_shapes=[pltpu.VMEM((7,) + square, F32), pltpu.SemaphoreType.DMA((7,))],
        ),
        out_shape=[jax.ShapeDtypeStruct(shape, F32) for shape in ((3,) + square, square, (2,) + square, square)],
        compiler_params=pltpu.CompilerParams(vmem_limit_bytes=VMEM_LIMIT),
        cost_estimate=pl.CostEstimate(flops=0, bytes_accessed=6_000_000, transcendentals=0),
        name="results",
    )(info, mine, other)
    return (edge_output, node_output, edge_grads, node_grads, *weights)


def solution(mesh):
    placed = (
        P("patch", "lat"),
        P("patch", "lat"),
        P("patch", None),
        P("patch", None),
        P("patch"),
        P(None, "lat", None),
        P("lat", None),
        P(None, "lat", None),
        P("lat", None),
        P("patch", "lat"),
        P("patch", "lat"),
    )
    return jax.shard_map(
        body,
        mesh=mesh,
        in_specs=placed,
        out_specs=(
            P("patch", "lat"),
            P("patch", "lat"),
            P("patch", "lat"),
            P("patch", "lat"),
            P(None, "lat", None),
            P("lat", None),
            P(None, "lat", None),
            P("lat", None),
        ),
        check_vma=False,
    )
```

time: 211 us -> 210 us (level); the launches traced: 208 us -> 209 us
  Pallas kernels: 0 us -> 30.1 us
  matrix products: 22.5 us -> 0 us
  waiting for transfers between devices: 52.7 us -> 71.9 us
  starting transfers between devices: 78.8 us -> 63.5 us
  other arithmetic: 22 us -> 11 us
    pallas_call x0 -> x8, Pallas kernels: none -> 30.1 us  [the longest x7 27.6 us: call(): pl.pallas_call(kernel, grid_spec=pltpu.PrefetchScalarGridSpec(num_scalar_...]
    ppermute x4, waiting for transfers between devices: 0.01 us -> 26.6 us  [other_neighbour(): return lax.ppermute(value, ('patch', 'lat'), pairs)]
    dot_general x27 -> x0, matrix products: 22.5 us -> none  [the longest x11 8.81 us: dot(): return jnp.dot(left, right, preferred_element_type=F32)]
    ppermute x9, waiting for transfers between devices: 20 us -> 4.58 us  [swap_lat(): return lax.ppermute(value, 'lat', [(0, 1), (1, 0)])]
    unnamed x114 -> x106, local copies, waits for them, and re-layouts: 5.74 us -> 20.9 us
    ppermute x9 -> x7, starting transfers between devices: 26.8 us -> 13 us  [swap_core(): return lax.ppermute(value, 'patch', [(i, i ^ 1) for i in range(count)])]
    dynamic_slice x15 -> x2, local copies, waits for them, and re-layouts: 11.2 us -> 0.16 us  [the longest x1 0.08 us: rows_of(): lax.dynamic_slice_in_dim(value, FINE + lat * longs, longs, 0)]
    slice x17 -> x13, local copies, waits for them, and re-layouts: 9.38 us -> 2.17 us  [the longest x2 1 us: back_to_columns(): got[:fine]]
  transfers between devices with their start and end apart: 29 -> 27, of which waited for: 9 -> 11; matrix products, arithmetic and copies ran while one was open for 24% -> 9% of each run, Pallas kernels for 0% -> 7%
where the time goes in v2:
time: 210 us; the launch traced here: 209 us
  waiting for transfers between devices  71.9 us (34%)
  starting transfers between devices  63.5 us (30%)
  local copies, waits for them, and re-layouts  30.5 us (15%)
  Pallas kernels  30.1 us (14%)
  other arithmetic  11 us (5%)
    all_to_all x2, waiting for transfers between devices, chips_all_to_all(): lax.all_to_all(value, 'patch', 0, 0, tiled=True, axis_index_groups=groups)  33.8 us
    pallas_call x7, Pallas kernels, call(): pl.pallas_call(kernel, grid_spec=pltpu.PrefetchScalarGridSpec(num_scalar_...  27.6 us
    ppermute x4, waiting for transfers between devices, other_neighbour(): return lax.ppermute(value, ('patch', 'lat'), pairs)  26.6 us
    unnamed x106, local copies, waits for them, and re-layouts  20.9 us
    all_to_all x1, starting transfers between devices, pairs_all_to_all(): lax.all_to_all(value, ('patch', 'lat'), 0, 0, tiled=True, axis_index_grou...  16.5 us
    all_to_all x2, starting transfers between devices, chips_all_to_all(): lax.all_to_all(value, 'patch', 0, 0, tiled=True, axis_index_groups=groups)  15.1 us
    ppermute x7, starting transfers between devices, swap_core(): return lax.ppermute(value, 'patch', [(i, i ^ 1) for i in range(count)])  13 us
    ppermute x9, starting transfers between devices, swap_lat(): return lax.ppermute(value, 'lat', [(0, 1), (1, 0)])  8.82 us
  transfers between devices with their start and end apart: 27, of which 11 were waited for; matrix products, arithmetic and copies ran while one was open for 9% of the time, Pallas kernels for 7%

profile of v2, /device:TPU:1, one launch (start us, length us, event | category | flops | bytes accessed | tf_op | source)
XLA Modules:
  0.0 209.1 jit_solution(1779155374510911226)
XLA Ops:
  8.9 1.7 pack.1
  12.1 16.5 %all-to-all-start = ((bf16[128,8,256]{2,1,0:T(8,128)(2,1)}), bf16[128,8,256]{2,1,0:T(8,128)(2,1)S(1)}, u32[]{:S(2)}, u32[]{:S(2)}) async-start(bf16[128,8,256]{2,1,0:T(8,128)(2,1)} %get-tuple-element.96), calls=%async_computation | async-start | bytes 1048576 | tf_op jit(solution)/shard_map/all_to_all | solution.py:91
  30.1 1.8 collective-permute-start.9
  35.1 21.9 %collective-permute-done.4.got = bf16[4,128,512]{2,1,0:T(8,128)(2,1)S(1)} collective-permute-done((bf16[4,128,512]{2,1,0:T(8,128)(2,1)}, bf16[4,128,512]{2,1,0:T(8,128)(2,1)S(1)}, u32[]{:S(2)}, u32[]{:S(2)}) %collective-permute-start.4) | collective-permute-done | bytes 524320 | tf_op jit(solution)/shard_map/ppermute | solution.py:76
  57.0 1.6 collective-permute-start.5
  59.5 1.3 collective-permute-start.2
  64.6 1.4 copy.35.far_other
  68.9 1.8 edge_weights.1
  73.0 6.0 %collective-permute-start.10 = (bf16[3,128,512]{2,1,0:T(8,128)(2,1)}, bf16[3,128,512]{2,1,0:T(8,128)(2,1)S(1)}, u32[]{:S(2)}, u32[]{:S(2)}) collective-permute-start(bf16[3,128,512]{2,1,0:T(8,128)(2,1)} %collective-permute-done.9.got), channel_id=1, source_target_pairs={{0,2},{2,0},{4,6},{6,4},{8,10},{10,8},{12,14},{14,12},{16,18},{18,... | collective-permute-start | bytes 1179656 | tf_op jit(solution)/shard_map/ppermute | solution.py:62
  79.0 5.6 %edges_forward_fine.1 = (f32[576,512]{1,0:T(8,128)S(1)}, bf16[576,512]{1,0:T(8,128)(2,1)S(1)}, f32[576,512]{1,0:T(8,128)}, f32[576,1]{1,0:T(8,128)S(1)}, bf16[57...) custom-call(s32[2]{0:T(128)S(1)} %pad_add_fusion.1.info, ...), custom_call_target="tpu_custom_call" | custom-call | flops 1585446912 | bytes 8000000 | tf_op jit(solution)/shard_map/edges_forward_fine/pallas_call | solution.py:103
  87.9 3.7 %edges_forward_long.1 = (f32[192,512]{1,0:T(8,128)S(1)}, bf16[192,512]{1,0:T(8,128)(2,1)S(1)}, f32[192,512]{1,0:T(8,128)S(1)}, f32[192,1]{1,0:T(8,128)S(1)}, bf1...) custom-call(s32[2]{0:T(128)S(1)} %pad_add_fusion.1.info, ...), custom_call_target="tpu_custom_call" | custom-call | flops 1283457024 | bytes 6000000 | tf_op jit(solution)/shard_map/edges_forward_long/pallas_call | solution.py:103
  92.2 1.5 collective-permute-start.8
  93.7 1.7 node_weights.1
  97.2 1.5 collective-permute-done.8.got
  98.7 11.0 %nodes_and_edges_backward.1 = (bf16[192,256]{1,0:T(8,128)(2,1)}, f32[192,256]{1,0:T(8,128)S(1)}, bf16[3,256,256]{2,1,0:T(8,128)(2,1)S(1)}, bf16[3,256,256]{2,1,0...) custom-call(s32[2]{0:T(128)S(1)} %pad_add_fusion.1.info, ...), custom_call_target="tpu_custom_call" | custom-call | flops 1610612736 | bytes 14000000 | tf_op jit(solution)/shard_map/nodes_and_edges_backward/pallas_call | solution.py:103
  113.2 1.5 collective-permute-start.21
  115.2 1.2 collective-permute-start.17
  116.4 1.6 collective-permute-start.18
  118.0 2.3 %collective-permute-done.22 = bf16[256,256]{1,0:T(8,128)(2,1)S(1)} collective-permute-done((bf16[256,256]{1,0:T(8,128)(2,1)S(1)}, bf16[256,256]{1,0:T(8,128)(2,1)S(1)}, u32[]{:S(2)}, u32[]{:S(2)}) %collective-permute-start.22) | collective-permute-done | bytes 131104 | tf_op jit(solution)/shard_map/ppermute | solution.py:76
  120.6 3.1 %collective-permute-done.17 = bf16[2,256,256]{2,1,0:T(8,128)(2,1)S(1)} collective-permute-done((bf16[2,256,256]{2,1,0:T(8,128)(2,1)S(1)}, bf16[2,256,256]{2,1,0:T(8,128)(2,1)S(1)}, u32[]{:S(2)}, u32[]{:S(2)}) %collective-permute-start.17) | collective-permute-done | bytes 262176 | tf_op jit(solution)/shard_map/ppermute | solution.py:57
  123.7 2.3 %collective-permute-done.18 = bf16[2,256,256]{2,1,0:T(8,128)(2,1)S(1)} collective-permute-done((bf16[2,256,256]{2,1,0:T(8,128)(2,1)S(1)}, bf16[2,256,256]{2,1,0:T(8,128)(2,1)S(1)}, u32[]{:S(2)}, u32[]{:S(2)}) %collective-permute-start.18) | collective-permute-done | bytes 262176 | tf_op jit(solution)/shard_map/ppermute | solution.py:76
  127.4 7.3 %all-to-all-start.1 = ((bf16[64,72,128]{2,1,0:T(8,128)(2,1)}), bf16[64,72,128]{2,1,0:T(8,128)(2,1)}, u32[]{:S(2)}, u32[]{:S(2)}) async-start(bf16[64,72,128]{2,1,0:T(8,128)(2,1)} %pad_maximum_fusion), calls=%async_computation.1 | async-start | bytes 2359296 | tf_op jit(solution)/shard_map/all_to_all | solution.py:82
  134.8 1.8 pad_maximum_fusion.5
  138.8 2.2 %input_gradients.1 = (bf16[768,256]{1,0:T(8,128)(2,1)S(1)}, bf16[768,256]{1,0:T(8,128)(2,1)}, f32[256,256]{1,0:T(8,128)S(1)}, bf16[256,256]{1,0:T(8,128)(2,1)}) custom-call(s32[2]{0:T(128)S(1)} %pad_add_fusion.1.info, bf16[768,512]{1,0:T(8,128)(2,1)S(1)} %copy-done.19, bf16[1536,256]{1,0:T(8,128)(2,1)S(1)} %copy-done.1, bf16[1536,256]{1,0:T(8,128)(2,1)S(1)} %copy-done.1, ...), custom_call_target="tpu_custom_call" | custom-call | flops 805306368 | bytes 5000000 | tf_op jit(solution)/shard_map/input_gradients/pallas_call | solution.py:103
  143.2 22.2 %all-to-all-done.1 = bf16[64,72,128]{2,1,0:T(8,128)(2,1)} async-done(((bf16[64,72,128]{2,1,0:T(8,128)(2,1)}), bf16[64,72,128]{2,1,0:T(8,128)(2,1)}, u32[]{:S(2)}, u32[]{:S(2)}) %all-to-all-start.1) | async-done | bytes 1179680 | tf_op jit(solution)/shard_map/all_to_all | solution.py:82
  165.4 1.5 convert_reduce_fusion
  167.9 7.8 %all-to-all-start.2 = ((bf16[64,56,128]{2,1,0:T(8,128)(2,1)}), bf16[64,56,128]{2,1,0:T(8,128)(2,1)S(1)}, u32[]{:S(2)}, u32[]{:S(2)}) async-start(bf16[64,56,128]{2,1,0:T(8,128)(2,1)} %broadcast_in_dim.59), calls=%async_computation.2 | async-start | bytes 1835008 | tf_op jit(solution)/shard_map/all_to_all | solution.py:82
  175.8 4.6 %collective-permute-start.15 = (bf16[32,256]{1,0:T(8,128)(2,1)S(1)}, bf16[32,256]{1,0:T(8,128)(2,1)S(1)}, u32[]{:S(2)}, u32[]{:S(2)}) collective-permute-start(bf16[32,256]{1,0:T(8,128)(2,1)S(1)} %get-tuple-element.153), channel_id=1, source_target_pairs={{0,2},{2,4},{4,6},{6,8},{8,10},{10,12},{12,14},{14,16},{16,18},{18... | collective-permute-start | bytes 49160 | tf_op jit(solution)/shard_map/ppermute | solution.py:67
  180.4 5.0 %collective-permute-done.14 = bf16[32,256]{1,0:T(8,128)(2,1)S(1)} collective-permute-done((bf16[32,256]{1,0:T(8,128)(2,1)S(1)}, bf16[32,256]{1,0:T(8,128)(2,1)S(1)}, u32[]{:S(2)}, u32[]{:S(2)}) %collective-permute-start.14) | collective-permute-done | bytes 16416 | tf_op jit(solution)/shard_map/ppermute | solution.py:67
  188.8 11.6 %all-to-all-done.2 = bf16[64,56,128]{2,1,0:T(8,128)(2,1)S(1)} async-done(((bf16[64,56,128]{2,1,0:T(8,128)(2,1)}), bf16[64,56,128]{2,1,0:T(8,128)(2,1)S(1)}, u32[]{:S(2)}, u32[]{:S(2)}) %all-to-all-start.2) | async-done | bytes 917536 | tf_op jit(solution)/shard_map/all_to_all | solution.py:82
  200.3 3.9 %collective-permute-start.23 = (bf16[2,1792,128]{2,1,0:T(8,128)(2,1)S(1)}, bf16[2,1792,128]{2,1,0:T(8,128)(2,1)S(1)}, u32[]{:S(2)}, u32[]{:S(2)}) collective-permute-start(bf16[2,1792,128]{2,1,0:T(8,128)(2,1)S(1)} %bitcast.30), channel_id=1, source_target_pairs={{0,2},{2,0},{4,6},{6,4},{8,10},{10,8},{12,14},{14,12},{16,18},{18,... | collective-permute-start | bytes 2752520 | tf_op jit(solution)/shard_map/ppermute | solution.py:62
  206.4 2.5 %results.1 = (f32[3,256,512]{2,1,0:T(8,128)}, f32[256,512]{1,0:T(8,128)}, f32[2,256,512]{2,1,0:T(8,128)}, f32[256,512]{1,0:T(8,128)}) custom-call(s32[2]{0:T(128)S(1)} %pad_add_fusion.1.info, bf16[2,1792,128]{2,1,0:T(8,128)(2,1)S(1)} %bitcast.31, bf16[2,1792,128]{2,1,0:T(8,128)(2,1)S(1)} %collective-permute-done.23.other), custom_call_target="tpu_custom_call" | custom-call | bytes 6000000 | tf_op jit(solution)/shard_map/results/pallas_call | solution.py:603
  (199 shorter events, 45.7 us)
Async XLA Ops:
  8.9 23.9 %copy-start.52 = (s32[12,128]{1,0:T(8,128)S(1)}, s32[12,128]{1,0:T(8,128)}, u32[]{:S(2)}) copy-start(s32[12,128]{1,0:T(8,128)} %param.20) | copy-start | bytes 18436
  8.9 24.8 %copy-start.51 = (s32[12,128]{1,0:T(8,128)S(1)}, s32[12,128]{1,0:T(8,128)}, u32[]{:S(2)}) copy-start(s32[12,128]{1,0:T(8,128)} %param.19) | copy-start | bytes 18436
  8.9 26.2 %copy-start.13 = (bf16[192,256]{1,0:T(8,128)(2,1)S(1)}, bf16[192,256]{1,0:T(8,128)(2,1)}, u32[]{:S(2)}) copy-start(bf16[192,256]{1,0:T(8,128)(2,1)} %n_own.5) | copy-start | bytes 294916
  12.1 55.7 %copy-start.7 = (bf16[3,256,512]{2,1,0:T(8,128)(2,1)S(1)}, bf16[3,256,512]{2,1,0:T(8,128)(2,1)}, u32[]{:S(2)}) copy-start(bf16[3,256,512]{2,1,0:T(8,128)(2,1)} %wi.4) | copy-start | bytes 2359300
  12.1 55.7 %copy-start.16 = (bf16[256,512]{1,0:T(8,128)(2,1)S(1)}, bf16[256,512]{1,0:T(8,128)(2,1)}, u32[]{:S(2)}) copy-start(bf16[256,512]{1,0:T(8,128)(2,1)} %wo.4) | copy-start | bytes 786436
  12.1 47.4 %all-to-all-start = ((bf16[128,8,256]{2,1,0:T(8,128)(2,1)}), bf16[128,8,256]{2,1,0:T(8,128)(2,1)S(1)}, u32[]{:S(2)}, u32[]{:S(2)}) async-start(bf16[128,8,256]{2,1,0:T(8,128)(2,1)} %get-tuple-element.96), calls=%async_computation | async-start | bytes 1048576 | tf_op jit(solution)/shard_map/all_to_all | solution.py:91
  28.6 30.9 %collective-permute-start.1 = (bf16[384,256]{1,0:T(8,128)(2,1)S(1)}, bf16[384,256]{1,0:T(8,128)(2,1)S(1)}, u32[]{:S(2)}, u32[]{:S(2)}) collective-permute-start(bf16[384,256]{1,0:T(8,128)(2,1)S(1)} %get-tuple-element.90), channel_id=1, source_target_pairs={{0,1},{1,0},{2,3},{3,2},{4,5},{5,4},{6,7},{7,6},{8,9},{9,8},{10,11... | collective-permute-start | bytes 589832 | tf_op jit(solution)/shard_map/ppermute | solution.py:57
  29.2 49.7 %collective-permute-start = (bf16[768,256]{1,0:T(8,128)(2,1)}, bf16[768,256]{1,0:T(8,128)(2,1)S(1)}, u32[]{:S(2)}, u32[]{:S(2)}) collective-permute-start(bf16[768,256]{1,0:T(8,128)(2,1)} %get-tuple-element.89), channel_id=1, source_target_pairs={{0,1},{1,0},{2,3},{3,2},{4,5},{5,4},{6,7},{7,6},{8,9},{9,8},{10,11... | collective-permute-start | bytes 1179656 | tf_op jit(solution)/shard_map/ppermute | solution.py:57
  30.1 42.9 %collective-permute-start.9 = (bf16[3,128,512]{2,1,0:T(8,128)(2,1)}, bf16[3,128,512]{2,1,0:T(8,128)(2,1)}, u32[]{:S(2)}, u32[]{:S(2)}) collective-permute-start(bf16[3,128,512]{2,1,0:T(8,128)(2,1)} %get-tuple-element.102), channel_id=1, source_target_pairs={{0,5},{1,4},{2,7},{3,6},{4,1},{5,0},{6,3},{7,2},{8,13},{9,12},{10,... | collective-permute-start | bytes 1179656 | tf_op jit(solution)/shard_map/ppermute | solution.py:76
  31.9 25.1 %collective-permute-start.4 = (bf16[4,128,512]{2,1,0:T(8,128)(2,1)}, bf16[4,128,512]{2,1,0:T(8,128)(2,1)S(1)}, u32[]{:S(2)}, u32[]{:S(2)}) collective-permute-start(bf16[4,128,512]{2,1,0:T(8,128)(2,1)} %copy-done.46), channel_id=1, source_target_pairs={{0,5},{1,4},{2,7},{3,6},{4,1},{5,0},{6,3},{7,2},{8,13},{9,12},{10,... | collective-permute-start | bytes 1572872 | tf_op jit(solution)/shard_map/ppermute | solution.py:76
  57.0 4.4 %collective-permute-start.5 = (bf16[4,128,512]{2,1,0:T(8,128)(2,1)S(1)}, bf16[4,128,512]{2,1,0:T(8,128)(2,1)}, u32[]{:S(2)}, u32[]{:S(2)}) collective-permute-start(bf16[4,128,512]{2,1,0:T(8,128)(2,1)S(1)} %collective-permute-done.4.got), channel_id=1, source_target_pairs={{0,2},{2,0},{4,6},{6,4},{8,10},{10,8},{12,14},{14,12},{16,18},{18,... | collective-permute-start | bytes 1572872 | tf_op jit(solution)/shard_map/ppermute | solution.py:62
  59.5 27.7 %collective-permute-start.6 = (bf16[128,8,256]{2,1,0:T(8,128)(2,1)S(1)}, bf16[128,8,256]{2,1,0:T(8,128)(2,1)}, u32[]{:S(2)}, u32[]{:S(2)}) collective-permute-start(bf16[128,8,256]{2,1,0:T(8,128)(2,1)S(1)} %all-to-all-done), channel_id=1, source_target_pairs={{0,2},{2,0},{4,6},{6,4},{8,10},{10,8},{12,14},{14,12},{16,18},{18,... | collective-permute-start | bytes 1572872 | tf_op jit(solution)/shard_map/ppermute | solution.py:62
  59.5 12.3 %collective-permute-start.2 = (bf16[32,512]{1,0:T(8,128)(2,1)S(1)}, bf16[32,512]{1,0:T(8,128)(2,1)S(1)}, u32[]{:S(2)}, u32[]{:S(2)}) collective-permute-start(bf16[32,512]{1,0:T(8,128)(2,1)S(1)} %pad_maximum_fusion.6), channel_id=1, source_target_pairs={{0,2},{2,4},{4,6},{6,8},{8,10},{10,12},{12,14},{14,16},{16,18},{18... | collective-permute-start | bytes 98312 | tf_op jit(solution)/shard_map/ppermute | solution.py:67
  61.4 17.5 %collective-permute-start.3 = (bf16[32,512]{1,0:T(8,128)(2,1)}, bf16[32,512]{1,0:T(8,128)(2,1)S(1)}, u32[]{:S(2)}, u32[]{:S(2)}) collective-permute-start(bf16[32,512]{1,0:T(8,128)(2,1)} %pad_maximum_fusion.7), channel_id=1, source_target_pairs={{0,254},{2,0},{4,2},{6,4},{8,6},{10,8},{12,10},{14,12},{16,14},{18... | collective-permute-start | bytes 98312 | tf_op jit(solution)/shard_map/ppermute | solution.py:67
  71.8 25.4 %collective-permute-start.11 = (bf16[768,256]{1,0:T(8,128)(2,1)S(1)}, bf16[768,256]{1,0:T(8,128)(2,1)S(1)}, u32[]{:S(2)}, u32[]{:S(2)}) collective-permute-start(bf16[768,256]{1,0:T(8,128)(2,1)S(1)} %copy-done.48), channel_id=1, source_target_pairs={{0,1},{1,0},{2,3},{3,2},{4,5},{5,4},{6,7},{7,6},{8,9},{9,8},{10,11... | collective-permute-start | bytes 1179656 | tf_op jit(solution)/shard_map/ppermute | solution.py:57
  73.0 20.7 %collective-permute-start.10 = (bf16[3,128,512]{2,1,0:T(8,128)(2,1)}, bf16[3,128,512]{2,1,0:T(8,128)(2,1)S(1)}, u32[]{:S(2)}, u32[]{:S(2)}) collective-permute-start(bf16[3,128,512]{2,1,0:T(8,128)(2,1)} %collective-permute-done.9.got), channel_id=1, source_target_pairs={{0,2},{2,0},{4,6},{6,4},{8,10},{10,8},{12,14},{14,12},{16,18},{18,... | collective-permute-start | bytes 1179656 | tf_op jit(solution)/shard_map/ppermute | solution.py:62
  92.2 6.5 %collective-permute-start.8 = (bf16[192,512]{1,0:T(8,128)(2,1)S(1)}, bf16[192,512]{1,0:T(8,128)(2,1)S(1)}, u32[]{:S(2)}, u32[]{:S(2)}) collective-permute-start(bf16[192,512]{1,0:T(8,128)(2,1)S(1)} %get-tuple-element.101), channel_id=1, source_target_pairs={{0,1},{1,0},{2,3},{3,2},{4,5},{5,4},{6,7},{7,6},{8,9},{9,8},{10,11... | collective-permute-start | bytes 589832 | tf_op jit(solution)/shard_map/ppermute | solution.py:57
  109.8 2.3 %collective-permute-start.19 = (bf16[3,256,256]{2,1,0:T(8,128)(2,1)S(1)}, bf16[3,256,256]{2,1,0:T(8,128)(2,1)S(1)}, u32[]{:S(2)}, u32[]{:S(2)}) collective-permute-start(bf16[3,256,256]{2,1,0:T(8,128)(2,1)S(1)} %get-tuple-element.127), channel_id=1, source_target_pairs={{0,2},{2,0},{4,6},{6,4},{8,10},{10,8},{12,14},{14,12},{16,18},{18,... | collective-permute-start | bytes 1179656 | tf_op jit(solution)/shard_map/ppermute | solution.py:62
  110.7 2.3 %collective-permute-start.20 = (bf16[512,512]{1,0:T(8,128)(2,1)}, bf16[512,512]{1,0:T(8,128)(2,1)S(1)}, u32[]{:S(2)}, u32[]{:S(2)}) collective-permute-start(bf16[512,512]{1,0:T(8,128)(2,1)} %get-tuple-element.129), channel_id=1, source_target_pairs={{0,2},{2,0},{4,6},{6,4},{8,10},{10,8},{12,14},{14,12},{16,18},{18,... | collective-permute-start | bytes 1572872 | tf_op jit(solution)/shard_map/ppermute | solution.py:62
  110.8 4.0 %collective-permute-start.16 = (bf16[2,4,256,256]{3,2,1,0:T(8,128)(2,1)}, bf16[2,4,256,256]{3,2,1,0:T(8,128)(2,1)S(1)}, u32[]{:S(2)}, u32[]{:S(2)}) collective-permute-start(bf16[2,4,256,256]{3,2,1,0:T(8,128)(2,1)} %get-tuple-element.125), channel_id=1, source_target_pairs={{0,2},{2,0},{4,6},{6,4},{8,10},{10,8},{12,14},{14,12},{16,18},{18,... | collective-permute-start | bytes 3145736 | tf_op jit(solution)/shard_map/ppermute | solution.py:62
  113.2 4.8 %collective-permute-start.21 = (bf16[256,256]{1,0:T(8,128)(2,1)S(1)}, bf16[256,256]{1,0:T(8,128)(2,1)S(1)}, u32[]{:S(2)}, u32[]{:S(2)}) collective-permute-start(bf16[256,256]{1,0:T(8,128)(2,1)S(1)} %get-tuple-element.147), channel_id=1, source_target_pairs={{0,1},{1,0},{2,3},{3,2},{4,5},{5,4},{6,7},{7,6},{8,9},{9,8},{10,11... | collective-permute-start | bytes 393224 | tf_op jit(solution)/shard_map/ppermute | solution.py:57
  114.8 5.6 %collective-permute-start.22 = (bf16[256,256]{1,0:T(8,128)(2,1)S(1)}, bf16[256,256]{1,0:T(8,128)(2,1)S(1)}, u32[]{:S(2)}, u32[]{:S(2)}) collective-permute-start(bf16[256,256]{1,0:T(8,128)(2,1)S(1)} %get-tuple-element.148), channel_id=1, source_target_pairs={{0,5},{1,4},{2,7},{3,6},{4,1},{5,0},{6,3},{7,2},{8,13},{9,12},{10,... | collective-permute-start | bytes 393224 | tf_op jit(solution)/shard_map/ppermute | solution.py:76
  115.2 8.5 %collective-permute-start.17 = (bf16[2,256,256]{2,1,0:T(8,128)(2,1)S(1)}, bf16[2,256,256]{2,1,0:T(8,128)(2,1)S(1)}, u32[]{:S(2)}, u32[]{:S(2)}) collective-permute-start(bf16[2,256,256]{2,1,0:T(8,128)(2,1)S(1)} %get-tuple-element.143), channel_id=1, source_target_pairs={{0,1},{1,0},{2,3},{3,2},{4,5},{5,4},{6,7},{7,6},{8,9},{9,8},{10,11... | collective-permute-start | bytes 786440 | tf_op jit(solution)/shard_map/ppermute | solution.py:57
  116.4 9.6 %collective-permute-start.18 = (bf16[2,256,256]{2,1,0:T(8,128)(2,1)S(1)}, bf16[2,256,256]{2,1,0:T(8,128)(2,1)S(1)}, u32[]{:S(2)}, u32[]{:S(2)}) collective-permute-start(bf16[2,256,256]{2,1,0:T(8,128)(2,1)S(1)} %get-tuple-element.144), channel_id=1, source_target_pairs={{0,5},{1,4},{2,7},{3,6},{4,1},{5,0},{6,3},{7,2},{8,13},{9,12},{10,... | collective-permute-start | bytes 786440 | tf_op jit(solution)/shard_map/ppermute | solution.py:76
  127.4 37.9 %all-to-all-start.1 = ((bf16[64,72,128]{2,1,0:T(8,128)(2,1)}), bf16[64,72,128]{2,1,0:T(8,128)(2,1)}, u32[]{:S(2)}, u32[]{:S(2)}) async-start(bf16[64,72,128]{2,1,0:T(8,128)(2,1)} %pad_maximum_fusion), calls=%async_computation.1 | async-start | bytes 2359296 | tf_op jit(solution)/shard_map/all_to_all | solution.py:82
  136.6 48.9 %collective-permute-start.7 = (bf16[768,256]{1,0:T(8,128)(2,1)}, bf16[768,256]{1,0:T(8,128)(2,1)}, u32[]{:S(2)}, u32[]{:S(2)}) collective-permute-start(bf16[768,256]{1,0:T(8,128)(2,1)} %pad_maximum_fusion.5), channel_id=1, source_target_pairs={{0,1},{1,0},{2,3},{3,2},{4,5},{5,4},{6,7},{7,6},{8,9},{9,8},{10,11... | collective-permute-start | bytes 1179656 | tf_op jit(solution)/shard_map/ppermute | solution.py:57
  141.7 34.0 %collective-permute-start.13 = (bf16[256,256]{1,0:T(8,128)(2,1)}, bf16[256,256]{1,0:T(8,128)(2,1)S(1)}, u32[]{:S(2)}, u32[]{:S(2)}) collective-permute-start(bf16[256,256]{1,0:T(8,128)(2,1)} %get-tuple-element.123), channel_id=1, source_target_pairs={{0,1},{1,0},{2,3},{3,2},{4,5},{5,4},{6,7},{7,6},{8,9},{9,8},{10,11... | collective-permute-start | bytes 393224 | tf_op jit(solution)/shard_map/ppermute | solution.py:57
  142.8 45.9 %collective-permute-start.12 = (bf16[768,256]{1,0:T(8,128)(2,1)}, bf16[768,256]{1,0:T(8,128)(2,1)S(1)}, u32[]{:S(2)}, u32[]{:S(2)}) collective-permute-start(bf16[768,256]{1,0:T(8,128)(2,1)} %get-tuple-element.120), channel_id=1, source_target_pairs={{0,1},{1,0},{2,3},{3,2},{4,5},{5,4},{6,7},{7,6},{8,9},{9,8},{10,11... | collective-permute-start | bytes 1179656 | tf_op jit(solution)/shard_map/ppermute | solution.py:57
  167.9 32.4 %all-to-all-start.2 = ((bf16[64,56,128]{2,1,0:T(8,128)(2,1)}), bf16[64,56,128]{2,1,0:T(8,128)(2,1)S(1)}, u32[]{:S(2)}, u32[]{:S(2)}) async-start(bf16[64,56,128]{2,1,0:T(8,128)(2,1)} %broadcast_in_dim.59), calls=%async_computation.2 | async-start | bytes 1835008 | tf_op jit(solution)/shard_map/all_to_all | solution.py:82
  175.8 9.7 %collective-permute-start.15 = (bf16[32,256]{1,0:T(8,128)(2,1)S(1)}, bf16[32,256]{1,0:T(8,128)(2,1)S(1)}, u32[]{:S(2)}, u32[]{:S(2)}) collective-permute-start(bf16[32,256]{1,0:T(8,128)(2,1)S(1)} %get-tuple-element.153), channel_id=1, source_target_pairs={{0,2},{2,4},{4,6},{6,8},{8,10},{10,12},{12,14},{14,16},{16,18},{18... | collective-permute-start | bytes 49160 | tf_op jit(solution)/shard_map/ppermute | solution.py:67
  180.4 5.0 %collective-permute-start.14 = (bf16[32,256]{1,0:T(8,128)(2,1)S(1)}, bf16[32,256]{1,0:T(8,128)(2,1)S(1)}, u32[]{:S(2)}, u32[]{:S(2)}) collective-permute-start(bf16[32,256]{1,0:T(8,128)(2,1)S(1)} %get-tuple-element.154), channel_id=1, source_target_pairs={{0,254},{2,0},{4,2},{6,4},{8,6},{10,8},{12,10},{14,12},{16,14},{18... | collective-permute-start | bytes 49160 | tf_op jit(solution)/shard_map/ppermute | solution.py:67
  200.3 6.0 %collective-permute-start.23 = (bf16[2,1792,128]{2,1,0:T(8,128)(2,1)S(1)}, bf16[2,1792,128]{2,1,0:T(8,128)(2,1)S(1)}, u32[]{:S(2)}, u32[]{:S(2)}) collective-permute-start(bf16[2,1792,128]{2,1,0:T(8,128)(2,1)S(1)} %bitcast.30), channel_id=1, source_target_pairs={{0,2},{2,0},{4,6},{6,4},{8,10},{10,8},{12,14},{14,12},{16,18},{18,... | collective-permute-start | bytes 2752520 | tf_op jit(solution)/shard_map/ppermute | solution.py:62
  (48 other events, 239.3 us)

commit v3 on v2

v3 whole, which is shorter than its diff:
```python
import functools

import jax
import jax.numpy as jnp
from jax import lax
from jax.experimental import pallas as pl
from jax.experimental.pallas import tpu as pltpu
from jax.sharding import PartitionSpec as P

HALO = 32
COARSE = 8
FINE = 1152
EPSILON = 1e-05
F32 = jnp.float32
BF16 = jnp.bfloat16
I32 = jnp.int32
LANES = 128
VMEM_LIMIT = 28 * 1024 * 1024


def dot(left, right):
    return jnp.dot(left, right, preferred_element_type=F32)


def contract_rows(left, right):
    return lax.dot_general(left, right, (((0,), (0,)), ((), ())), preferred_element_type=F32)


def contract_cols(left, right):
    return lax.dot_general(left, right, (((1,), (1,)), ((), ())), preferred_element_type=F32)


def layer_norm(values):
    centered = values - jnp.mean(values, axis=1, keepdims=True)
    inverse = lax.rsqrt(jnp.mean(centered * centered, axis=1, keepdims=True) + EPSILON)
    return centered * inverse, inverse


def norm_backward(cotangent, normed, inverse):
    mean = jnp.mean(cotangent, axis=1, keepdims=True)
    crossed = jnp.mean(cotangent * normed, axis=1, keepdims=True)
    return (cotangent - mean - normed * crossed) * inverse


def swish_parts(values):
    sigmoid = jax.nn.sigmoid(values)
    return values * sigmoid, sigmoid * (1.0 + values * (1.0 - sigmoid))


def one_hot(index, width):
    return (index == lax.broadcasted_iota(I32, (index.shape[0], width), 1)).astype(F32).astype(BF16)


def one_hot_t(index, width):
    return (index == lax.broadcasted_iota(I32, (width, index.shape[1]), 0)).astype(F32).astype(BF16)


def swap_lat(value):
    return lax.ppermute(value, "lat", [(0, 1), (1, 0)])


def swap_core(value):
    count = lax.axis_size("patch")
    return lax.ppermute(value, "patch", [(i, i ^ 1) for i in range(count)])


def shifted(value, steps):
    count = lax.axis_size("patch")
    return lax.ppermute(value, "patch", [(i, (i + steps) % count) for i in range(count)])


def other_neighbour(value):
    count = lax.axis_size("patch")
    pairs = []
    for patch in range(count):
        for lat in range(2):
            pairs.append((patch * 2 + lat, (patch ^ 2) * 2 + (1 - lat)))
    return lax.ppermute(value, ("patch", "lat"), pairs)


def chips_all_to_all(value):
    count = lax.axis_size("patch")
    groups = [list(range(core, count, 2)) for core in range(2)]
    return lax.all_to_all(value, "patch", 0, 0, tiled=True, axis_index_groups=groups)


def whole(shape):
    return pl.BlockSpec(shape, lambda i, s: (0,) * len(shape), pipeline_mode=pl.Buffered(1))


def block(shape, index):
    return pl.BlockSpec(shape, index, pipeline_mode=pl.Buffered(1))


def call(kernel, info, operands, in_specs, outs, scratch=(), flops=0, moved=0, name=None):
    return pl.pallas_call(
        kernel,
        grid_spec=pltpu.PrefetchScalarGridSpec(
            num_scalar_prefetch=1,
            grid=(1,),
            in_specs=in_specs,
            out_specs=[whole(shape) for shape, _ in outs],
            scratch_shapes=list(scratch),
        ),
        out_shape=[jax.ShapeDtypeStruct(shape, dtype) for shape, dtype in outs],
        compiler_params=pltpu.CompilerParams(vmem_limit_bytes=VMEM_LIMIT),
        cost_estimate=pl.CostEstimate(flops=flops, bytes_accessed=moved, transcendentals=0),
        name=name,
    )(info, *operands)


def pinned(value):
    return pltpu.with_memory_space_constraint(value, pltpu.HBM)


def pack_kernel(info, xf, xl, n, ng, wi, wo, xs, ns, wes):
    fine, nodes = xf.shape[0], n.shape[0]
    ns[:nodes] = n[...]
    ns[nodes:] = ng[...]
    wes[:3] = wi[...]
    wes[3] = wo[...]
    xs[:fine] = xf[...]
    xs[fine:] = xl[...]


def coarse_kernel(info, n_own, n_got, idx_f, idx_l, out):
    rows = jnp.concatenate([n_own[:COARSE], n_got[:COARSE]], 1)
    out[...] = jnp.broadcast_to(rows[None], out.shape)


def lat_stage_kernel(info, keep, got, first, second):
    rows = first.shape[0]
    first[...] = (keep[:rows].astype(F32) + got[:rows].astype(F32)).astype(BF16)
    second[...] = (keep[rows:].astype(F32) + got[rows:].astype(F32)).astype(BF16)


def combine_kernel(info, keep, got, first, second, out):
    chips = out.shape[0]
    rows = first.shape[0]
    edge_rows_count, far_rows = 2 * rows - chips * COARSE, chips * COARSE
    half_chips = chips // 2
    total = keep[...].astype(F32) + got[...].astype(F32)
    pair = jnp.concatenate([first[...], second[...]], 0).astype(F32)
    weights = jnp.concatenate(
        [total[:edge_rows_count] + pair[:edge_rows_count], total[edge_rows_count:-far_rows]], 0
    )
    far = total[-far_rows:] + pair[edge_rows_count:]
    share = weights.shape[0] // half_chips
    parts = [weights[:, i * LANES : (i + 1) * LANES].reshape(half_chips, share, LANES) for i in range(2)]
    coarse = [far[:, i * LANES : (i + 1) * LANES].reshape(chips, COARSE, LANES) for i in range(2)]
    out[...] = jnp.concatenate([jnp.concatenate(parts, 0)] + coarse, 1).astype(BF16)


def share_kernel(info, arrived, output, grads, low, high, weights, coarse, *, scale):
    share = weights.shape[1]
    total = jnp.sum(arrived[...].astype(F32), 0)
    weights[...] = jnp.broadcast_to((total[:share] * scale).astype(BF16)[None], weights.shape)
    coarse[...] = total[share:]


def rows_kernel(info, own_f, own_l, got, out):
    lat = info[0]
    fine, longs = own_f.shape[0], own_l.shape[0]
    for side, f, l in ((lat, own_f[...], own_l[...]), (1 - lat, got[:fine], got[fine:])):
        out[pl.ds(pl.multiple_of(side * fine, 64), fine)] = f
        out[pl.ds(pl.multiple_of(FINE + side * longs, 64), longs)] = l


def results_kernel(info, mine, other, inner, outer, node_inner, node_outer, staged, sems):
    first = info[1] == 0
    blocks, half = mine.shape[0], staged.shape[1]
    targets = [inner.at[0], inner.at[1], inner.at[2], outer, node_inner.at[0], node_inner.at[1], node_outer]
    copies = []
    for k, target in enumerate(targets):
        rows = slice(k * half, (k + 1) * half)
        for i in range(blocks):
            a, b = mine[i, rows].astype(F32), other[i, rows].astype(F32)
            staged[k, :, i * LANES : (i + 1) * LANES] = jnp.where(first, a, b)
            staged[k, :, half + i * LANES : half + (i + 1) * LANES] = jnp.where(first, b, a)
        copies.append(pltpu.make_async_copy(staged.at[k], target, sems.at[k]))
        copies[-1].start()
    for copy in copies:
        copy.wait()


def edge_weights_kernel(info, wi, wo, got, again, gf, gl, ni, no, after, full_in, full_out, gs, wns):
    fine = gf.shape[0]
    wns[:2] = ni[...]
    wns[2] = no[...]
    gs[:fine] = gf[...]
    gs[fine:] = gl[...]
    weights_kernel(info, wi, wo, got, again, full_in, full_out)


def weights_kernel(info, wi, wo, got, again, full_in, full_out):
    lat, core = info[0], info[1]
    half = wo.shape[0]
    quarter = half // 2
    inner = wi.shape[0]
    first = core == 0
    for k in range(inner):
        full_in[k, :half] = wi[k]
        full_in[k, half : half + quarter] = jnp.where(first, got[k], again[k])
        full_in[k, half + quarter :] = jnp.where(first, again[k], got[k])
    own = wo[...]
    top = jnp.where(first, got[inner], again[inner])
    bottom = jnp.where(first, again[inner], got[inner])
    missing = jnp.concatenate([top, bottom], 0)
    low = lat == 0
    for rows, value in ((slice(0, half), jnp.where(low, own, missing)), (slice(half, 2 * half), jnp.where(low, missing, own))):
        full_out[rows, :half] = jnp.where(low, value[:, :half], value[:, half:])
        full_out[rows, half:] = jnp.where(low, value[:, half:], value[:, :half])


def edge_rows(x, sender, receiver, mask, w_in, w_out, rows, half, slope, act, normed, inverse, out_own, out_sent, update):
    pre = dot(x, w_in[0]) + dot(sender, w_in[1]) + dot(receiver, w_in[2])
    value, derivative = swish_parts(pre)
    value = value.astype(BF16)
    slope[rows] = derivative
    act[rows] = value
    scaled, scale = layer_norm(dot(value, w_out[...]))
    normed[rows] = scaled
    inverse[rows] = scale
    change = scaled if mask is None else scaled * mask
    out = (x.astype(F32) + change).astype(BF16)
    out_own[rows] = out[:, :half]
    out_sent[rows] = out[:, half:]
    update[rows] = change.astype(BF16)


def fine_kernel(info, x_own, x_got, n_own, n_got, low, high, idx_c, idx_r, w_in, w_out,
                slope, act, normed, inverse, out_own, out_sent, partial, sent, ext, update):
    half = x_own.shape[1]
    nodes = n_own.shape[0]
    ext[:HALO] = low[...]
    ext[HALO : HALO + nodes, :half] = n_own[...]
    ext[HALO : HALO + nodes, half:] = n_got[...]
    ext[HALO + nodes :] = high[...]
    node_x = ext[HALO : HALO + nodes]
    chunk = 192
    for start in range(0, x_own.shape[0], chunk):
        rows = pl.ds(start, chunk)
        x = jnp.concatenate([x_own[rows], x_got[rows]], 1)
        sender = dot(one_hot(idx_c[rows, 0:1], ext.shape[0]), ext[...]).astype(BF16)
        receiver = dot(one_hot(idx_c[rows, 1:2], nodes), node_x).astype(BF16)
        edge_rows(x, sender, receiver, None, w_in, w_out, rows, half, slope, act, normed, inverse, out_own, out_sent, update)
    total = dot(one_hot_t(idx_r[1:2], nodes), update[...])
    partial[...] = total
    sent[...] = total.astype(BF16)


def long_kernel(info, x_own, x_got, n_own, n_got, same, other, idx_c, idx_r, w_in, w_out,
                slope, act, normed, inverse, out_own, out_sent, partial, sent, sender_rows, update):
    half = x_own.shape[1]
    rows = pl.ds(0, x_own.shape[0])
    count = same.shape[0]
    value = dot(one_hot(idx_c[:, 0:1], count), same[...])
    value = value + dot(one_hot(idx_c[:, 0:1] - count, count), other[...])
    sender_rows[...] = value.astype(BF16)
    x = jnp.concatenate([x_own[...], x_got[...]], 1)
    near = n_own.shape[0]
    node_x = jnp.concatenate([n_own[...], n_got[...]], 1)
    receiver = dot(one_hot(idx_c[:, 1:2], near), node_x).astype(BF16)
    edge_rows(x, sender_rows[...], receiver, idx_c[:, 2:3].astype(F32), w_in, w_out, rows, half, slope, act, normed, inverse, out_own, out_sent, update)
    total = dot(one_hot_t(idx_r[1:2], near), update[...])
    partial[...] = total
    sent[...] = total.astype(BF16)


def back_kernel(info, partial, got, partial_l, got_l, n_own, n_got, ng_own, ng_got, low, high, nin, nout,
                xf_own, xl_own, xf_got, xl_got, gf_own, gl_own, gf_got, gl_got,
                slope_f, slope_l, act_f, act_l, normed_f, normed_l, inverse_f, inverse_l, srow_l,
                idx_cf, idx_cl, idx_rf, idx_rl, w_in, w_out,
                node_out, node_self, keep_own, send_own, keep_pair, send_pair, dpre, near_sum, recv_sum,
                ndpre, ndy, nact, agg_grad, dy, ext):
    lat, core = info[0], info[1]
    half = n_own.shape[1]
    nodes = n_own.shape[0]
    fine, longs = xf_own.shape[0], xl_own.shape[0]
    mine = pl.ds(pl.multiple_of(core * half, half), half)
    theirs = pl.ds(pl.multiple_of((1 - core) * half, half), half)
    turn = (core + lat) % 2
    mine_own = pl.ds(pl.multiple_of(turn * half, half), half)
    theirs_own = pl.ds(pl.multiple_of((1 - turn) * half, half), half)
    hidden_mine = pl.ds(pl.multiple_of(lat * half, half), half)
    hidden_theirs = pl.ds(pl.multiple_of((1 - lat) * half, half), half)

    ext[:HALO] = low[...]
    ext[HALO : HALO + nodes, :half] = n_own[...]
    ext[HALO : HALO + nodes, half:] = n_got[...]
    ext[HALO + nodes :] = high[...]
    node_x = ext[HALO : HALO + nodes]
    received, received_l = got[...].astype(F32), got_l[...].astype(F32)
    total = partial[...] + jnp.concatenate([received[:, half:], received[:, :half]], 1)
    coarse = partial_l[...] + jnp.concatenate([received_l[:, half:], received_l[:, :half]], 1)
    near = coarse.shape[0]
    agg = jnp.concatenate([total[:near] + coarse, total[near:]], 0).astype(BF16)
    node_value, node_slope = swish_parts(dot(node_x, nin[0]) + dot(agg, nin[1]))
    nact[...] = node_value.astype(BF16)
    node_normed, node_inverse = layer_norm(dot(nact[...], nout[...]))
    node_out[...] = (n_own[...].astype(F32) + node_normed[:, :half]).astype(BF16)
    node_g = jnp.concatenate([ng_own[...], ng_got[...]], 1).astype(F32)
    ndy[...] = norm_backward(node_g, node_normed, node_inverse).astype(BF16)
    ndpre[...] = (contract_cols(ndy[...], nout[...]) * node_slope).astype(BF16)
    agg_grad[...] = contract_cols(ndpre[...], nin[1]).astype(BF16)
    node_self[...] = ng_own[...].astype(F32) + contract_cols(ndpre[...], nin[0, :half])

    chunk = 192
    for start in range(0, fine + longs, chunk):
        rows = pl.ds(start, chunk)
        if start < fine:
            part = pl.ds(start, chunk)
            idx_c = idx_cf
            g_own, g_got, normed, inverse, slope = gf_own, gf_got, normed_f, inverse_f, slope_f
        else:
            part = pl.ds(start - fine, chunk)
            idx_c = idx_cl
            g_own, g_got, normed, inverse, slope = gl_own, gl_got, normed_l, inverse_l, slope_l
        cotangent = jnp.concatenate([g_own[part], g_got[part]], 1).astype(F32)
        cotangent = cotangent + dot(one_hot(idx_c[part, 1:2], nodes), agg_grad[...])
        if start >= fine:
            cotangent = cotangent * idx_cl[part, 2:3].astype(F32)
        dy[rows] = norm_backward(cotangent, normed[part], inverse[part]).astype(BF16)
        dpre[rows] = (contract_cols(dy[rows], w_out[...]) * slope[part]).astype(BF16)

    tail = pl.ds(fine, longs)
    head = pl.ds(0, fine)
    srow_grads = contract_cols(dpre[tail], w_in[1]).astype(BF16)
    rows_pair, rows_own = keep_pair.shape[0], keep_own.shape[0]
    edge_count, far_count = 4 * half, keep_pair.shape[0] - 4 * half
    far = dot(one_hot_t(idx_rl[0:1], 2 * far_count), srow_grads).astype(BF16)
    for value, own, pair in (
        (far[:far_count], keep_own, keep_pair),
        (far[far_count:], send_own, send_pair),
    ):
        own[rows_own - far_count :] = value[:, :half]
        pair[rows_pair - far_count :] = value[:, half:]
    near_sum[...] = dot(one_hot_t(idx_rf[0:1], ext.shape[0]), dpre[head]).astype(BF16)
    recv_sum[...] = (
        dot(one_hot_t(idx_rf[1:2], nodes), dpre[head]) + dot(one_hot_t(idx_rl[1:2], nodes), dpre[tail])
    ).astype(BF16)
    for own, pair, columns, columns_own in (
        (send_own, send_pair, theirs, theirs_own),
        (keep_own, keep_pair, mine, mine_own),
    ):
        for out, xf, xl, hidden, cols in (
            (pair, xf_got, xl_got, hidden_theirs, slice(half, 2 * half)),
            (own, xf_own, xl_own, hidden_mine, slice(0, half)),
        ):
            grad = contract_rows(xf[...], dpre[head, columns]) + contract_rows(xl[...], dpre[tail, columns])
            out[:half] = grad.astype(BF16)
            grad = contract_rows(ext[:, cols], near_sum[:, columns]) + contract_rows(srow_l[:, cols], dpre[tail, columns])
            out[half : 2 * half] = grad.astype(BF16)
            grad = contract_rows(ext[HALO : HALO + nodes, cols], recv_sum[:, columns])
            out[2 * half : 3 * half] = grad.astype(BF16)
            grad = contract_rows(act_f[:, hidden], dy[head, columns_own]) + contract_rows(act_l[:, hidden], dy[tail, columns_own])
            out[3 * half : 4 * half] = grad.astype(BF16)
        own[4 * half : 5 * half] = contract_rows(n_own[...], ndpre[:, columns]).astype(BF16)
        own[5 * half : 6 * half] = contract_rows(agg[:, :half], ndpre[:, columns]).astype(BF16)
        own[6 * half : 7 * half] = contract_rows(nact[:, hidden_mine], ndy[:, columns_own]).astype(BF16)


def inputs_kernel(info, dpre, gf_own, gl_own, g_got, near_sum, recv_sum, w_in,
                  grads_own, grads_sent, rim_own, rim_sent):
    half = g_got.shape[1]
    fine, longs = gf_own.shape[0], gl_own.shape[0]
    nodes = recv_sum.shape[0]
    for start, rows, own in ((0, fine, gf_own), (fine, longs, gl_own)):
        part = pl.ds(start, rows)
        change = contract_cols(dpre[part], w_in[0])
        grads_own[part] = (own[...].astype(F32) + change[:, :half]).astype(BF16)
        grads_sent[part] = (g_got[part].astype(F32) + change[:, half:]).astype(BF16)
    near = contract_cols(near_sum[...], w_in[1])
    received = contract_cols(recv_sum[...], w_in[2])
    for rows, value in (
        (slice(0, HALO), near[:HALO]),
        (slice(HALO, HALO + nodes), near[HALO : HALO + nodes] + received),
        (slice(HALO + nodes, 2 * HALO + nodes), near[HALO + nodes :]),
    ):
        rim_own[rows] = value[:, :half]
        rim_sent[rows] = value[:, half:].astype(BF16)


def body(
    node_latents,
    edge_latents,
    senders,
    receivers,
    long_count,
    edge_inner,
    edge_outer,
    node_inner,
    node_outer,
    node_cotangent,
    edge_cotangent,
):
    nodes, half = node_latents.shape
    full = 2 * half
    edges = edge_latents.shape[0]
    rows = edges // 2
    fine, longs = FINE // 2, (edges - FINE) // 2
    quarter = half // 2
    patches = lax.axis_size("patch")
    chips = patches // 2
    extent = nodes + 2 * HALO
    lat = lax.axis_index("lat")
    patch = lax.axis_index("patch")
    core = patch % 2
    first_node = patch * nodes
    info = jnp.stack([lat, core]).astype(I32)

    x_hbm, g_hbm = pinned(edge_latents), pinned(edge_cotangent)
    n_hbm, ng_hbm = pinned(node_latents), pinned(node_cotangent)
    wi_hbm, wo_hbm = pinned(edge_inner), pinned(edge_outer)
    ni_hbm, no_hbm = pinned(node_inner), pinned(node_outer)

    def rows_of(value):
        return (
            lax.dynamic_slice_in_dim(value, lat * fine, fine, 0),
            lax.dynamic_slice_in_dim(value, FINE + lat * longs, longs, 0),
        )

    near_ids, far_ids = rows_of(senders.reshape(edges))
    recv_f, recv_l = rows_of(receivers.reshape(edges))
    near = (near_ids - first_node + HALO) % (nodes * patches)
    far_patch, far_row = far_ids // nodes, far_ids % nodes
    is_same = far_patch % 2 == core
    far_slot = jnp.where(is_same, 0, chips * COARSE) + far_patch // 2 * COARSE + far_row
    live = (jnp.arange(longs, dtype=I32) + lat * longs < long_count[0]).astype(I32)
    idx_rf = jnp.stack([near, recv_f - first_node])
    idx_rl = jnp.stack([far_slot, recv_l - first_node, live])
    idx_cf, idx_cl = idx_rf.T, idx_rl.T

    fine_other = block((fine, half), lambda i, s: (1 - s[0], 0))
    long_other = block((longs, half), lambda i, s: (FINE // longs + 1 - s[0], 0))
    quarter_rows = block((quarter, full), lambda i, s: (s[1], 0))
    sent_x, sent_n, sent_we = call(
        pack_kernel,
        info,
        (x_hbm, x_hbm, n_hbm, ng_hbm, wi_hbm, wo_hbm),
        [
            fine_other, long_other, whole((nodes, half)), whole((nodes, half)),
            block((3, quarter, full), lambda i, s: (0, s[1], 0)), quarter_rows,
        ],
        [((rows, half), BF16), ((2 * nodes, half), BF16), ((4, quarter, full), BF16)],
        moved=3_000_000,
        name="pack",
    )
    node_got = swap_lat(sent_n)
    we_got = other_neighbour(sent_we)
    x_got = swap_lat(sent_x)
    (sent_coarse,) = call(
        coarse_kernel,
        info,
        (n_hbm, node_got, idx_cf, idx_cl),
        [whole((16, half)), whole((16, half)), whole((fine, 2)), whole((longs, 3))],
        [((chips, COARSE, full), BF16)],
        moved=600_000,
        name="coarse_rows",
    )
    far_rows = chips * COARSE
    same = chips_all_to_all(sent_coarse)
    other = swap_core(same).reshape(far_rows, full)
    same = same.reshape(far_rows, full)
    low = shifted(
        jnp.concatenate([node_latents[nodes - HALO :], node_got[nodes - HALO : nodes]], 1), 1
    )
    high = shifted(jnp.concatenate([node_latents[:HALO], node_got[:HALO]], 1), -1)
    we_again = swap_core(we_got)

    got_spec = [whole((4, quarter, full))] * 2
    w_in, w_out, sent_g, sent_wn = call(
        edge_weights_kernel,
        info,
        (wi_hbm, wo_hbm, we_got, we_again, g_hbm, g_hbm, ni_hbm, no_hbm, x_got),
        [whole((3, half, full)), whole((half, full))] + got_spec + [
            fine_other, long_other, block((2, quarter, full), lambda i, s: (0, s[1], 0)), quarter_rows,
            pl.BlockSpec(memory_space=pl.ANY),
        ],
        [((3, full, full), BF16), ((full, full), BF16), ((rows, half), BF16), ((3, quarter, full), BF16)],
        moved=7_000_000,
        name="edge_weights",
    )
    wn_got = other_neighbour(sent_wn)
    wn_again = swap_core(wn_got)
    g_got = swap_lat(sent_g)
    nin, nout = call(
        weights_kernel,
        info,
        (ni_hbm, no_hbm, wn_got, wn_again),
        [whole((2, half, full)), whole((half, full)), whole((3, quarter, full)), whole((3, quarter, full))],
        [((2, full, full), BF16), ((full, full), BF16)],
        moved=3_000_000,
        name="node_weights",
    )

    def fine_own():
        return block((fine, half), lambda i, s: (s[0], 0))

    def long_own():
        return block((longs, half), lambda i, s: (FINE // longs + s[0], 0))

    def fine_got():
        return whole((fine, half))

    def long_got():
        return block((longs, half), lambda i, s: (fine // longs, 0))

    node_spec = whole((nodes, half))
    second_nodes = block((nodes, half), lambda i, s: (1, 0))
    rim = whole((HALO, full))
    win_spec, wout_spec = whole((3, full, full)), whole((full, full))

    def forward_outs(count, reach):
        return [
            ((count, full), F32),
            ((count, full), BF16),
            ((count, full), F32),
            ((count, 1), F32),
            ((count, half), BF16),
            ((count, half), BF16),
            ((reach, full), F32),
            ((reach, full), BF16),
        ]

    slope_f, act_f, normed_f, inverse_f, fine_out, fine_sent, partial_f, partial_f_sent = call(
        fine_kernel,
        info,
        (x_hbm, x_got, n_hbm, node_got, low, high, idx_cf, idx_rf, w_in, w_out),
        [
            fine_own(), fine_got(), node_spec, whole((nodes, half)), rim, rim,
            whole((fine, 2)), whole((2, fine)), win_spec, wout_spec,
        ],
        forward_outs(fine, nodes),
        [pltpu.VMEM((extent, full), BF16), pltpu.VMEM((fine, full), BF16)],
        flops=2 * fine * full * (4 * full + extent + 2 * nodes),
        moved=8_000_000,
        name="edges_forward_fine",
    )
    slope_l, act_l, normed_l, inverse_l, long_out, long_sent, partial_l, partial_l_sent, srow_l = call(
        long_kernel,
        info,
        (x_hbm, x_got, n_hbm, node_got, pinned(same), pinned(other), idx_cl, idx_rl, w_in, w_out),
        [
            long_own(), long_got(), whole((16, half)), whole((16, half)),
            whole((far_rows, full)), whole((far_rows, full)),
            whole((longs, 3)), whole((3, longs)), win_spec, wout_spec,
        ],
        forward_outs(longs, 16) + [((longs, full), BF16)],
        [pltpu.VMEM((longs, full), BF16)],
        flops=2 * longs * full * (4 * full + 4 * patches * COARSE + 2 * nodes),
        moved=6_000_000,
        name="edges_forward_long",
    )
    partial_f_got = swap_lat(partial_f_sent)
    partial_l_got = swap_lat(partial_l_sent)

    edge_out_got = swap_lat(jnp.concatenate([fine_sent, long_sent], 0))
    rows_pair, rows_own = 4 * half + far_rows, 7 * half + far_rows

    (node_output, node_self, keep_own, send_own, keep_pair, send_pair, dpre, near_sum, recv_sum) = call(
        back_kernel,
        info,
        (partial_f, partial_f_got, partial_l, partial_l_got, n_hbm, node_got, ng_hbm, node_got, low, high, nin, nout,
         x_hbm, x_hbm, x_got, x_got, g_hbm, g_hbm, g_got, g_got,
         slope_f, slope_l, act_f, act_l, normed_f, normed_l, inverse_f, inverse_l, srow_l,
         idx_cf, idx_cl, idx_rf, idx_rl, w_in, w_out),
        [
            whole((nodes, full)), whole((nodes, full)), whole((16, full)), whole((16, full)),
            node_spec, whole((nodes, half)), node_spec, second_nodes,
            rim, rim, whole((2, full, full)), wout_spec,
            fine_own(), long_own(), fine_got(), long_got(), fine_own(), long_own(), fine_got(), long_got(),
            whole((fine, full)), whole((longs, full)), whole((fine, full)), whole((longs, full)),
            whole((fine, full)), whole((longs, full)), whole((fine, 1)), whole((longs, 1)),
            whole((longs, full)),
            whole((fine, 2)), whole((longs, 3)), whole((2, fine)), whole((3, longs)), win_spec, wout_spec,
        ],
        [
            ((nodes, half), BF16),
            ((nodes, half), F32),
            ((rows_own, half), BF16),
            ((rows_own, half), BF16),
            ((rows_pair, half), BF16),
            ((rows_pair, half), BF16),
            ((rows, full), BF16),
            ((extent, full), BF16),
            ((nodes, full), BF16),
        ],
        [
            pltpu.VMEM((nodes, full), BF16),
            pltpu.VMEM((nodes, full), BF16),
            pltpu.VMEM((nodes, full), BF16),
            pltpu.VMEM((nodes, full), BF16),
            pltpu.VMEM((rows, full), BF16),
            pltpu.VMEM((extent, full), BF16),
        ],
        flops=8 * rows * full * full,
        moved=14_000_000,
        name="nodes_and_edges_backward",
    )

    core_pair, core_own = swap_core(send_pair), swap_core(send_own)
    by_lat, by_other = call(
        lat_stage_kernel,
        info,
        (keep_pair, core_pair),
        [whole((rows_pair, half)), whole((rows_pair, half))],
        [((rows_pair // 2, half), BF16), ((rows_pair // 2, half), BF16)],
        moved=2_400_000,
        name="lat_stage",
    )
    blocks = half // LANES
    total_rows = 7 * half * blocks
    share = total_rows // chips
    slot = share + blocks * COARSE
    (gathered,) = call(
        combine_kernel,
        info,
        (keep_own, core_own, swap_lat(by_lat), other_neighbour(by_other)),
        [whole((rows_own, half)), whole((rows_own, half)), whole((rows_pair // 2, half)), whole((rows_pair // 2, half))],
        [((chips, slot, LANES), BF16)],
        moved=4_300_000,
        name="combine",
    )
    arrived = chips_all_to_all(gathered)

    grads_own, grads_sent, rim_own, rim_sent = call(
        inputs_kernel,
        info,
        (dpre, g_hbm, g_hbm, g_got, near_sum, recv_sum, w_in),
        [
            whole((rows, full)), fine_own(), long_own(), whole((rows, half)),
            whole((extent, full)), whole((nodes, full)), win_spec,
        ],
        [((rows, half), BF16), ((rows, half), BF16), ((extent, half), F32), ((extent, half), BF16)],
        flops=4 * rows * full * full,
        moved=5_000_000,
        name="input_gradients",
    )

    (edge_output,) = call(
        rows_kernel,
        info,
        (fine_out, long_out, edge_out_got),
        [whole((fine, half)), whole((longs, half)), whole((rows, half))],
        [((edges, half), BF16)],
        moved=1_600_000,
        name="edge_output_rows",
    )
    (edge_grads,) = call(
        rows_kernel,
        info,
        (grads_own, grads_own, swap_lat(grads_sent)),
        [whole((fine, half)), block((longs, half), lambda i, s: (fine // longs, 0)), whole((rows, half))],
        [((edges, half), BF16)],
        moved=1_600_000,
        name="edge_gradient_rows",
    )
    summed = rim_own + swap_lat(rim_sent).astype(F32)
    to_low = shifted(summed[:HALO].astype(BF16), -1).astype(F32)
    to_high = shifted(summed[HALO + nodes :].astype(BF16), 1).astype(F32)

    weight_share, coarse_total = call(
        functools.partial(share_kernel, scale=1.0 / patches),
        info,
        (arrived, edge_output, edge_grads, to_low, to_high),
        [whole((chips, slot, LANES))] + [pl.BlockSpec(memory_space=pl.ANY)] * 4,
        [((chips, share, LANES), BF16), ((blocks * COARSE, LANES), F32)],
        moved=2_200_000,
        name="share",
    )
    coarse_share = jnp.concatenate(
        [coarse_total[i * COARSE : (i + 1) * COARSE] for i in range(blocks)], 1
    )
    own_grads = node_self + summed[HALO : HALO + nodes]
    own_grads = own_grads.at[nodes - HALO :].add(to_low)
    own_grads = own_grads.at[:HALO].add(to_high)
    own_grads = own_grads.at[:COARSE].add(coarse_share)
    node_grads = own_grads.astype(BF16)
    mine = chips_all_to_all(weight_share)
    mine = mine.reshape(blocks, total_rows // blocks, LANES)
    other = swap_core(mine)
    square = (half, full)
    weights = pl.pallas_call(
        results_kernel,
        grid_spec=pltpu.PrefetchScalarGridSpec(
            num_scalar_prefetch=1,
            grid=(1,),
            in_specs=[whole(mine.shape)] * 2,
            out_specs=[pl.BlockSpec(memory_space=pl.ANY)] * 4,
            scratch_shapes=[pltpu.VMEM((7,) + square, F32), pltpu.SemaphoreType.DMA((7,))],
        ),
        out_shape=[jax.ShapeDtypeStruct(shape, F32) for shape in ((3,) + square, square, (2,) + square, square)],
        compiler_params=pltpu.CompilerParams(vmem_limit_bytes=VMEM_LIMIT),
        cost_estimate=pl.CostEstimate(flops=0, bytes_accessed=6_000_000, transcendentals=0),
        name="results",
    )(info, mine, other)
    return (edge_output, node_output, edge_grads, node_grads, *weights)


def solution(mesh):
    placed = (
        P("patch", "lat"),
        P("patch", "lat"),
        P("patch", None),
        P("patch", None),
        P("patch"),
        P(None, "lat", None),
        P("lat", None),
        P(None, "lat", None),
        P("lat", None),
        P("patch", "lat"),
        P("patch", "lat"),
    )
    return jax.shard_map(
        body,
        mesh=mesh,
        in_specs=placed,
        out_specs=(
            P("patch", "lat"),
            P("patch", "lat"),
            P("patch", "lat"),
            P("patch", "lat"),
            P(None, "lat", None),
            P("lat", None),
            P(None, "lat", None),
            P("lat", None),
        ),
        check_vma=False,
    )
```

time: 210 us -> 204 us (0.971)
  blocking collectives: 0 us -> 35.9 us
  local copies, waits for them, and re-layouts: 30.5 us -> 9.25 us
  other arithmetic: 11 us -> 1.08 us
  waiting for transfers between devices: 71.9 us -> 63.5 us
  starting transfers between devices: 63.5 us -> 56.4 us
  Pallas kernels: 30.1 us -> 35.4 us
    all_to_all x0 -> x1, blocking collectives: none -> 35.9 us  [chips_all_to_all(): lax.all_to_all(value, 'patch', 0, 0, tiled=True, axis_index_groups=groups)]
    all_to_all x2, waiting for transfers between devices: 33.8 us -> 0.01 us  [chips_all_to_all(): lax.all_to_all(value, 'patch', 0, 0, tiled=True, axis_index_groups=groups)]
    ppermute x9, waiting for transfers between devices: 4.58 us -> 27 us  [swap_lat(): return lax.ppermute(value, 'lat', [(0, 1), (1, 0)])]
    ppermute x4, waiting for transfers between devices: 5 us -> 25.5 us  [shifted(): lax.ppermute(value, 'patch', [(i, (i + steps) % count) for i in range(cou...]
    ppermute x4 -> x3, waiting for transfers between devices: 26.6 us -> 7.67 us  [other_neighbour(): return lax.ppermute(value, ('patch', 'lat'), pairs)]
    all_to_all x1 -> x0, starting transfers between devices: 16.5 us -> none  [pairs_all_to_all(): lax.all_to_all(value, ('patch', 'lat'), 0, 0, tiled=True, axis_index_grou...]
    unnamed x106 -> x46, local copies, waits for them, and re-layouts: 20.9 us -> 8.22 us
    all_to_all x2, starting transfers between devices: 15.1 us -> 24.3 us  [chips_all_to_all(): lax.all_to_all(value, 'patch', 0, 0, tiled=True, axis_index_groups=groups)]
  transfers between devices with their start and end apart: 27 -> 24, of which waited for: 11 -> 10; matrix products, arithmetic and copies ran while one was open for 9% -> 1% of each run, Pallas kernels for 7% -> 10%
where the time goes in v3:
time: 204 us; the launch traced here: 203 us
  waiting for transfers between devices  63.5 us (31%)
  starting transfers between devices  56.4 us (28%)
  blocking collectives  35.9 us (18%)
  Pallas kernels  35.4 us (17%)
  local copies, waits for them, and re-layouts  9.25 us (5%)
    all_to_all x1, blocking collectives, chips_all_to_all(): lax.all_to_all(value, 'patch', 0, 0, tiled=True, axis_index_groups=groups)  35.9 us
    pallas_call x13, Pallas kernels, call(): pl.pallas_call(kernel, grid_spec=pltpu.PrefetchScalarGridSpec(num_scalar_...  32.9 us
    ppermute x9, waiting for transfers between devices, swap_lat(): return lax.ppermute(value, 'lat', [(0, 1), (1, 0)])  27 us
    ppermute x4, waiting for transfers between devices, shifted(): lax.ppermute(value, 'patch', [(i, (i + steps) % count) for i in range(cou...  25.5 us
    all_to_all x2, starting transfers between devices, chips_all_to_all(): lax.all_to_all(value, 'patch', 0, 0, tiled=True, axis_index_groups=groups)  24.3 us
    ppermute x6, starting transfers between devices, swap_core(): return lax.ppermute(value, 'patch', [(i, i ^ 1) for i in range(count)])  11.1 us
    ppermute x4, starting transfers between devices, shifted(): lax.ppermute(value, 'patch', [(i, (i + steps) % count) for i in range(cou...  8.56 us
    unnamed x46, local copies, waits for them, and re-layouts  8.22 us
  transfers between devices with their start and end apart: 24, of which 10 were waited for; matrix products, arithmetic and copies ran while one was open for 1% of the time, Pallas kernels for 10%

profile of v3, /device:TPU:1, one launch (start us, length us, event | category | flops | bytes accessed | tf_op | source)
XLA Modules:
  0.0 203.4 jit_solution(7102881790793713981)
XLA Ops:
  0.7 1.9 pack.1
  2.6 2.1 %collective-permute-start.1 = (bf16[384,256]{1,0:T(8,128)(2,1)S(1)}, bf16[384,256]{1,0:T(8,128)(2,1)S(1)}, u32[]{:S(2)}, u32[]{:S(2)}) collective-permute-start(bf16[384,256]{1,0:T(8,128)(2,1)S(1)} %get-tuple-element.92), channel_id=1, source_target_pairs={{0,1},{1,0},{2,3},{3,2},{4,5},{5,4},{6,7},{7,6},{8,9},{9,8},{10,11... | collective-permute-start | bytes 589832 | tf_op jit(solution)/shard_map/ppermute | solution.py:59
  4.7 1.8 collective-permute-start.4
  8.0 2.1 %coarse_rows.1 = bf16[64,8,512]{2,1,0:T(8,128)(2,1)} custom-call(s32[2]{0:T(128)S(1)} %pad_add_fusion.2.info, bf16[192,256]{1,0:T(8,128)(2,1)} %n_own.7, bf16[384,256]{1,0:T(8,128)(2,1)S(1)} %collective-permute-done.1.n_got.ng_got, s32[576,2]{1,0:T(8,128)S(1)} %copy.19.idx_c.idx_f.idx_cf, s32[192,3]{1,0:T(8,128)S(1)} %copy.21.idx_l.idx_c.idx_cl), custom_call_target="tpu_custom_call" | custom-call | bytes 600000 | tf_op jit(solution)/shard_map/coarse_rows/pallas_call | solution.py:96
  10.1 15.8 %all-to-all-start = ((bf16[64,8,512]{2,1,0:T(8,128)(2,1)}), bf16[64,8,512]{2,1,0:T(8,128)(2,1)}, u32[]{:S(2)}, u32[]{:S(2)}) async-start(bf16[64,8,512]{2,1,0:T(8,128)(2,1)} %coarse_rows.1), calls=%async_computation | async-start | bytes 1048576 | tf_op jit(solution)/shard_map/all_to_all | solution.py:84
  25.9 1.9 collective-permute-start.5
  28.2 14.7 %collective-permute-done.after.x_got.xf_got.xl_got = bf16[768,256]{1,0:T(8,128)(2,1)S(1)} collective-permute-done((bf16[768,256]{1,0:T(8,128)(2,1)S(1)}, bf16[768,256]{1,0:T(8,128)(2,1)S(1)}, u32[]{:S(2)}, u32[]{:S(2)}) %collective-permute-start) | collective-permute-done | bytes 393248 | tf_op jit(solution)/shard_map/ppermute | solution.py:59
  42.8 2.9 %edge_weights.1 = (bf16[3,512,512]{2,1,0:T(8,128)(2,1)S(1)}, bf16[512,512]{1,0:T(8,128)(2,1)S(1)}, bf16[768,256]{1,0:T(8,128)(2,1)S(1)}, bf16[3,128,512]{2,1,0:T(8,128)(2,1)}) custom-call(s32[2]{0:T(128)S(1)} %pad_add_fusion.2.info, bf16[3,256,512]{2,1,0:T(8,128)(2,1)} %wi.4, bf16[256,512]{1,0:T(8,128)(2,1)} %wo.4, ...), custom_call_target="tpu_custom_call" | custom-call | bytes 7000000 | tf_op jit(solution)/shard_map/edge_weights/pallas_call | solution.py:96
  47.2 2.7 %collective-permute-start.10 = (bf16[3,128,512]{2,1,0:T(8,128)(2,1)}, bf16[3,128,512]{2,1,0:T(8,128)(2,1)S(1)}, u32[]{:S(2)}, u32[]{:S(2)}) collective-permute-start(bf16[3,128,512]{2,1,0:T(8,128)(2,1)} %get-tuple-element.104), channel_id=1, source_target_pairs={{0,5},{1,4},{2,7},{3,6},{4,1},{5,0},{6,3},{7,2},{8,13},{9,12},{10,... | collective-permute-start | bytes 1179656 | tf_op jit(solution)/shard_map/ppermute | solution.py:78
  52.2 6.4 %collective-permute-done.10.got = bf16[3,128,512]{2,1,0:T(8,128)(2,1)S(1)} collective-permute-done((bf16[3,128,512]{2,1,0:T(8,128)(2,1)}, bf16[3,128,512]{2,1,0:T(8,128)(2,1)S(1)}, u32[]{:S(2)}, u32[]{:S(2)}) %collective-permute-start.10) | collective-permute-done | bytes 393248 | tf_op jit(solution)/shard_map/ppermute | solution.py:78
  58.6 1.9 collective-permute-start.11
  60.6 4.8 %collective-permute-done.3.high = bf16[32,512]{1,0:T(8,128)(2,1)S(1)} collective-permute-done((bf16[32,512]{1,0:T(8,128)(2,1)S(1)}, bf16[32,512]{1,0:T(8,128)(2,1)S(1)}, u32[]{:S(2)}, u32[]{:S(2)}) %collective-permute-start.3) | collective-permute-done | bytes 32800 | tf_op jit(solution)/shard_map/ppermute | solution.py:69
  66.4 4.3 %edges_forward_fine.1 = (f32[576,512]{1,0:T(8,128)S(1)}, bf16[576,512]{1,0:T(8,128)(2,1)S(1)}, f32[576,512]{1,0:T(8,128)S(1)}, f32[576,1]{1,0:T(8,128)S(1)}, bf1...) custom-call(s32[2]{0:T(128)S(1)} %pad_add_fusion.2.info, ...), custom_call_target="tpu_custom_call" | custom-call | flops 1585446912 | bytes 8000000 | tf_op jit(solution)/shard_map/edges_forward_fine/pallas_call | solution.py:96
  72.3 3.2 %edges_forward_long.1 = (f32[192,512]{1,0:T(8,128)S(1)}, bf16[192,512]{1,0:T(8,128)(2,1)S(1)}, f32[192,512]{1,0:T(8,128)S(1)}, f32[192,1]{1,0:T(8,128)S(1)}, bf1...) custom-call(s32[2]{0:T(128)S(1)} %pad_add_fusion.2.info, ...), custom_call_target="tpu_custom_call" | custom-call | flops 1283457024 | bytes 6000000 | tf_op jit(solution)/shard_map/edges_forward_long/pallas_call | solution.py:96
  75.5 1.7 collective-permute-start.9
  77.2 1.8 node_weights.1
  79.1 7.9 %nodes_and_edges_backward.1 = (bf16[192,256]{1,0:T(8,128)(2,1)}, f32[192,256]{1,0:T(8,128)S(1)}, bf16[2304,256]{1,0:T(8,128)(2,1)S(1)}, bf16[2304,256]{1,0:T(8,1...) custom-call(s32[2]{0:T(128)S(1)} %pad_add_fusion.2.info, ...), custom_call_target="tpu_custom_call" | custom-call | flops 1610612736 | bytes 14000000 | tf_op jit(solution)/shard_map/nodes_and_edges_backward/pallas_call | solution.py:96
  87.9 4.6 %collective-permute-start.18 = (bf16[1536,256]{1,0:T(8,128)(2,1)S(1)}, bf16[1536,256]{1,0:T(8,128)(2,1)S(1)}, u32[]{:S(2)}, u32[]{:S(2)}) collective-permute-start(bf16[1536,256]{1,0:T(8,128)(2,1)S(1)} %get-tuple-element.129), channel_id=1, source_target_pairs={{0,2},{2,0},{4,6},{6,4},{8,10},{10,8},{12,14},{14,12},{16,18},{18,... | collective-permute-start | bytes 2359304 | tf_op jit(solution)/shard_map/ppermute | solution.py:64
  92.5 1.9 collective-permute-done.18.got
  95.6 10.0 %collective-permute-done.19.first = bf16[768,256]{1,0:T(8,128)(2,1)S(1)} collective-permute-done((bf16[768,256]{1,0:T(8,128)(2,1)S(1)}, bf16[768,256]{1,0:T(8,128)(2,1)S(1)}, u32[]{:S(2)}, u32[]{:S(2)}) %collective-permute-start.19) | collective-permute-done | bytes 393248 | tf_op jit(solution)/shard_map/ppermute | solution.py:59
  106.8 2.0 combine.1
  108.8 8.5 %all-to-all-start.1 = ((bf16[64,72,128]{2,1,0:T(8,128)(2,1)}), bf16[64,72,128]{2,1,0:T(8,128)(2,1)S(1)}, u32[]{:S(2)}, u32[]{:S(2)}) async-start(bf16[64,72,128]{2,1,0:T(8,128)(2,1)} %combine.1), calls=%async_computation.1 | async-start | bytes 2359296 | tf_op jit(solution)/shard_map/all_to_all | solution.py:84
  119.3 2.5 %input_gradients.1 = (bf16[768,256]{1,0:T(8,128)(2,1)S(1)}, bf16[768,256]{1,0:T(8,128)(2,1)S(1)}, f32[256,256]{1,0:T(8,128)S(1)}, bf16[256,256]{1,0:T(8,128)(2,1)S(1)}) custom-call(s32[2]{0:T(128)S(1)} %pad_add_fusion.2.info, bf16[768,512]{1,0:T(8,128)(2,1)S(1)} %copy-done.3, bf16[1536,256]{1,0:T(8,128)(2,1)} %gl_own.3, bf16[1536,256]{1,0:T(8,128)(2,1)} %gl_own.3, ...), custom_call_target="tpu_custom_call" | custom-call | flops 805306368 | bytes 5000000 | tf_op jit(solution)/shard_map/input_gradients/pallas_call | solution.py:96
  124.7 2.1 %collective-permute-done.14 = bf16[256,256]{1,0:T(8,128)(2,1)S(1)} collective-permute-done((bf16[256,256]{1,0:T(8,128)(2,1)S(1)}, bf16[256,256]{1,0:T(8,128)(2,1)S(1)}, u32[]{:S(2)}, u32[]{:S(2)}) %collective-permute-start.14) | collective-permute-done | bytes 131104 | tf_op jit(solution)/shard_map/ppermute | solution.py:59
  126.9 5.8 %collective-permute-start.15 = (bf16[32,256]{1,0:T(8,128)(2,1)S(1)}, bf16[32,256]{1,0:T(8,128)(2,1)S(1)}, u32[]{:S(2)}, u32[]{:S(2)}) collective-permute-start(bf16[32,256]{1,0:T(8,128)(2,1)S(1)} %get-tuple-element.145), channel_id=1, source_target_pairs={{0,254},{2,0},{4,2},{6,4},{8,6},{10,8},{12,10},{14,12},{16,14},{18... | collective-permute-start | bytes 49160 | tf_op jit(solution)/shard_map/ppermute | solution.py:69
  132.7 2.7 %collective-permute-start.16 = (bf16[32,256]{1,0:T(8,128)(2,1)S(1)}, bf16[32,256]{1,0:T(8,128)(2,1)S(1)}, u32[]{:S(2)}, u32[]{:S(2)}) collective-permute-start(bf16[32,256]{1,0:T(8,128)(2,1)S(1)} %get-tuple-element.144), channel_id=1, source_target_pairs={{0,2},{2,4},{4,6},{6,8},{8,10},{10,12},{12,14},{14,16},{16,18},{18... | collective-permute-start | bytes 49160 | tf_op jit(solution)/shard_map/ppermute | solution.py:69
  135.4 20.7 %collective-permute-done.15 = bf16[32,256]{1,0:T(8,128)(2,1)S(1)} collective-permute-done((bf16[32,256]{1,0:T(8,128)(2,1)S(1)}, bf16[32,256]{1,0:T(8,128)(2,1)S(1)}, u32[]{:S(2)}, u32[]{:S(2)}) %collective-permute-start.15) | collective-permute-done | bytes 16416 | tf_op jit(solution)/shard_map/ppermute | solution.py:69
  156.1 1.5 edge_output_rows.1.output
  157.6 1.5 edge_gradient_rows.1.grads
  161.0 35.9 %all_to_all.15 = bf16[64,56,128]{2,1,0:T(8,128)(2,1)S(1)} all-to-all(bf16[64,56,128]{2,1,0:T(8,128)(2,1)S(1)} %get-tuple-element.133), channel_id=1, replica_groups={{0,4,8,12,16,20,24,28,32,36,40,44,48,52,56,60,64,68,72,76,80,84,88,92,9..., dimensions={0} | all-to-all | bytes 1835008 | tf_op jit(solution)/shard_map/all_to_all | solution.py:84
  196.9 1.7 collective-permute-start.21
  200.7 2.5 %results.1 = (f32[3,256,512]{2,1,0:T(8,128)}, f32[256,512]{1,0:T(8,128)}, f32[2,256,512]{2,1,0:T(8,128)}, f32[256,512]{1,0:T(8,128)}) custom-call(s32[2]{0:T(128)S(1)} %pad_add_fusion.2.info, bf16[2,1792,128]{2,1,0:T(8,128)(2,1)S(1)} %bitcast.16, bf16[2,1792,128]{2,1,0:T(8,128)(2,1)S(1)} %collective-permute-done.21.other), custom_call_target="tpu_custom_call" | custom-call | bytes 6000000 | tf_op jit(solution)/shard_map/results/pallas_call | solution.py:684
  (102 shorter events, 19.9 us)
Async XLA Ops:
  0.7 6.5 %copy-start.20 = (s32[12,128]{1,0:T(8,128)S(1)}, s32[12,128]{1,0:T(8,128)}, u32[]{:S(2)}) copy-start(s32[12,128]{1,0:T(8,128)} %param.19) | copy-start | bytes 18436
  0.7 6.5 %copy-start.21 = (s32[12,128]{1,0:T(8,128)S(1)}, s32[12,128]{1,0:T(8,128)}, u32[]{:S(2)}) copy-start(s32[12,128]{1,0:T(8,128)} %param.20) | copy-start | bytes 18436
  2.6 5.4 %collective-permute-start.1 = (bf16[384,256]{1,0:T(8,128)(2,1)S(1)}, bf16[384,256]{1,0:T(8,128)(2,1)S(1)}, u32[]{:S(2)}, u32[]{:S(2)}) collective-permute-start(bf16[384,256]{1,0:T(8,128)(2,1)S(1)} %get-tuple-element.92), channel_id=1, source_target_pairs={{0,1},{1,0},{2,3},{3,2},{4,5},{5,4},{6,7},{7,6},{8,9},{9,8},{10,11... | collective-permute-start | bytes 589832 | tf_op jit(solution)/shard_map/ppermute | solution.py:59
  4.7 21.2 %collective-permute-start.4 = (bf16[4,128,512]{2,1,0:T(8,128)(2,1)S(1)}, bf16[4,128,512]{2,1,0:T(8,128)(2,1)S(1)}, u32[]{:S(2)}, u32[]{:S(2)}) collective-permute-start(bf16[4,128,512]{2,1,0:T(8,128)(2,1)S(1)} %get-tuple-element.93), channel_id=1, source_target_pairs={{0,5},{1,4},{2,7},{3,6},{4,1},{5,0},{6,3},{7,2},{8,13},{9,12},{10,... | collective-permute-start | bytes 1572872 | tf_op jit(solution)/shard_map/ppermute | solution.py:78
  10.1 40.6 %all-to-all-start = ((bf16[64,8,512]{2,1,0:T(8,128)(2,1)}), bf16[64,8,512]{2,1,0:T(8,128)(2,1)}, u32[]{:S(2)}, u32[]{:S(2)}) async-start(bf16[64,8,512]{2,1,0:T(8,128)(2,1)} %coarse_rows.1), calls=%async_computation | async-start | bytes 1048576 | tf_op jit(solution)/shard_map/all_to_all | solution.py:84
  25.9 16.9 %collective-permute-start.5 = (bf16[4,128,512]{2,1,0:T(8,128)(2,1)S(1)}, bf16[4,128,512]{2,1,0:T(8,128)(2,1)S(1)}, u32[]{:S(2)}, u32[]{:S(2)}) collective-permute-start(bf16[4,128,512]{2,1,0:T(8,128)(2,1)S(1)} %collective-permute-done.4.got), channel_id=1, source_target_pairs={{0,2},{2,0},{4,6},{6,4},{8,10},{10,8},{12,14},{14,12},{16,18},{18,... | collective-permute-start | bytes 1572872 | tf_op jit(solution)/shard_map/ppermute | solution.py:64
  27.8 15.0 %collective-permute-start = (bf16[768,256]{1,0:T(8,128)(2,1)S(1)}, bf16[768,256]{1,0:T(8,128)(2,1)S(1)}, u32[]{:S(2)}, u32[]{:S(2)}) collective-permute-start(bf16[768,256]{1,0:T(8,128)(2,1)S(1)} %get-tuple-element.91), channel_id=1, source_target_pairs={{0,1},{1,0},{2,3},{3,2},{4,5},{5,4},{6,7},{7,6},{8,9},{9,8},{10,11... | collective-permute-start | bytes 1179656 | tf_op jit(solution)/shard_map/ppermute | solution.py:59
  47.2 11.4 %collective-permute-start.10 = (bf16[3,128,512]{2,1,0:T(8,128)(2,1)}, bf16[3,128,512]{2,1,0:T(8,128)(2,1)S(1)}, u32[]{:S(2)}, u32[]{:S(2)}) collective-permute-start(bf16[3,128,512]{2,1,0:T(8,128)(2,1)} %get-tuple-element.104), channel_id=1, source_target_pairs={{0,5},{1,4},{2,7},{3,6},{4,1},{5,0},{6,3},{7,2},{8,13},{9,12},{10,... | collective-permute-start | bytes 1179656 | tf_op jit(solution)/shard_map/ppermute | solution.py:78
  50.7 20.8 %collective-permute-start.6 = (bf16[64,8,512]{2,1,0:T(8,128)(2,1)}, bf16[64,8,512]{2,1,0:T(8,128)(2,1)S(1)}, u32[]{:S(2)}, u32[]{:S(2)}) collective-permute-start(bf16[64,8,512]{2,1,0:T(8,128)(2,1)} %all-to-all-done), channel_id=1, source_target_pairs={{0,2},{2,0},{4,6},{6,4},{8,10},{10,8},{12,14},{14,12},{16,18},{18,... | collective-permute-start | bytes 1572872 | tf_op jit(solution)/shard_map/ppermute | solution.py:64
  51.6 9.0 %collective-permute-start.2 = (bf16[32,512]{1,0:T(8,128)(2,1)S(1)}, bf16[32,512]{1,0:T(8,128)(2,1)S(1)}, u32[]{:S(2)}, u32[]{:S(2)}) collective-permute-start(bf16[32,512]{1,0:T(8,128)(2,1)S(1)} %pad_maximum_fusion.1), channel_id=1, source_target_pairs={{0,2},{2,4},{4,6},{6,8},{8,10},{10,12},{12,14},{14,16},{16,18},{18... | collective-permute-start | bytes 98312 | tf_op jit(solution)/shard_map/ppermute | solution.py:69
  51.6 27.4 %collective-permute-start.12 = (bf16[768,256]{1,0:T(8,128)(2,1)}, bf16[768,256]{1,0:T(8,128)(2,1)S(1)}, u32[]{:S(2)}, u32[]{:S(2)}) collective-permute-start(bf16[768,256]{1,0:T(8,128)(2,1)} %copy-done.19), channel_id=1, source_target_pairs={{0,1},{1,0},{2,3},{3,2},{4,5},{5,4},{6,7},{7,6},{8,9},{9,8},{10,11... | collective-permute-start | bytes 1179656 | tf_op jit(solution)/shard_map/ppermute | solution.py:59
  58.6 18.6 %collective-permute-start.11 = (bf16[3,128,512]{2,1,0:T(8,128)(2,1)S(1)}, bf16[3,128,512]{2,1,0:T(8,128)(2,1)S(1)}, u32[]{:S(2)}, u32[]{:S(2)}) collective-permute-start(bf16[3,128,512]{2,1,0:T(8,128)(2,1)S(1)} %collective-permute-done.10.got), channel_id=1, source_target_pairs={{0,2},{2,0},{4,6},{6,4},{8,10},{10,8},{12,14},{14,12},{16,18},{18,... | collective-permute-start | bytes 1179656 | tf_op jit(solution)/shard_map/ppermute | solution.py:64
  60.6 4.8 %collective-permute-start.3 = (bf16[32,512]{1,0:T(8,128)(2,1)S(1)}, bf16[32,512]{1,0:T(8,128)(2,1)S(1)}, u32[]{:S(2)}, u32[]{:S(2)}) collective-permute-start(bf16[32,512]{1,0:T(8,128)(2,1)S(1)} %pad_maximum_fusion.2), channel_id=1, source_target_pairs={{0,254},{2,0},{4,2},{6,4},{8,6},{10,8},{12,10},{14,12},{16,14},{18... | collective-permute-start | bytes 98312 | tf_op jit(solution)/shard_map/ppermute | solution.py:69
  71.5 7.6 %collective-permute-start.8 = (bf16[192,512]{1,0:T(8,128)(2,1)S(1)}, bf16[192,512]{1,0:T(8,128)(2,1)S(1)}, u32[]{:S(2)}, u32[]{:S(2)}) collective-permute-start(bf16[192,512]{1,0:T(8,128)(2,1)S(1)} %get-tuple-element.101), channel_id=1, source_target_pairs={{0,1},{1,0},{2,3},{3,2},{4,5},{5,4},{6,7},{7,6},{8,9},{9,8},{10,11... | collective-permute-start | bytes 589832 | tf_op jit(solution)/shard_map/ppermute | solution.py:59
  75.5 11.5 %copy-start.15 = (bf16[192,256]{1,0:T(8,128)(2,1)}, bf16[192,256]{1,0:T(8,128)(2,1)S(1)}, u32[]{:S(2)}) copy-start(bf16[192,256]{1,0:T(8,128)(2,1)S(1)} %get-tuple-element.97.own_l) | copy-start | bytes 294916
  75.5 3.6 %collective-permute-start.9 = (bf16[16,512]{1,0:T(8,128)(2,1)S(1)}, bf16[16,512]{1,0:T(8,128)(2,1)S(1)}, u32[]{:S(2)}, u32[]{:S(2)}) collective-permute-start(bf16[16,512]{1,0:T(8,128)(2,1)S(1)} %get-tuple-element.103), channel_id=1, source_target_pairs={{0,1},{1,0},{2,3},{3,2},{4,5},{5,4},{6,7},{7,6},{8,9},{9,8},{10,11... | collective-permute-start | bytes 49160 | tf_op jit(solution)/shard_map/ppermute | solution.py:59
  87.9 18.9 %copy-start.11 = (bf16[192,512]{1,0:T(8,128)(2,1)}, bf16[192,512]{1,0:T(8,128)(2,1)S(1)}, u32[]{:S(2)}) copy-start(bf16[192,512]{1,0:T(8,128)(2,1)S(1)} %get-tuple-element.120.recv_sum) | copy-start | bytes 589828
  87.9 18.9 %copy-start.13 = (f32[192,256]{1,0:T(8,128)}, f32[192,256]{1,0:T(8,128)S(1)}, u32[]{:S(2)}) copy-start(f32[192,256]{1,0:T(8,128)S(1)} %get-tuple-element.123) | copy-start | bytes 589828
  87.9 6.5 %collective-permute-start.18 = (bf16[1536,256]{1,0:T(8,128)(2,1)S(1)}, bf16[1536,256]{1,0:T(8,128)(2,1)S(1)}, u32[]{:S(2)}, u32[]{:S(2)}) collective-permute-start(bf16[1536,256]{1,0:T(8,128)(2,1)S(1)} %get-tuple-element.129), channel_id=1, source_target_pairs={{0,2},{2,0},{4,6},{6,4},{8,10},{10,8},{12,14},{14,12},{16,18},{18,... | collective-permute-start | bytes 2359304 | tf_op jit(solution)/shard_map/ppermute | solution.py:64
  92.5 14.3 %collective-permute-start.17 = (bf16[2304,256]{1,0:T(8,128)(2,1)S(1)}, bf16[2304,256]{1,0:T(8,128)(2,1)S(1)}, u32[]{:S(2)}, u32[]{:S(2)}) collective-permute-start(bf16[2304,256]{1,0:T(8,128)(2,1)S(1)} %get-tuple-element.127), channel_id=1, source_target_pairs={{0,2},{2,0},{4,6},{6,4},{8,10},{10,8},{12,14},{14,12},{16,18},{18,... | collective-permute-start | bytes 3538952 | tf_op jit(solution)/shard_map/ppermute | solution.py:64
  95.1 10.4 %collective-permute-start.19 = (bf16[768,256]{1,0:T(8,128)(2,1)S(1)}, bf16[768,256]{1,0:T(8,128)(2,1)S(1)}, u32[]{:S(2)}, u32[]{:S(2)}) collective-permute-start(bf16[768,256]{1,0:T(8,128)(2,1)S(1)} %get-tuple-element.130), channel_id=1, source_target_pairs={{0,1},{1,0},{2,3},{3,2},{4,5},{5,4},{6,7},{7,6},{8,9},{9,8},{10,11... | collective-permute-start | bytes 1179656 | tf_op jit(solution)/shard_map/ppermute | solution.py:59
  95.6 11.2 %collective-permute-start.20 = (bf16[768,256]{1,0:T(8,128)(2,1)S(1)}, bf16[768,256]{1,0:T(8,128)(2,1)S(1)}, u32[]{:S(2)}, u32[]{:S(2)}) collective-permute-start(bf16[768,256]{1,0:T(8,128)(2,1)S(1)} %get-tuple-element.131), channel_id=1, source_target_pairs={{0,5},{1,4},{2,7},{3,6},{4,1},{5,0},{6,3},{7,2},{8,13},{9,12},{10,... | collective-permute-start | bytes 1179656 | tf_op jit(solution)/shard_map/ppermute | solution.py:78
  108.8 50.3 %all-to-all-start.1 = ((bf16[64,72,128]{2,1,0:T(8,128)(2,1)}), bf16[64,72,128]{2,1,0:T(8,128)(2,1)S(1)}, u32[]{:S(2)}, u32[]{:S(2)}) async-start(bf16[64,72,128]{2,1,0:T(8,128)(2,1)} %combine.1), calls=%async_computation.1 | async-start | bytes 2359296 | tf_op jit(solution)/shard_map/all_to_all | solution.py:84
  121.8 34.3 %copy-start.10 = (bf16[576,256]{1,0:T(8,128)(2,1)S(1)}, bf16[576,256]{1,0:T(8,128)(2,1)}, u32[]{:S(2)}) copy-start(bf16[576,256]{1,0:T(8,128)(2,1)} %copy-done.9) | copy-start | bytes 884740
  121.8 34.3 %copy-start.16 = (bf16[192,256]{1,0:T(8,128)(2,1)S(1)}, bf16[192,256]{1,0:T(8,128)(2,1)}, u32[]{:S(2)}) copy-start(bf16[192,256]{1,0:T(8,128)(2,1)} %copy-done.15) | copy-start | bytes 294916
  121.8 5.0 %collective-permute-start.14 = (bf16[256,256]{1,0:T(8,128)(2,1)S(1)}, bf16[256,256]{1,0:T(8,128)(2,1)S(1)}, u32[]{:S(2)}, u32[]{:S(2)}) collective-permute-start(bf16[256,256]{1,0:T(8,128)(2,1)S(1)} %get-tuple-element.125), channel_id=1, source_target_pairs={{0,1},{1,0},{2,3},{3,2},{4,5},{5,4},{6,7},{7,6},{8,9},{9,8},{10,11... | collective-permute-start | bytes 393224 | tf_op jit(solution)/shard_map/ppermute | solution.py:59
  123.2 32.9 %collective-permute-start.7 = (bf16[768,256]{1,0:T(8,128)(2,1)S(1)}, bf16[768,256]{1,0:T(8,128)(2,1)S(1)}, u32[]{:S(2)}, u32[]{:S(2)}) collective-permute-start(bf16[768,256]{1,0:T(8,128)(2,1)S(1)} %pad_maximum_fusion), channel_id=1, source_target_pairs={{0,1},{1,0},{2,3},{3,2},{4,5},{5,4},{6,7},{7,6},{8,9},{9,8},{10,11... | collective-permute-start | bytes 1179656 | tf_op jit(solution)/shard_map/ppermute | solution.py:59
  123.5 34.1 %collective-permute-start.13 = (bf16[768,256]{1,0:T(8,128)(2,1)S(1)}, bf16[768,256]{1,0:T(8,128)(2,1)S(1)}, u32[]{:S(2)}, u32[]{:S(2)}) collective-permute-start(bf16[768,256]{1,0:T(8,128)(2,1)S(1)} %get-tuple-element.122), channel_id=1, source_target_pairs={{0,1},{1,0},{2,3},{3,2},{4,5},{5,4},{6,7},{7,6},{8,9},{9,8},{10,11... | collective-permute-start | bytes 1179656 | tf_op jit(solution)/shard_map/ppermute | solution.py:59
  126.9 29.2 %collective-permute-start.15 = (bf16[32,256]{1,0:T(8,128)(2,1)S(1)}, bf16[32,256]{1,0:T(8,128)(2,1)S(1)}, u32[]{:S(2)}, u32[]{:S(2)}) collective-permute-start(bf16[32,256]{1,0:T(8,128)(2,1)S(1)} %get-tuple-element.145), channel_id=1, source_target_pairs={{0,254},{2,0},{4,2},{6,4},{8,6},{10,8},{12,10},{14,12},{16,14},{18... | collective-permute-start | bytes 49160 | tf_op jit(solution)/shard_map/ppermute | solution.py:69
  132.7 23.4 %collective-permute-start.16 = (bf16[32,256]{1,0:T(8,128)(2,1)S(1)}, bf16[32,256]{1,0:T(8,128)(2,1)S(1)}, u32[]{:S(2)}, u32[]{:S(2)}) collective-permute-start(bf16[32,256]{1,0:T(8,128)(2,1)S(1)} %get-tuple-element.144), channel_id=1, source_target_pairs={{0,2},{2,4},{4,6},{6,8},{8,10},{10,12},{12,14},{14,16},{16,18},{18... | collective-permute-start | bytes 49160 | tf_op jit(solution)/shard_map/ppermute | solution.py:69
  161.0 37.6 %copy-start.14 = (f32[192,256]{1,0:T(8,128)S(1)}, f32[192,256]{1,0:T(8,128)}, u32[]{:S(2)}) copy-start(f32[192,256]{1,0:T(8,128)} %copy-done.13) | copy-start | bytes 589828
  196.9 3.8 %collective-permute-start.21 = (bf16[2,1792,128]{2,1,0:T(8,128)(2,1)S(1)}, bf16[2,1792,128]{2,1,0:T(8,128)(2,1)S(1)}, u32[]{:S(2)}, u32[]{:S(2)}) collective-permute-start(bf16[2,1792,128]{2,1,0:T(8,128)(2,1)S(1)} %bitcast.15), channel_id=1, source_target_pairs={{0,2},{2,0},{4,6},{6,4},{8,10},{10,8},{12,14},{14,12},{16,18},{18,... | collective-permute-start | bytes 2752520 | tf_op jit(solution)/shard_map/ppermute | solution.py:64
  (15 other events, 28.6 us)

commit v4 on v3

--- a/solution.py
+++ b/solution.py
@@ -15,7 +15,7 @@
 BF16 = jnp.bfloat16
 I32 = jnp.int32
 LANES = 128
-VMEM_LIMIT = 28 * 1024 * 1024
+MIB = 1024 * 1024
 
 
 def dot(left, right):
@@ -92,18 +92,21 @@
     return pl.BlockSpec(shape, index, pipeline_mode=pl.Buffered(1))
 
 
-def call(kernel, info, operands, in_specs, outs, scratch=(), flops=0, moved=0, name=None):
+def call(kernel, info, operands, in_specs, outs, scratch=(), flops=0, moved=0, name=None, in_hbm=(), limit=14):
     return pl.pallas_call(
         kernel,
         grid_spec=pltpu.PrefetchScalarGridSpec(
             num_scalar_prefetch=1,
             grid=(1,),
             in_specs=in_specs,
-            out_specs=[whole(shape) for shape, _ in outs],
+            out_specs=[
+                pl.BlockSpec(memory_space=pltpu.HBM) if i in in_hbm else whole(shape)
+                for i, (shape, _) in enumerate(outs)
+            ],
             scratch_shapes=list(scratch),
         ),
         out_shape=[jax.ShapeDtypeStruct(shape, dtype) for shape, dtype in outs],
-        compiler_params=pltpu.CompilerParams(vmem_limit_bytes=VMEM_LIMIT),
+        compiler_params=pltpu.CompilerParams(vmem_limit_bytes=limit * MIB),
         cost_estimate=pl.CostEstimate(flops=flops, bytes_accessed=moved, transcendentals=0),
         name=name,
     )(info, *operands)
@@ -113,19 +116,41 @@
     return pltpu.with_memory_space_constraint(value, pltpu.HBM)
 
 
-def pack_kernel(info, xf, xl, n, ng, wi, wo, xs, ns, wes):
-    fine, nodes = xf.shape[0], n.shape[0]
-    ns[:nodes] = n[...]
-    ns[nodes:] = ng[...]
+def pack_kernel(info, xf, xl, n, wi, wo, xs, wes, low, high):
+    fine = xf.shape[0]
+    low[...] = n[:HALO]
+    high[...] = n[n.shape[0] - HALO :]
     wes[:3] = wi[...]
     wes[3] = wo[...]
     xs[:fine] = xf[...]
-    xs[fine:] = xl[...]
-
-
-def coarse_kernel(info, n_own, n_got, idx_f, idx_l, out):
-    rows = jnp.concatenate([n_own[:COARSE], n_got[:COARSE]], 1)
-    out[...] = jnp.broadcast_to(rows[None], out.shape)
+    xs[fine : fine + xl.shape[0]] = xl[...]
+    xs[fine + xl.shape[0] :] = n[...]
+
+
+def coarse_kernel(info, n_own, n_got, after, out, staged, sem):
+    half = n_own.shape[1]
+    for columns, n in ((slice(0, half), n_own), (slice(half, 2 * half), n_got)):
+        staged[:, :, columns] = jnp.broadcast_to(n[:COARSE][None], (staged.shape[0], COARSE, half))
+    copy = pltpu.make_async_copy(staged, out, sem)
+    copy.start()
+    copy.wait()
+
+
+def gate_kernel(info, value, *rest):
+    pass
+
+
+def gated(info, value, after, space=pl.ANY):
+    anywhere = pl.BlockSpec(memory_space=pl.ANY)
+    return pl.pallas_call(
+        gate_kernel,
+        in_specs=[pl.BlockSpec(memory_space=pltpu.SMEM)] + [anywhere] + [pl.BlockSpec(memory_space=space)] * len(after),
+        out_specs=anywhere,
+        out_shape=jax.ShapeDtypeStruct(value.shape, value.dtype),
+        input_output_aliases={1: 0},
+        compiler_params=pltpu.CompilerParams(vmem_limit_bytes=MIB),
+        name="gate",
+    )(info, value, *after)
 
 
 def lat_stage_kernel(info, keep, got, first, second):
@@ -134,7 +159,7 @@
     second[...] = (keep[rows:].astype(F32) + got[rows:].astype(F32)).astype(BF16)
 
 
-def combine_kernel(info, keep, got, first, second, out):
+def combine_kernel(info, keep, got, first, second, out, staged, sem):
     chips = out.shape[0]
     rows = first.shape[0]
     edge_rows_count, far_rows = 2 * rows - chips * COARSE, chips * COARSE
@@ -148,22 +173,40 @@
     share = weights.shape[0] // half_chips
     parts = [weights[:, i * LANES : (i + 1) * LANES].reshape(half_chips, share, LANES) for i in range(2)]
     coarse = [far[:, i * LANES : (i + 1) * LANES].reshape(chips, COARSE, LANES) for i in range(2)]
-    out[...] = jnp.concatenate([jnp.concatenate(parts, 0)] + coarse, 1).astype(BF16)
-
-
-def share_kernel(info, arrived, output, grads, low, high, weights, coarse, *, scale):
-    share = weights.shape[1]
-    total = jnp.sum(arrived[...].astype(F32), 0)
-    weights[...] = jnp.broadcast_to((total[:share] * scale).astype(BF16)[None], weights.shape)
+    staged[...] = jnp.concatenate([jnp.concatenate(parts, 0)] + coarse, 1).astype(BF16)
+    copy = pltpu.make_async_copy(staged, out, sem)
+    copy.start()
+    copy.wait()
+
+
+def share_kernel(info, arrived, output, low, high, weights, coarse, taken, staged, sem, *, scale):
+    share = staged.shape[1]
+    copy = pltpu.make_async_copy(arrived, taken, sem)
+    copy.start()
+    copy.wait()
+    total = jnp.sum(taken[...].astype(F32), 0)
+    staged[...] = jnp.broadcast_to((total[:share] * scale).astype(BF16)[None], staged.shape)
+    copy = pltpu.make_async_copy(staged, weights, sem)
+    copy.start()
     coarse[...] = total[share:]
-
-
-def rows_kernel(info, own_f, own_l, got, out):
+    copy.wait()
+
+
+def rows_kernel(info, own_f, own_l, got, out, sems):
     lat = info[0]
     fine, longs = own_f.shape[0], own_l.shape[0]
-    for side, f, l in ((lat, own_f[...], own_l[...]), (1 - lat, got[:fine], got[fine:])):
-        out[pl.ds(pl.multiple_of(side * fine, 64), fine)] = f
-        out[pl.ds(pl.multiple_of(FINE + side * longs, 64), longs)] = l
+    copies = []
+    for side, f, l in (
+        (lat, own_f, own_l),
+        (1 - lat, got.at[pl.ds(0, fine)], got.at[pl.ds(fine, longs)]),
+    ):
+        copies.append((f, out.at[pl.ds(pl.multiple_of(side * fine, 64), fine)]))
+        copies.append((l, out.at[pl.ds(pl.multiple_of(FINE + side * longs, 64), longs)]))
+    made = [pltpu.make_async_copy(a, b, sems.at[k]) for k, (a, b) in enumerate(copies)]
+    for copy in made:
+        copy.start()
+    for copy in made:
+        copy.wait()
 
 
 def results_kernel(info, mine, other, inner, outer, node_inner, node_outer, staged, sems):
@@ -183,12 +226,13 @@
         copy.wait()
 
 
-def edge_weights_kernel(info, wi, wo, got, again, gf, gl, ni, no, after, full_in, full_out, gs, wns):
+def edge_weights_kernel(info, wi, wo, got, again, gf, gl, ng, ni, no, after, idx_f, idx_l, full_in, full_out, gs, wns):
     fine = gf.shape[0]
     wns[:2] = ni[...]
     wns[2] = no[...]
     gs[:fine] = gf[...]
-    gs[fine:] = gl[...]
+    gs[fine : fine + gl.shape[0]] = gl[...]
+    gs[fine + gl.shape[0] :] = ng[...]
     weights_kernel(info, wi, wo, got, again, full_in, full_out)
 
 
@@ -228,14 +272,16 @@
     update[rows] = change.astype(BF16)
 
 
-def fine_kernel(info, x_own, x_got, n_own, n_got, low, high, idx_c, idx_r, w_in, w_out,
+def fine_kernel(info, x_own, x_got, n_own, n_got, low, high, rims_got, idx_c, idx_r, w_in, w_out,
                 slope, act, normed, inverse, out_own, out_sent, partial, sent, ext, update):
     half = x_own.shape[1]
     nodes = n_own.shape[0]
-    ext[:HALO] = low[...]
+    ext[:HALO, :half] = low[...]
+    ext[:HALO, half:] = rims_got[:HALO]
     ext[HALO : HALO + nodes, :half] = n_own[...]
     ext[HALO : HALO + nodes, half:] = n_got[...]
-    ext[HALO + nodes :] = high[...]
+    ext[HALO + nodes :, :half] = high[...]
+    ext[HALO + nodes :, half:] = rims_got[HALO:]
     node_x = ext[HALO : HALO + nodes]
     chunk = 192
     for start in range(0, x_own.shape[0], chunk):
@@ -267,34 +313,58 @@
     sent[...] = total.astype(BF16)
 
 
-def back_kernel(info, partial, got, partial_l, got_l, n_own, n_got, ng_own, ng_got, low, high, nin, nout,
+def column_halves(info, half):
+    lat, core = info[0], info[1]
+    turn = (core + lat) % 2
+
+    def at(which):
+        return pl.ds(pl.multiple_of(which * half, half), half)
+
+    return at(core), at(1 - core), at(turn), at(1 - turn), at(lat), at(1 - lat)
+
+
+def edge_weight_grads(outs, xf, xl, node_x, extended, srow, cols, act_f, act_l, hidden, dpre, dy, near_sum, recv_sum, fine):
+    half = xf.shape[1]
+    head, tail = pl.ds(0, fine), pl.ds(fine, dpre.shape[0] - fine)
+    for out, columns, columns_own in outs:
+        grad = contract_rows(xf[...], dpre[head, columns]) + contract_rows(xl[...], dpre[tail, columns])
+        out[:half] = grad.astype(BF16)
+        grad = contract_rows(extended, near_sum[:, columns]) + contract_rows(srow[:, cols], dpre[tail, columns])
+        out[half : 2 * half] = grad.astype(BF16)
+        out[2 * half : 3 * half] = contract_rows(node_x, recv_sum[:, columns]).astype(BF16)
+        grad = contract_rows(act_f[:, hidden], dy[head, columns_own]) + contract_rows(act_l[:, hidden], dy[tail, columns_own])
+        out[3 * half : 4 * half] = grad.astype(BF16)
+
+
+def far_sums(idx_r, dpre_long, weights, keep, send, count):
+    grads = contract_cols(dpre_long, weights).astype(BF16)
+    far = dot(one_hot_t(idx_r[0:1], 2 * count), grads).astype(BF16)
+    keep[keep.shape[0] - count :] = far[:count]
+    send[send.shape[0] - count :] = far[count:]
+
+
+def back_kernel(info, partial, got, partial_l, got_l, n_own, n_got, ng_own, ng_got, low, high, rims_got, nin, nout,
                 xf_own, xl_own, xf_got, xl_got, gf_own, gl_own, gf_got, gl_got,
                 slope_f, slope_l, act_f, act_l, normed_f, normed_l, inverse_f, inverse_l, srow_l,
                 idx_cf, idx_cl, idx_rf, idx_rl, w_in, w_out,
-                node_out, node_self, keep_own, send_own, keep_pair, send_pair, dpre, near_sum, recv_sum,
-                ndpre, ndy, nact, agg_grad, dy, ext):
-    lat, core = info[0], info[1]
+                node_out, node_self, keep_pair, send_pair, keep_own, send_own, dpre, near_sum, recv_sum,
+                dy, ndpre, ndy, nact, agg_own, agg_grad, ext, ext_own):
+    mine, theirs, mine_own, theirs_own, hidden_mine, hidden_theirs = column_halves(info, n_own.shape[1])
     half = n_own.shape[1]
     nodes = n_own.shape[0]
-    fine, longs = xf_own.shape[0], xl_own.shape[0]
-    mine = pl.ds(pl.multiple_of(core * half, half), half)
-    theirs = pl.ds(pl.multiple_of((1 - core) * half, half), half)
-    turn = (core + lat) % 2
-    mine_own = pl.ds(pl.multiple_of(turn * half, half), half)
-    theirs_own = pl.ds(pl.multiple_of((1 - turn) * half, half), half)
-    hidden_mine = pl.ds(pl.multiple_of(lat * half, half), half)
-    hidden_theirs = pl.ds(pl.multiple_of((1 - lat) * half, half), half)
-
-    ext[:HALO] = low[...]
-    ext[HALO : HALO + nodes, :half] = n_own[...]
-    ext[HALO : HALO + nodes, half:] = n_got[...]
-    ext[HALO + nodes :] = high[...]
-    node_x = ext[HALO : HALO + nodes]
+    fine, longs = xf_got.shape[0], xl_got.shape[0]
+    far_count = keep_pair.shape[0] - 4 * half
+
+    ext[:HALO] = rims_got[:HALO]
+    ext[HALO : HALO + nodes] = n_got[...]
+    ext[HALO + nodes :] = rims_got[HALO:]
+    node_x = jnp.concatenate([n_own[...], n_got[...]], 1)
     received, received_l = got[...].astype(F32), got_l[...].astype(F32)
     total = partial[...] + jnp.concatenate([received[:, half:], received[:, :half]], 1)
     coarse = partial_l[...] + jnp.concatenate([received_l[:, half:], received_l[:, :half]], 1)
     near = coarse.shape[0]
     agg = jnp.concatenate([total[:near] + coarse, total[near:]], 0).astype(BF16)
+    agg_own[...] = agg[:, :half]
     node_value, node_slope = swish_parts(dot(node_x, nin[0]) + dot(agg, nin[1]))
     nact[...] = node_value.astype(BF16)
     node_normed, node_inverse = layer_norm(dot(nact[...], nout[...]))
@@ -325,39 +395,29 @@
 
     tail = pl.ds(fine, longs)
     head = pl.ds(0, fine)
-    srow_grads = contract_cols(dpre[tail], w_in[1]).astype(BF16)
-    rows_pair, rows_own = keep_pair.shape[0], keep_own.shape[0]
-    edge_count, far_count = 4 * half, keep_pair.shape[0] - 4 * half
-    far = dot(one_hot_t(idx_rl[0:1], 2 * far_count), srow_grads).astype(BF16)
-    for value, own, pair in (
-        (far[:far_count], keep_own, keep_pair),
-        (far[far_count:], send_own, send_pair),
-    ):
-        own[rows_own - far_count :] = value[:, :half]
-        pair[rows_pair - far_count :] = value[:, half:]
     near_sum[...] = dot(one_hot_t(idx_rf[0:1], ext.shape[0]), dpre[head]).astype(BF16)
     recv_sum[...] = (
         dot(one_hot_t(idx_rf[1:2], nodes), dpre[head]) + dot(one_hot_t(idx_rl[1:2], nodes), dpre[tail])
     ).astype(BF16)
-    for own, pair, columns, columns_own in (
-        (send_own, send_pair, theirs, theirs_own),
-        (keep_own, keep_pair, mine, mine_own),
-    ):
-        for out, xf, xl, hidden, cols in (
-            (pair, xf_got, xl_got, hidden_theirs, slice(half, 2 * half)),
-            (own, xf_own, xl_own, hidden_mine, slice(0, half)),
-        ):
-            grad = contract_rows(xf[...], dpre[head, columns]) + contract_rows(xl[...], dpre[tail, columns])
-            out[:half] = grad.astype(BF16)
-            grad = contract_rows(ext[:, cols], near_sum[:, columns]) + contract_rows(srow_l[:, cols], dpre[tail, columns])
-            out[half : 2 * half] = grad.astype(BF16)
-            grad = contract_rows(ext[HALO : HALO + nodes, cols], recv_sum[:, columns])
-            out[2 * half : 3 * half] = grad.astype(BF16)
-            grad = contract_rows(act_f[:, hidden], dy[head, columns_own]) + contract_rows(act_l[:, hidden], dy[tail, columns_own])
-            out[3 * half : 4 * half] = grad.astype(BF16)
+    far_sums(idx_rl, dpre[tail], w_in[1, half:], keep_pair, send_pair, far_count)
+    edge_weight_grads(
+        ((send_pair, theirs, theirs_own), (keep_pair, mine, mine_own)),
+        xf_got, xl_got, n_got[...], ext[...], srow_l, slice(half, 2 * half), act_f, act_l, hidden_theirs,
+        dpre, dy, near_sum, recv_sum, fine,
+    )
+    ext_own[:HALO] = low[...]
+    ext_own[HALO : HALO + nodes] = n_own[...]
+    ext_own[HALO + nodes :] = high[...]
+    for own, columns, columns_own in ((send_own, theirs, theirs_own), (keep_own, mine, mine_own)):
         own[4 * half : 5 * half] = contract_rows(n_own[...], ndpre[:, columns]).astype(BF16)
-        own[5 * half : 6 * half] = contract_rows(agg[:, :half], ndpre[:, columns]).astype(BF16)
+        own[5 * half : 6 * half] = contract_rows(agg_own[...], ndpre[:, columns]).astype(BF16)
         own[6 * half : 7 * half] = contract_rows(nact[:, hidden_mine], ndy[:, columns_own]).astype(BF16)
+    far_sums(idx_rl, dpre[tail], w_in[1, :half], keep_own, send_own, far_count)
+    edge_weight_grads(
+        ((send_own, theirs, theirs_own), (keep_own, mine, mine_own)),
+        xf_own, xl_own, n_own[...], ext_own[...], srow_l, slice(0, half), act_f, act_l, hidden_mine,
+        dpre, dy, near_sum, recv_sum, fine,
+    )
 
 
 def inputs_kernel(info, dpre, gf_own, gl_own, g_got, near_sum, recv_sum, w_in,
@@ -434,66 +494,53 @@
     fine_other = block((fine, half), lambda i, s: (1 - s[0], 0))
     long_other = block((longs, half), lambda i, s: (FINE // longs + 1 - s[0], 0))
     quarter_rows = block((quarter, full), lambda i, s: (s[1], 0))
-    sent_x, sent_n, sent_we = call(
+    sent_x, sent_we, rim_low, rim_high = call(
         pack_kernel,
         info,
-        (x_hbm, x_hbm, n_hbm, ng_hbm, wi_hbm, wo_hbm),
+        (x_hbm, x_hbm, n_hbm, wi_hbm, wo_hbm),
         [
-            fine_other, long_other, whole((nodes, half)), whole((nodes, half)),
+            fine_other, long_other, whole((nodes, half)),
             block((3, quarter, full), lambda i, s: (0, s[1], 0)), quarter_rows,
         ],
-        [((rows, half), BF16), ((2 * nodes, half), BF16), ((4, quarter, full), BF16)],
+        [((rows + nodes, half), BF16), ((4, quarter, full), BF16), ((HALO, half), BF16), ((HALO, half), BF16)],
         moved=3_000_000,
         name="pack",
     )
-    node_got = swap_lat(sent_n)
     we_got = other_neighbour(sent_we)
-    x_got = swap_lat(sent_x)
+    x_got = pinned(swap_lat(sent_x))
+    low, high = shifted(rim_high, 1), shifted(rim_low, -1)
+    far_rows = chips * COARSE
     (sent_coarse,) = call(
         coarse_kernel,
         info,
-        (n_hbm, node_got, idx_cf, idx_cl),
-        [whole((16, half)), whole((16, half)), whole((fine, 2)), whole((longs, 3))],
+        (n_hbm, swap_lat(node_latents[:16]), rim_low),
+        [whole((16, half)), whole((16, half)), pl.BlockSpec(memory_space=pl.ANY)],
         [((chips, COARSE, full), BF16)],
+        [pltpu.VMEM((chips, COARSE, full), BF16), pltpu.SemaphoreType.DMA],
         moved=600_000,
         name="coarse_rows",
-    )
-    far_rows = chips * COARSE
+        in_hbm=(0,),
+    )
     same = chips_all_to_all(sent_coarse)
-    other = swap_core(same).reshape(far_rows, full)
-    same = same.reshape(far_rows, full)
-    low = shifted(
-        jnp.concatenate([node_latents[nodes - HALO :], node_got[nodes - HALO : nodes]], 1), 1
-    )
-    high = shifted(jnp.concatenate([node_latents[:HALO], node_got[:HALO]], 1), -1)
     we_again = swap_core(we_got)
+    rims_got = swap_lat(jnp.concatenate([low, high], 0))
 
     got_spec = [whole((4, quarter, full))] * 2
     w_in, w_out, sent_g, sent_wn = call(
         edge_weights_kernel,
         info,
-        (wi_hbm, wo_hbm, we_got, we_again, g_hbm, g_hbm, ni_hbm, no_hbm, x_got),
+        (wi_hbm, wo_hbm, pinned(we_got), pinned(we_again), g_hbm, g_hbm, ng_hbm, ni_hbm, no_hbm, rims_got, idx_cf, idx_cl),
         [whole((3, half, full)), whole((half, full))] + got_spec + [
-            fine_other, long_other, block((2, quarter, full), lambda i, s: (0, s[1], 0)), quarter_rows,
-            pl.BlockSpec(memory_space=pl.ANY),
+            fine_other, long_other, whole((nodes, half)),
+            block((2, quarter, full), lambda i, s: (0, s[1], 0)), quarter_rows,
+            pl.BlockSpec(memory_space=pl.ANY), whole((fine, 2)), whole((longs, 3)),
         ],
-        [((3, full, full), BF16), ((full, full), BF16), ((rows, half), BF16), ((3, quarter, full), BF16)],
+        [((3, full, full), BF16), ((full, full), BF16), ((rows + nodes, half), BF16), ((3, quarter, full), BF16)],
         moved=7_000_000,
         name="edge_weights",
     )
     wn_got = other_neighbour(sent_wn)
-    wn_again = swap_core(wn_got)
     g_got = swap_lat(sent_g)
-    nin, nout = call(
-        weights_kernel,
-        info,
-        (ni_hbm, no_hbm, wn_got, wn_again),
-        [whole((2, half, full)), whole((half, full)), whole((3, quarter, full)), whole((3, quarter, full))],
-        [((2, full, full), BF16), ((full, full), BF16)],
-        moved=3_000_000,
-        name="node_weights",
-    )
-
     def fine_own():
         return block((fine, half), lambda i, s: (s[0], 0))
 
@@ -507,8 +554,8 @@
         return block((longs, half), lambda i, s: (fine // longs, 0))
 
     node_spec = whole((nodes, half))
-    second_nodes = block((nodes, half), lambda i, s: (1, 0))
-    rim = whole((HALO, full))
+    got_nodes = block((nodes, half), lambda i, s: (rows // nodes, 0))
+    rim = whole((HALO, half))
     win_spec, wout_spec = whole((3, full, full)), whole((full, full))
 
     def forward_outs(count, reach):
@@ -526,9 +573,9 @@
     slope_f, act_f, normed_f, inverse_f, fine_out, fine_sent, partial_f, partial_f_sent = call(
         fine_kernel,
         info,
-        (x_hbm, x_got, n_hbm, node_got, low, high, idx_cf, idx_rf, w_in, w_out),
+        (x_hbm, x_got, n_hbm, x_got, low, high, rims_got, idx_cf, idx_rf, w_in, w_out),
         [
-            fine_own(), fine_got(), node_spec, whole((nodes, half)), rim, rim,
+            fine_own(), fine_got(), node_spec, got_nodes, rim, rim, whole((2 * HALO, half)),
             whole((fine, 2)), whole((2, fine)), win_spec, wout_spec,
         ],
         forward_outs(fine, nodes),
@@ -537,12 +584,14 @@
         moved=8_000_000,
         name="edges_forward_fine",
     )
+    other = swap_core(same).reshape(far_rows, full)
+    same = same.reshape(far_rows, full)
     slope_l, act_l, normed_l, inverse_l, long_out, long_sent, partial_l, partial_l_sent, srow_l = call(
         long_kernel,
         info,
-        (x_hbm, x_got, n_hbm, node_got, pinned(same), pinned(other), idx_cl, idx_rl, w_in, w_out),
+        (x_hbm, x_got, n_hbm, x_got, same, other, idx_cl, idx_rl, w_in, w_out),
         [
-            long_own(), long_got(), whole((16, half)), whole((16, half)),
+            long_own(), long_got(), whole((16, half)), block((16, half), lambda i, s: (rows // 16, 0)),
             whole((far_rows, full)), whole((far_rows, full)),
             whole((longs, 3)), whole((3, longs)), win_spec, wout_spec,
         ],
@@ -552,23 +601,34 @@
         moved=6_000_000,
         name="edges_forward_long",
     )
+    wn_got = gated(info, wn_got, (partial_l_sent, partial_f_sent))
+    wn_again = swap_core(wn_got)
+    nin, nout = call(
+        weights_kernel,
+        info,
+        (ni_hbm, no_hbm, wn_got, wn_again),
+        [whole((2, half, full)), whole((half, full)), whole((3, quarter, full)), whole((3, quarter, full))],
+        [((2, full, full), BF16), ((full, full), BF16)],
+        moved=3_000_000,
+        name="node_weights",
+    )
     partial_f_got = swap_lat(partial_f_sent)
     partial_l_got = swap_lat(partial_l_sent)
 
     edge_out_got = swap_lat(jnp.concatenate([fine_sent, long_sent], 0))
     rows_pair, rows_own = 4 * half + far_rows, 7 * half + far_rows
 
-    (node_output, node_self, keep_own, send_own, keep_pair, send_pair, dpre, near_sum, recv_sum) = call(
+    node_output, node_self, keep_pair, send_pair, keep_own, send_own, dpre, near_sum, recv_sum = call(
         back_kernel,
         info,
-        (partial_f, partial_f_got, partial_l, partial_l_got, n_hbm, node_got, ng_hbm, node_got, low, high, nin, nout,
+        (partial_f, partial_f_got, partial_l, partial_l_got, n_hbm, x_got, ng_hbm, g_got, low, high, rims_got, nin, nout,
          x_hbm, x_hbm, x_got, x_got, g_hbm, g_hbm, g_got, g_got,
          slope_f, slope_l, act_f, act_l, normed_f, normed_l, inverse_f, inverse_l, srow_l,
          idx_cf, idx_cl, idx_rf, idx_rl, w_in, w_out),
         [
             whole((nodes, full)), whole((nodes, full)), whole((16, full)), whole((16, full)),
-            node_spec, whole((nodes, half)), node_spec, second_nodes,
-            rim, rim, whole((2, full, full)), wout_spec,
+            node_spec, got_nodes, node_spec, got_nodes,
+            rim, rim, whole((2 * HALO, half)), whole((2, full, full)), wout_spec,
             fine_own(), long_own(), fine_got(), long_got(), fine_own(), long_own(), fine_got(), long_got(),
             whole((fine, full)), whole((longs, full)), whole((fine, full)), whole((longs, full)),
             whole((fine, full)), whole((longs, full)), whole((fine, 1)), whole((longs, 1)),
@@ -578,27 +638,29 @@
         [
             ((nodes, half), BF16),
             ((nodes, half), F32),
+            ((rows_pair, half), BF16),
+            ((rows_pair, half), BF16),
             ((rows_own, half), BF16),
             ((rows_own, half), BF16),
-            ((rows_pair, half), BF16),
-            ((rows_pair, half), BF16),
             ((rows, full), BF16),
             ((extent, full), BF16),
             ((nodes, full), BF16),
         ],
         [
+            pltpu.VMEM((rows, full), BF16),
             pltpu.VMEM((nodes, full), BF16),
             pltpu.VMEM((nodes, full), BF16),
             pltpu.VMEM((nodes, full), BF16),
+            pltpu.VMEM((nodes, half), BF16),
             pltpu.VMEM((nodes, full), BF16),
-            pltpu.VMEM((rows, full), BF16),
-            pltpu.VMEM((extent, full), BF16),
+            pltpu.VMEM((extent, half), BF16),
+            pltpu.VMEM((extent, half), BF16),
         ],
         flops=8 * rows * full * full,
         moved=14_000_000,
         name="nodes_and_edges_backward",
-    )
-
+        limit=28,
+    )
     core_pair, core_own = swap_core(send_pair), swap_core(send_own)
     by_lat, by_other = call(
         lat_stage_kernel,
@@ -619,15 +681,17 @@
         (keep_own, core_own, swap_lat(by_lat), other_neighbour(by_other)),
         [whole((rows_own, half)), whole((rows_own, half)), whole((rows_pair // 2, half)), whole((rows_pair // 2, half))],
         [((chips, slot, LANES), BF16)],
+        [pltpu.VMEM((chips, slot, LANES), BF16), pltpu.SemaphoreType.DMA],
         moved=4_300_000,
         name="combine",
+        in_hbm=(0,),
     )
     arrived = chips_all_to_all(gathered)
 
     grads_own, grads_sent, rim_own, rim_sent = call(
         inputs_kernel,
         info,
-        (dpre, g_hbm, g_hbm, g_got, near_sum, recv_sum, w_in),
+        (pinned(dpre), g_hbm, g_hbm, g_got, pinned(near_sum), pinned(recv_sum), w_in),
         [
             whole((rows, full)), fine_own(), long_own(), whole((rows, half)),
             whole((extent, full)), whole((nodes, full)), win_spec,
@@ -644,8 +708,10 @@
         (fine_out, long_out, edge_out_got),
         [whole((fine, half)), whole((longs, half)), whole((rows, half))],
         [((edges, half), BF16)],
+        [pltpu.SemaphoreType.DMA((4,))],
         moved=1_600_000,
         name="edge_output_rows",
+        in_hbm=(0,),
     )
     (edge_grads,) = call(
         rows_kernel,
@@ -653,8 +719,10 @@
         (grads_own, grads_own, swap_lat(grads_sent)),
         [whole((fine, half)), block((longs, half), lambda i, s: (fine // longs, 0)), whole((rows, half))],
         [((edges, half), BF16)],
+        [pltpu.SemaphoreType.DMA((4,))],
         moved=1_600_000,
         name="edge_gradient_rows",
+        in_hbm=(0,),
     )
     summed = rim_own + swap_lat(rim_sent).astype(F32)
     to_low = shifted(summed[:HALO].astype(BF16), -1).astype(F32)
@@ -663,9 +731,16 @@
     weight_share, coarse_total = call(
         functools.partial(share_kernel, scale=1.0 / patches),
         info,
-        (arrived, edge_output, edge_grads, to_low, to_high),
-        [whole((chips, slot, LANES))] + [pl.BlockSpec(memory_space=pl.ANY)] * 4,
+        (arrived, pinned(edge_output), to_low, to_high),
+        [pl.BlockSpec(memory_space=pl.ANY), pl.BlockSpec(memory_space=pltpu.HBM)]
+        + [pl.BlockSpec(memory_space=pl.ANY)] * 2,
         [((chips, share, LANES), BF16), ((blocks * COARSE, LANES), F32)],
+        [
+            pltpu.VMEM((chips, slot, LANES), BF16),
+            pltpu.VMEM((chips, share, LANES), BF16),
+            pltpu.SemaphoreType.DMA,
+        ],
+        in_hbm=(0,),
         moved=2_200_000,
         name="share",
     )
@@ -677,7 +752,7 @@
     own_grads = own_grads.at[:HALO].add(to_high)
     own_grads = own_grads.at[:COARSE].add(coarse_share)
     node_grads = own_grads.astype(BF16)
-    mine = chips_all_to_all(weight_share)
+    mine = gated(info, chips_all_to_all(weight_share), (pinned(edge_grads), pinned(node_grads)), pltpu.HBM)
     mine = mine.reshape(blocks, total_rows // blocks, LANES)
     other = swap_core(mine)
     square = (half, full)
@@ -691,7 +766,7 @@
             scratch_shapes=[pltpu.VMEM((7,) + square, F32), pltpu.SemaphoreType.DMA((7,))],
         ),
         out_shape=[jax.ShapeDtypeStruct(shape, F32) for shape in ((3,) + square, square, (2,) + square, square)],
-        compiler_params=pltpu.CompilerParams(vmem_limit_bytes=VMEM_LIMIT),
+        compiler_params=pltpu.CompilerParams(vmem_limit_bytes=14 * MIB),
         cost_estimate=pl.CostEstimate(flops=0, bytes_accessed=6_000_000, transcendentals=0),
         name="results",
     )(info, mine, other)

time: 204 us -> 183 us (0.90)
  blocking collectives: 35.9 us -> 0 us
  starting transfers between devices: 56.4 us -> 64.9 us
  waiting for transfers between devices: 63.5 us -> 71 us
  local copies, waits for them, and re-layouts: 9.25 us -> 4.69 us
  Pallas kernels: 35.4 us -> 37.9 us
    all_to_all x1 -> x0, blocking collectives: 35.9 us -> none  [chips_all_to_all(): lax.all_to_all(value, 'patch', 0, 0, tiled=True, axis_index_groups=groups)]
    ppermute x4, waiting for transfers between devices: 25.5 us -> 3.63 us  [shifted(): lax.ppermute(value, 'patch', [(i, (i + steps) % count) for i in range(cou...]
    ppermute x9 -> x10, waiting for transfers between devices: 27 us -> 40.1 us  [swap_lat(): return lax.ppermute(value, 'lat', [(0, 1), (1, 0)])]
    ppermute x3, waiting for transfers between devices: 7.67 us -> 16.6 us  [other_neighbour(): return lax.ppermute(value, ('patch', 'lat'), pairs)]
    all_to_all x2 -> x3, starting transfers between devices: 24.3 us -> 32.9 us  [chips_all_to_all(): lax.all_to_all(value, 'patch', 0, 0, tiled=True, axis_index_groups=groups)]
    all_to_all x2 -> x3, waiting for transfers between devices: 0.01 us -> 6.78 us  [chips_all_to_all(): lax.all_to_all(value, 'patch', 0, 0, tiled=True, axis_index_groups=groups)]
    unnamed x46 -> x48, local copies, waits for them, and re-layouts: 8.22 us -> 3.69 us
    ppermute x4, starting transfers between devices: 8.56 us -> 11.4 us  [shifted(): lax.ppermute(value, 'patch', [(i, (i + steps) % count) for i in range(cou...]
  transfers between devices with their start and end apart: 24 -> 26, of which waited for: 10 -> 15; matrix products, arithmetic and copies ran while one was open for 1% -> 1% of each run, Pallas kernels for 10% -> 12%
where the time goes in v4:
time: 183 us; the launch traced here: 182 us
  waiting for transfers between devices  71 us (39%)
  starting transfers between devices  64.9 us (35%)
  Pallas kernels  37.9 us (21%)
  local copies, waits for them, and re-layouts  4.69 us (3%)
  between operations  1.87 us (1%)
    ppermute x10, waiting for transfers between devices, swap_lat(): return lax.ppermute(value, 'lat', [(0, 1), (1, 0)])  40.1 us
    pallas_call x13, Pallas kernels, call(): pl.pallas_call(kernel, grid_spec=pltpu.PrefetchScalarGridSpec(num_scalar_...  34.3 us
    all_to_all x3, starting transfers between devices, chips_all_to_all(): lax.all_to_all(value, 'patch', 0, 0, tiled=True, axis_index_groups=groups)  32.9 us
    ppermute x3, waiting for transfers between devices, other_neighbour(): return lax.ppermute(value, ('patch', 'lat'), pairs)  16.6 us
    ppermute x4, starting transfers between devices, shifted(): lax.ppermute(value, 'patch', [(i, (i + steps) % count) for i in range(cou...  11.4 us
    ppermute x6, starting transfers between devices, swap_core(): return lax.ppermute(value, 'patch', [(i, i ^ 1) for i in range(count)])  9.92 us
    all_to_all x3, waiting for transfers between devices, chips_all_to_all(): lax.all_to_all(value, 'patch', 0, 0, tiled=True, axis_index_groups=groups)  6.78 us
    ppermute x10, starting transfers between devices, swap_lat(): return lax.ppermute(value, 'lat', [(0, 1), (1, 0)])  6.15 us
  transfers between devices with their start and end apart: 26, of which 15 were waited for; matrix products, arithmetic and copies ran while one was open for 1% of the time, Pallas kernels for 12%

profile of v4, /device:TPU:1, one launch (start us, length us, event | category | flops | bytes accessed | tf_op | source)
XLA Modules:
  0.0 182.1 jit_solution(14834245418889160815)
XLA Ops:
  1.3 2.0 %collective-permute-start.6 = (bf16[16,256]{1,0:T(8,128)(2,1)S(1)}, bf16[16,256]{1,0:T(8,128)(2,1)S(1)}, u32[]{:S(2)}, u32[]{:S(2)}) collective-permute-start(bf16[16,256]{1,0:T(8,128)(2,1)S(1)} %slice.78), channel_id=1, source_target_pairs={{0,1},{1,0},{2,3},{3,2},{4,5},{5,4},{6,7},{7,6},{8,9},{9,8},{10,11... | collective-permute-start | bytes 24584 | tf_op jit(solution)/shard_map/ppermute | solution.py:59
  3.4 2.6 %pack.1 = (bf16[960,256]{1,0:T(8,128)(2,1)}, bf16[4,128,512]{2,1,0:T(8,128)(2,1)S(1)}, bf16[32,256]{1,0:T(8,128)(2,1)S(1)}, bf16[32,256]{1,0:T(8,128)(2,1)S(1)}) custom-call(s32[2]{0:T(128)S(1)} %pad_add_fusion.2.info, bf16[1536,256]{1,0:T(8,128)(2,1)} %xl_own.1, bf16[1536,256]{1,0:T(8,128)(2,1)} %xl_own.1, bf16[192,256]{1,0:T(8,128)(2,1)} %n_own.7, ...), custom_call_target="tpu_custom_call" | custom-call | bytes 3000000 | tf_op jit(solution)/shard_map/pack/pallas_call | solution.py:96
  6.0 2.1 %coarse_rows.1 = bf16[64,8,512]{2,1,0:T(8,128)(2,1)} custom-call(s32[2]{0:T(128)S(1)} %pad_add_fusion.2.info, bf16[192,256]{1,0:T(8,128)(2,1)} %n_own.7, bf16[16,256]{1,0:T(8,128)(2,1)S(1)} %collective-permute-done.6.n_got, bf16[32,256]{1,0:T(8,128)(2,1)S(1)} %get-tuple-element.94.after), custom_call_target="tpu_custom_call" | custom-call | bytes 600000 | tf_op jit(solution)/shard_map/coarse_rows/pallas_call | solution.py:96
  8.1 14.0 %all-to-all-start = ((bf16[64,8,512]{2,1,0:T(8,128)(2,1)}), bf16[64,8,512]{2,1,0:T(8,128)(2,1)S(1)}, u32[]{:S(2)}, u32[]{:S(2)}) async-start(bf16[64,8,512]{2,1,0:T(8,128)(2,1)} %coarse_rows.1), calls=%async_computation | async-start | bytes 1048576 | tf_op jit(solution)/shard_map/all_to_all | solution.py:84
  22.1 2.0 %collective-permute-start.4 = (bf16[4,128,512]{2,1,0:T(8,128)(2,1)S(1)}, bf16[4,128,512]{2,1,0:T(8,128)(2,1)S(1)}, u32[]{:S(2)}, u32[]{:S(2)}) collective-permute-start(bf16[4,128,512]{2,1,0:T(8,128)(2,1)S(1)} %get-tuple-element.95), channel_id=1, source_target_pairs={{0,5},{1,4},{2,7},{3,6},{4,1},{5,0},{6,3},{7,2},{8,13},{9,12},{10,... | collective-permute-start | bytes 1572872 | tf_op jit(solution)/shard_map/ppermute | solution.py:78
  24.1 2.0 %collective-permute-start.2 = (bf16[32,256]{1,0:T(8,128)(2,1)S(1)}, bf16[32,256]{1,0:T(8,128)(2,1)S(1)}, u32[]{:S(2)}, u32[]{:S(2)}) collective-permute-start(bf16[32,256]{1,0:T(8,128)(2,1)S(1)} %get-tuple-element.94.after), channel_id=1, source_target_pairs={{0,254},{2,0},{4,2},{6,4},{8,6},{10,8},{12,10},{14,12},{16,14},{18... | collective-permute-start | bytes 49160 | tf_op jit(solution)/shard_map/ppermute | solution.py:69
  27.8 13.9 %collective-permute-done.4.got = bf16[4,128,512]{2,1,0:T(8,128)(2,1)S(1)} collective-permute-done((bf16[4,128,512]{2,1,0:T(8,128)(2,1)S(1)}, bf16[4,128,512]{2,1,0:T(8,128)(2,1)S(1)}, u32[]{:S(2)}, u32[]{:S(2)}) %collective-permute-start.4) | collective-permute-done | bytes 524320 | tf_op jit(solution)/shard_map/ppermute | solution.py:78
  41.7 1.7 collective-permute-start.5
  45.9 2.4 %collective-permute-done.3.after.rims_got = bf16[64,256]{1,0:T(8,128)(2,1)S(1)} collective-permute-done((bf16[64,256]{1,0:T(8,128)(2,1)S(1)}, bf16[64,256]{1,0:T(8,128)(2,1)S(1)}, u32[]{:S(2)}, u32[]{:S(2)}) %collective-permute-start.3) | collective-permute-done | bytes 32800 | tf_op jit(solution)/shard_map/ppermute | solution.py:59
  48.3 2.6 %edge_weights.1 = (bf16[3,512,512]{2,1,0:T(8,128)(2,1)S(1)}, bf16[512,512]{1,0:T(8,128)(2,1)S(1)}, bf16[960,256]{1,0:T(8,128)(2,1)S(1)}, bf16[3,128,512]{2,1,0:T(8,128)(2,1)S(1)}) custom-call(s32[2]{0:T(128)S(1)} %pad_add_fusion.2.info, bf16[3,256,512]{2,1,0:T(8,128)(2,1)} %wi.4, bf16[256,512]{1,0:T(8,128)(2,1)} %wo.4, bf16[4,128,512]{2,1,0:T(8,128)(2,1)} %copy-done.21, ...), custom_call_target="tpu_custom_call" | custom-call | bytes 7000000 | tf_op jit(solution)/shard_map/edge_weights/pallas_call | solution.py:96
  52.2 4.4 %edges_forward_fine.1 = (f32[576,512]{1,0:T(8,128)S(1)}, bf16[576,512]{1,0:T(8,128)(2,1)S(1)}, f32[576,512]{1,0:T(8,128)S(1)}, f32[576,1]{1,0:T(8,128)S(1)}, bf1...) custom-call(s32[2]{0:T(128)S(1)} %pad_add_fusion.2.info, ...), custom_call_target="tpu_custom_call" | custom-call | flops 1585446912 | bytes 8000000 | tf_op jit(solution)/shard_map/edges_forward_fine/pallas_call | solution.py:96
  56.7 2.9 %edges_forward_long.1 = (f32[192,512]{1,0:T(8,128)S(1)}, bf16[192,512]{1,0:T(8,128)(2,1)S(1)}, f32[192,512]{1,0:T(8,128)S(1)}, f32[192,1]{1,0:T(8,128)S(1)}, bf1...) custom-call(s32[2]{0:T(128)S(1)} %pad_add_fusion.2.info, ...), custom_call_target="tpu_custom_call" | custom-call | flops 1283457024 | bytes 6000000 | tf_op jit(solution)/shard_map/edges_forward_long/pallas_call | solution.py:96
  61.7 2.6 %collective-permute-start.13 = (bf16[3,128,512]{2,1,0:T(8,128)(2,1)S(1)}, bf16[3,128,512]{2,1,0:T(8,128)(2,1)S(1)}, u32[]{:S(2)}, u32[]{:S(2)}) collective-permute-start(bf16[3,128,512]{2,1,0:T(8,128)(2,1)S(1)} %gate.2.got), channel_id=1, source_target_pairs={{0,2},{2,0},{4,6},{6,4},{8,10},{10,8},{12,14},{14,12},{16,18},{18,... | collective-permute-start | bytes 1179656 | tf_op jit(solution)/shard_map/ppermute | solution.py:64
  65.9 1.8 %node_weights.1 = (bf16[2,512,512]{2,1,0:T(8,128)(2,1)S(1)}, bf16[512,512]{1,0:T(8,128)(2,1)S(1)}) custom-call(s32[2]{0:T(128)S(1)} %pad_add_fusion.2.info, bf16[2,256,512]{2,1,0:T(8,128)(2,1)} %wi.5, bf16[256,512]{1,0:T(8,128)(2,1)} %wo.5, bf16[3,128,512]{2,1,0:T(8,128)(2,1)S(1)} %gate.2.got, bf16[3,128,512]{2,1,0:T(8,128)(2,1)S(1)} %collective-permute-done.13.again), custom_call_target="tpu_custom_call" | custom-call | bytes 3000000 | tf_op jit(solution)/shard_map/node_weights/pallas_call | solution.py:96
  67.7 3.1 %collective-permute-done.9.got = bf16[192,512]{1,0:T(8,128)(2,1)S(1)} collective-permute-done((bf16[192,512]{1,0:T(8,128)(2,1)S(1)}, bf16[192,512]{1,0:T(8,128)(2,1)S(1)}, u32[]{:S(2)}, u32[]{:S(2)}) %collective-permute-start.9) | collective-permute-done | bytes 196640 | tf_op jit(solution)/shard_map/ppermute | solution.py:59
  71.2 8.3 %nodes_and_edges_backward.1 = (bf16[192,256]{1,0:T(8,128)(2,1)}, f32[192,256]{1,0:T(8,128)S(1)}, bf16[1536,256]{1,0:T(8,128)(2,1)S(1)}, bf16[1536,256]{1,0:T(8,1...) custom-call(s32[2]{0:T(128)S(1)} %pad_add_fusion.2.info, ...), custom_call_target="tpu_custom_call" | custom-call | flops 1610612736 | bytes 14000000 | tf_op jit(solution)/shard_map/nodes_and_edges_backward/pallas_call | solution.py:96
  80.5 1.8 collective-permute-done.19.got
  84.4 9.0 %collective-permute-done.20.first = bf16[768,256]{1,0:T(8,128)(2,1)S(1)} collective-permute-done((bf16[768,256]{1,0:T(8,128)(2,1)S(1)}, bf16[768,256]{1,0:T(8,128)(2,1)S(1)}, u32[]{:S(2)}, u32[]{:S(2)}) %collective-permute-start.20) | collective-permute-done | bytes 393248 | tf_op jit(solution)/shard_map/ppermute | solution.py:59
  94.6 2.0 %combine.1 = bf16[64,72,128]{2,1,0:T(8,128)(2,1)} custom-call(s32[2]{0:T(128)S(1)} %pad_add_fusion.2.info, bf16[2304,256]{1,0:T(8,128)(2,1)S(1)} %get-tuple-element.128.keep, bf16[2304,256]{1,0:T(8,128)(2,1)S(1)} %collective-permute-done.18.got, bf16[768,256]{1,0:T(8,128)(2,1)S(1)} %collective-permute-done.20.first, ...), custom_call_target="tpu_custom_call" | custom-call | bytes 4300000 | tf_op jit(solution)/shard_map/combine/pallas_call | solution.py:96
  96.6 10.0 %all-to-all-start.1 = ((bf16[64,72,128]{2,1,0:T(8,128)(2,1)}), bf16[64,72,128]{2,1,0:T(8,128)(2,1)S(1)}, u32[]{:S(2)}, u32[]{:S(2)}) async-start(bf16[64,72,128]{2,1,0:T(8,128)(2,1)} %combine.1), calls=%async_computation.1 | async-start | bytes 2359296 | tf_op jit(solution)/shard_map/all_to_all | solution.py:84
  106.6 2.8 %input_gradients.1 = (bf16[768,256]{1,0:T(8,128)(2,1)S(1)}, bf16[768,256]{1,0:T(8,128)(2,1)S(1)}, f32[256,256]{1,0:T(8,128)S(1)}, bf16[256,256]{1,0:T(8,128)(2,1)S(1)}) custom-call(s32[2]{0:T(128)S(1)} %pad_add_fusion.2.info, bf16[768,512]{1,0:T(8,128)(2,1)} %copy-done.3, bf16[1536,256]{1,0:T(8,128)(2,1)} %gl_own.3, bf16[1536,256]{1,0:T(8,128)(2,1)} %gl_own.3, ...), custom_call_target="tpu_custom_call" | custom-call | flops 805306368 | bytes 5000000 | tf_op jit(solution)/shard_map/input_gradients/pallas_call | solution.py:96
  112.5 3.4 %collective-permute-done.15 = bf16[256,256]{1,0:T(8,128)(2,1)S(1)} collective-permute-done((bf16[256,256]{1,0:T(8,128)(2,1)S(1)}, bf16[256,256]{1,0:T(8,128)(2,1)S(1)}, u32[]{:S(2)}, u32[]{:S(2)}) %collective-permute-start.15) | collective-permute-done | bytes 131104 | tf_op jit(solution)/shard_map/ppermute | solution.py:59
  116.7 5.4 %collective-permute-start.16 = (bf16[32,256]{1,0:T(8,128)(2,1)S(1)}, bf16[32,256]{1,0:T(8,128)(2,1)S(1)}, u32[]{:S(2)}, u32[]{:S(2)}) collective-permute-start(bf16[32,256]{1,0:T(8,128)(2,1)S(1)} %get-tuple-element.145), channel_id=1, source_target_pairs={{0,254},{2,0},{4,2},{6,4},{8,6},{10,8},{12,10},{14,12},{16,14},{18... | collective-permute-start | bytes 49160 | tf_op jit(solution)/shard_map/ppermute | solution.py:69
  122.1 2.8 %collective-permute-start.17 = (bf16[32,256]{1,0:T(8,128)(2,1)S(1)}, bf16[32,256]{1,0:T(8,128)(2,1)S(1)}, u32[]{:S(2)}, u32[]{:S(2)}) collective-permute-start(bf16[32,256]{1,0:T(8,128)(2,1)S(1)} %get-tuple-element.144), channel_id=1, source_target_pairs={{0,2},{2,4},{4,6},{6,8},{8,10},{10,12},{12,14},{14,16},{16,18},{18... | collective-permute-start | bytes 49160 | tf_op jit(solution)/shard_map/ppermute | solution.py:69
  124.9 6.6 %collective-permute-done.8.got = bf16[768,256]{1,0:T(8,128)(2,1)S(1)} collective-permute-done((bf16[768,256]{1,0:T(8,128)(2,1)S(1)}, bf16[768,256]{1,0:T(8,128)(2,1)S(1)}, u32[]{:S(2)}, u32[]{:S(2)}) %collective-permute-start.8) | collective-permute-done | bytes 393248 | tf_op jit(solution)/shard_map/ppermute | solution.py:59
  132.9 3.6 %collective-permute-done.16 = bf16[32,256]{1,0:T(8,128)(2,1)S(1)} collective-permute-done((bf16[32,256]{1,0:T(8,128)(2,1)S(1)}, bf16[32,256]{1,0:T(8,128)(2,1)S(1)}, u32[]{:S(2)}, u32[]{:S(2)}) %collective-permute-start.16) | collective-permute-done | bytes 16416 | tf_op jit(solution)/shard_map/ppermute | solution.py:69
  139.2 8.9 %all-to-all-start.2 = ((bf16[64,56,128]{2,1,0:T(8,128)(2,1)}), bf16[64,56,128]{2,1,0:T(8,128)(2,1)S(1)}, u32[]{:S(2)}, u32[]{:S(2)}) async-start(bf16[64,56,128]{2,1,0:T(8,128)(2,1)} %copy-done.2), calls=%async_computation.2 | async-start | bytes 1835008 | tf_op jit(solution)/shard_map/all_to_all | solution.py:84
  148.9 15.1 %collective-permute-done.14.got = bf16[768,256]{1,0:T(8,128)(2,1)S(1)} collective-permute-done((bf16[768,256]{1,0:T(8,128)(2,1)S(1)}, bf16[768,256]{1,0:T(8,128)(2,1)S(1)}, u32[]{:S(2)}, u32[]{:S(2)}) %collective-permute-start.14) | collective-permute-done | bytes 393248 | tf_op jit(solution)/shard_map/ppermute | solution.py:59
  166.1 6.3 %all-to-all-done.2.value = bf16[64,56,128]{2,1,0:T(8,128)(2,1)S(1)} async-done(((bf16[64,56,128]{2,1,0:T(8,128)(2,1)}), bf16[64,56,128]{2,1,0:T(8,128)(2,1)S(1)}, u32[]{:S(2)}, u32[]{:S(2)}) %all-to-all-start.2) | async-done | bytes 917536 | tf_op jit(solution)/shard_map/all_to_all | solution.py:84
  173.0 4.4 %collective-permute-start.22 = (bf16[2,1792,128]{2,1,0:T(8,128)(2,1)S(1)}, bf16[2,1792,128]{2,1,0:T(8,128)(2,1)S(1)}, u32[]{:S(2)}, u32[]{:S(2)}) collective-permute-start(bf16[2,1792,128]{2,1,0:T(8,128)(2,1)S(1)} %bitcast.15), channel_id=1, source_target_pairs={{0,2},{2,0},{4,6},{6,4},{8,10},{10,8},{12,14},{14,12},{16,18},{18,... | collective-permute-start | bytes 2752520 | tf_op jit(solution)/shard_map/ppermute | solution.py:64
  177.4 2.1 %collective-permute-done.22.other = bf16[2,1792,128]{2,1,0:T(8,128)(2,1)S(1)} collective-permute-done((bf16[2,1792,128]{2,1,0:T(8,128)(2,1)S(1)}, bf16[2,1792,128]{2,1,0:T(8,128)(2,1)S(1)}, u32[]{:S(2)}, u32[]{:S(2)}) %collective-permute-start.22) | collective-permute-done | bytes 917536 | tf_op jit(solution)/shard_map/ppermute | solution.py:64
  179.5 2.5 %results.1 = (f32[3,256,512]{2,1,0:T(8,128)}, f32[256,512]{1,0:T(8,128)}, f32[2,256,512]{2,1,0:T(8,128)}, f32[256,512]{1,0:T(8,128)}) custom-call(s32[2]{0:T(128)S(1)} %pad_add_fusion.2.info, bf16[2,1792,128]{2,1,0:T(8,128)(2,1)S(1)} %bitcast.16, bf16[2,1792,128]{2,1,0:T(8,128)(2,1)S(1)} %collective-permute-done.22.other), custom_call_target="tpu_custom_call" | custom-call | bytes 6000000 | tf_op jit(solution)/shard_map/results/pallas_call | solution.py:759
  (107 shorter events, 25.0 us)
Async XLA Ops:
  1.3 4.7 %collective-permute-start.6 = (bf16[16,256]{1,0:T(8,128)(2,1)S(1)}, bf16[16,256]{1,0:T(8,128)(2,1)S(1)}, u32[]{:S(2)}, u32[]{:S(2)}) collective-permute-start(bf16[16,256]{1,0:T(8,128)(2,1)S(1)} %slice.78), channel_id=1, source_target_pairs={{0,1},{1,0},{2,3},{3,2},{4,5},{5,4},{6,7},{7,6},{8,9},{9,8},{10,11... | collective-permute-start | bytes 24584 | tf_op jit(solution)/shard_map/ppermute | solution.py:59
  6.0 21.6 %copy-start.22 = (s32[12,128]{1,0:T(8,128)S(1)}, s32[12,128]{1,0:T(8,128)}, u32[]{:S(2)}) copy-start(s32[12,128]{1,0:T(8,128)} %param.19) | copy-start | bytes 18436
  6.0 21.6 %copy-start.23 = (s32[12,128]{1,0:T(8,128)S(1)}, s32[12,128]{1,0:T(8,128)}, u32[]{:S(2)}) copy-start(s32[12,128]{1,0:T(8,128)} %param.20) | copy-start | bytes 18436
  8.1 36.0 %all-to-all-start = ((bf16[64,8,512]{2,1,0:T(8,128)(2,1)}), bf16[64,8,512]{2,1,0:T(8,128)(2,1)S(1)}, u32[]{:S(2)}, u32[]{:S(2)}) async-start(bf16[64,8,512]{2,1,0:T(8,128)(2,1)} %coarse_rows.1), calls=%async_computation | async-start | bytes 1048576 | tf_op jit(solution)/shard_map/all_to_all | solution.py:84
  22.1 19.6 %collective-permute-start.4 = (bf16[4,128,512]{2,1,0:T(8,128)(2,1)S(1)}, bf16[4,128,512]{2,1,0:T(8,128)(2,1)S(1)}, u32[]{:S(2)}, u32[]{:S(2)}) collective-permute-start(bf16[4,128,512]{2,1,0:T(8,128)(2,1)S(1)} %get-tuple-element.95), channel_id=1, source_target_pairs={{0,5},{1,4},{2,7},{3,6},{4,1},{5,0},{6,3},{7,2},{8,13},{9,12},{10,... | collective-permute-start | bytes 1572872 | tf_op jit(solution)/shard_map/ppermute | solution.py:78
  24.1 20.2 %collective-permute-start.2 = (bf16[32,256]{1,0:T(8,128)(2,1)S(1)}, bf16[32,256]{1,0:T(8,128)(2,1)S(1)}, u32[]{:S(2)}, u32[]{:S(2)}) collective-permute-start(bf16[32,256]{1,0:T(8,128)(2,1)S(1)} %get-tuple-element.94.after), channel_id=1, source_target_pairs={{0,254},{2,0},{4,2},{6,4},{8,6},{10,8},{12,10},{14,12},{16,14},{18... | collective-permute-start | bytes 49160 | tf_op jit(solution)/shard_map/ppermute | solution.py:69
  26.0 18.2 %collective-permute-start.1 = (bf16[32,256]{1,0:T(8,128)(2,1)S(1)}, bf16[32,256]{1,0:T(8,128)(2,1)S(1)}, u32[]{:S(2)}, u32[]{:S(2)}) collective-permute-start(bf16[32,256]{1,0:T(8,128)(2,1)S(1)} %get-tuple-element.93), channel_id=1, source_target_pairs={{0,2},{2,4},{4,6},{6,8},{8,10},{10,12},{12,14},{14,16},{16,18},{18... | collective-permute-start | bytes 49160 | tf_op jit(solution)/shard_map/ppermute | solution.py:69
  27.3 24.8 %collective-permute-start = (bf16[960,256]{1,0:T(8,128)(2,1)}, bf16[960,256]{1,0:T(8,128)(2,1)}, u32[]{:S(2)}, u32[]{:S(2)}) collective-permute-start(bf16[960,256]{1,0:T(8,128)(2,1)} %get-tuple-element.92), channel_id=1, source_target_pairs={{0,1},{1,0},{2,3},{3,2},{4,5},{5,4},{6,7},{7,6},{8,9},{9,8},{10,11... | collective-permute-start | bytes 1474568 | tf_op jit(solution)/shard_map/ppermute | solution.py:59
  41.7 6.6 %collective-permute-start.5 = (bf16[4,128,512]{2,1,0:T(8,128)(2,1)S(1)}, bf16[4,128,512]{2,1,0:T(8,128)(2,1)}, u32[]{:S(2)}, u32[]{:S(2)}) collective-permute-start(bf16[4,128,512]{2,1,0:T(8,128)(2,1)S(1)} %collective-permute-done.4.got), channel_id=1, source_target_pairs={{0,2},{2,0},{4,6},{6,4},{8,10},{10,8},{12,14},{14,12},{16,18},{18,... | collective-permute-start | bytes 1572872 | tf_op jit(solution)/shard_map/ppermute | solution.py:64
  44.2 12.5 %collective-permute-start.7 = (bf16[64,8,512]{2,1,0:T(8,128)(2,1)S(1)}, bf16[64,8,512]{2,1,0:T(8,128)(2,1)S(1)}, u32[]{:S(2)}, u32[]{:S(2)}) collective-permute-start(bf16[64,8,512]{2,1,0:T(8,128)(2,1)S(1)} %all-to-all-done), channel_id=1, source_target_pairs={{0,2},{2,0},{4,6},{6,4},{8,10},{10,8},{12,14},{14,12},{16,18},{18,... | collective-permute-start | bytes 1572872 | tf_op jit(solution)/shard_map/ppermute | solution.py:64
  45.5 2.8 %collective-permute-start.3 = (bf16[64,256]{1,0:T(8,128)(2,1)S(1)}, bf16[64,256]{1,0:T(8,128)(2,1)S(1)}, u32[]{:S(2)}, u32[]{:S(2)}) collective-permute-start(bf16[64,256]{1,0:T(8,128)(2,1)S(1)} %pad_maximum_fusion.1), channel_id=1, source_target_pairs={{0,1},{1,0},{2,3},{3,2},{4,5},{5,4},{6,7},{7,6},{8,9},{9,8},{10,11... | collective-permute-start | bytes 98312 | tf_op jit(solution)/shard_map/ppermute | solution.py:59
  50.9 10.3 %collective-permute-start.12 = (bf16[3,128,512]{2,1,0:T(8,128)(2,1)S(1)}, bf16[3,128,512]{2,1,0:T(8,128)(2,1)S(1)}, u32[]{:S(2)}, u32[]{:S(2)}) collective-permute-start(bf16[3,128,512]{2,1,0:T(8,128)(2,1)S(1)} %get-tuple-element.107), channel_id=1, source_target_pairs={{0,5},{1,4},{2,7},{3,6},{4,1},{5,0},{6,3},{7,2},{8,13},{9,12},{10,... | collective-permute-start | bytes 1179656 | tf_op jit(solution)/shard_map/ppermute | solution.py:78
  52.2 18.7 %collective-permute-start.11 = (bf16[960,256]{1,0:T(8,128)(2,1)S(1)}, bf16[960,256]{1,0:T(8,128)(2,1)S(1)}, u32[]{:S(2)}, u32[]{:S(2)}) collective-permute-start(bf16[960,256]{1,0:T(8,128)(2,1)S(1)} %get-tuple-element.106), channel_id=1, source_target_pairs={{0,1},{1,0},{2,3},{3,2},{4,5},{5,4},{6,7},{7,6},{8,9},{9,8},{10,11... | collective-permute-start | bytes 1474568 | tf_op jit(solution)/shard_map/ppermute | solution.py:59
  61.7 4.1 %collective-permute-start.13 = (bf16[3,128,512]{2,1,0:T(8,128)(2,1)S(1)}, bf16[3,128,512]{2,1,0:T(8,128)(2,1)S(1)}, u32[]{:S(2)}, u32[]{:S(2)}) collective-permute-start(bf16[3,128,512]{2,1,0:T(8,128)(2,1)S(1)} %gate.2.got), channel_id=1, source_target_pairs={{0,2},{2,0},{4,6},{6,4},{8,10},{10,8},{12,14},{14,12},{16,18},{18,... | collective-permute-start | bytes 1179656 | tf_op jit(solution)/shard_map/ppermute | solution.py:64
  64.4 6.5 %collective-permute-start.9 = (bf16[192,512]{1,0:T(8,128)(2,1)S(1)}, bf16[192,512]{1,0:T(8,128)(2,1)S(1)}, u32[]{:S(2)}, u32[]{:S(2)}) collective-permute-start(bf16[192,512]{1,0:T(8,128)(2,1)S(1)} %get-tuple-element.103.rest_1_), channel_id=1, source_target_pairs={{0,1},{1,0},{2,3},{3,2},{4,5},{5,4},{6,7},{7,6},{8,9},{9,8},{10,11... | collective-permute-start | bytes 589832 | tf_op jit(solution)/shard_map/ppermute | solution.py:59
  64.4 6.8 %collective-permute-start.10 = (bf16[16,512]{1,0:T(8,128)(2,1)S(1)}, bf16[16,512]{1,0:T(8,128)(2,1)S(1)}, u32[]{:S(2)}, u32[]{:S(2)}) collective-permute-start(bf16[16,512]{1,0:T(8,128)(2,1)S(1)} %get-tuple-element.105.rest_0_), channel_id=1, source_target_pairs={{0,1},{1,0},{2,3},{3,2},{4,5},{5,4},{6,7},{7,6},{8,9},{9,8},{10,11... | collective-permute-start | bytes 49160 | tf_op jit(solution)/shard_map/ppermute | solution.py:59
  79.4 15.2 %copy-start.9 = (bf16[192,512]{1,0:T(8,128)(2,1)}, bf16[192,512]{1,0:T(8,128)(2,1)S(1)}, u32[]{:S(2)}) copy-start(bf16[192,512]{1,0:T(8,128)(2,1)S(1)} %get-tuple-element.122.recv_sum) | copy-start | bytes 589828
  79.4 2.9 %collective-permute-start.19 = (bf16[1536,256]{1,0:T(8,128)(2,1)S(1)}, bf16[1536,256]{1,0:T(8,128)(2,1)S(1)}, u32[]{:S(2)}, u32[]{:S(2)}) collective-permute-start(bf16[1536,256]{1,0:T(8,128)(2,1)S(1)} %get-tuple-element.131), channel_id=1, source_target_pairs={{0,2},{2,0},{4,6},{6,4},{8,10},{10,8},{12,14},{14,12},{16,18},{18,... | collective-permute-start | bytes 2359304 | tf_op jit(solution)/shard_map/ppermute | solution.py:64
  80.4 14.2 %collective-permute-start.18 = (bf16[2304,256]{1,0:T(8,128)(2,1)S(1)}, bf16[2304,256]{1,0:T(8,128)(2,1)S(1)}, u32[]{:S(2)}, u32[]{:S(2)}) collective-permute-start(bf16[2304,256]{1,0:T(8,128)(2,1)S(1)} %get-tuple-element.129), channel_id=1, source_target_pairs={{0,2},{2,0},{4,6},{6,4},{8,10},{10,8},{12,14},{14,12},{16,18},{18,... | collective-permute-start | bytes 3538952 | tf_op jit(solution)/shard_map/ppermute | solution.py:64
  83.1 10.4 %collective-permute-start.20 = (bf16[768,256]{1,0:T(8,128)(2,1)S(1)}, bf16[768,256]{1,0:T(8,128)(2,1)S(1)}, u32[]{:S(2)}, u32[]{:S(2)}) collective-permute-start(bf16[768,256]{1,0:T(8,128)(2,1)S(1)} %get-tuple-element.132), channel_id=1, source_target_pairs={{0,1},{1,0},{2,3},{3,2},{4,5},{5,4},{6,7},{7,6},{8,9},{9,8},{10,11... | collective-permute-start | bytes 1179656 | tf_op jit(solution)/shard_map/ppermute | solution.py:59
  83.2 11.4 %collective-permute-start.21 = (bf16[768,256]{1,0:T(8,128)(2,1)S(1)}, bf16[768,256]{1,0:T(8,128)(2,1)S(1)}, u32[]{:S(2)}, u32[]{:S(2)}) collective-permute-start(bf16[768,256]{1,0:T(8,128)(2,1)S(1)} %get-tuple-element.133), channel_id=1, source_target_pairs={{0,5},{1,4},{2,7},{3,6},{4,1},{5,0},{6,3},{7,2},{8,13},{9,12},{10,... | collective-permute-start | bytes 1179656 | tf_op jit(solution)/shard_map/ppermute | solution.py:78
  96.6 40.5 %all-to-all-start.1 = ((bf16[64,72,128]{2,1,0:T(8,128)(2,1)}), bf16[64,72,128]{2,1,0:T(8,128)(2,1)S(1)}, u32[]{:S(2)}, u32[]{:S(2)}) async-start(bf16[64,72,128]{2,1,0:T(8,128)(2,1)} %combine.1), calls=%async_computation.1 | async-start | bytes 2359296 | tf_op jit(solution)/shard_map/all_to_all | solution.py:84
  110.9 20.5 %copy-start.7 = (bf16[576,256]{1,0:T(8,128)(2,1)S(1)}, bf16[576,256]{1,0:T(8,128)(2,1)}, u32[]{:S(2)}) copy-start(bf16[576,256]{1,0:T(8,128)(2,1)} %copy-done.6) | copy-start | bytes 884740
  110.9 20.5 %copy-start.11 = (bf16[192,256]{1,0:T(8,128)(2,1)S(1)}, bf16[192,256]{1,0:T(8,128)(2,1)}, u32[]{:S(2)}) copy-start(bf16[192,256]{1,0:T(8,128)(2,1)} %copy-done.10) | copy-start | bytes 294916
  110.9 5.0 %collective-permute-start.15 = (bf16[256,256]{1,0:T(8,128)(2,1)S(1)}, bf16[256,256]{1,0:T(8,128)(2,1)S(1)}, u32[]{:S(2)}, u32[]{:S(2)}) collective-permute-start(bf16[256,256]{1,0:T(8,128)(2,1)S(1)} %get-tuple-element.127), channel_id=1, source_target_pairs={{0,1},{1,0},{2,3},{3,2},{4,5},{5,4},{6,7},{7,6},{8,9},{9,8},{10,11... | collective-permute-start | bytes 393224 | tf_op jit(solution)/shard_map/ppermute | solution.py:59
  112.0 19.5 %collective-permute-start.8 = (bf16[768,256]{1,0:T(8,128)(2,1)S(1)}, bf16[768,256]{1,0:T(8,128)(2,1)S(1)}, u32[]{:S(2)}, u32[]{:S(2)}) collective-permute-start(bf16[768,256]{1,0:T(8,128)(2,1)S(1)} %pad_maximum_fusion), channel_id=1, source_target_pairs={{0,1},{1,0},{2,3},{3,2},{4,5},{5,4},{6,7},{7,6},{8,9},{9,8},{10,11... | collective-permute-start | bytes 1179656 | tf_op jit(solution)/shard_map/ppermute | solution.py:59
  116.7 19.9 %collective-permute-start.16 = (bf16[32,256]{1,0:T(8,128)(2,1)S(1)}, bf16[32,256]{1,0:T(8,128)(2,1)S(1)}, u32[]{:S(2)}, u32[]{:S(2)}) collective-permute-start(bf16[32,256]{1,0:T(8,128)(2,1)S(1)} %get-tuple-element.145), channel_id=1, source_target_pairs={{0,254},{2,0},{4,2},{6,4},{8,6},{10,8},{12,10},{14,12},{16,14},{18... | collective-permute-start | bytes 49160 | tf_op jit(solution)/shard_map/ppermute | solution.py:69
  122.1 14.4 %collective-permute-start.17 = (bf16[32,256]{1,0:T(8,128)(2,1)S(1)}, bf16[32,256]{1,0:T(8,128)(2,1)S(1)}, u32[]{:S(2)}, u32[]{:S(2)}) collective-permute-start(bf16[32,256]{1,0:T(8,128)(2,1)S(1)} %get-tuple-element.144), channel_id=1, source_target_pairs={{0,2},{2,4},{4,6},{6,8},{8,10},{10,12},{12,14},{14,16},{16,18},{18... | collective-permute-start | bytes 49160 | tf_op jit(solution)/shard_map/ppermute | solution.py:69
  139.2 24.8 %copy-start.1 = (bf16[768,256]{1,0:T(8,128)(2,1)S(1)}, bf16[768,256]{1,0:T(8,128)(2,1)}, u32[]{:S(2)}) copy-start(bf16[768,256]{1,0:T(8,128)(2,1)} %copy-done) | copy-start | bytes 1179652
  139.2 33.2 %all-to-all-start.2 = ((bf16[64,56,128]{2,1,0:T(8,128)(2,1)}), bf16[64,56,128]{2,1,0:T(8,128)(2,1)S(1)}, u32[]{:S(2)}, u32[]{:S(2)}) async-start(bf16[64,56,128]{2,1,0:T(8,128)(2,1)} %copy-done.2), calls=%async_computation.2 | async-start | bytes 1835008 | tf_op jit(solution)/shard_map/all_to_all | solution.py:84
  148.1 15.8 %collective-permute-start.14 = (bf16[768,256]{1,0:T(8,128)(2,1)S(1)}, bf16[768,256]{1,0:T(8,128)(2,1)S(1)}, u32[]{:S(2)}, u32[]{:S(2)}) collective-permute-start(bf16[768,256]{1,0:T(8,128)(2,1)S(1)} %copy-done.19), channel_id=1, source_target_pairs={{0,1},{1,0},{2,3},{3,2},{4,5},{5,4},{6,7},{7,6},{8,9},{9,8},{10,11... | collective-permute-start | bytes 1179656 | tf_op jit(solution)/shard_map/ppermute | solution.py:59
  173.0 6.5 %collective-permute-start.22 = (bf16[2,1792,128]{2,1,0:T(8,128)(2,1)S(1)}, bf16[2,1792,128]{2,1,0:T(8,128)(2,1)S(1)}, u32[]{:S(2)}, u32[]{:S(2)}) collective-permute-start(bf16[2,1792,128]{2,1,0:T(8,128)(2,1)S(1)} %bitcast.15), channel_id=1, source_target_pairs={{0,2},{2,0},{4,6},{6,4},{8,10},{10,8},{12,14},{14,12},{16,18},{18,... | collective-permute-start | bytes 2752520 | tf_op jit(solution)/shard_map/ppermute | solution.py:64
  (18 other events, 92.7 us)

commit v5 on v4

--- a/solution.py
+++ b/solution.py
@@ -295,7 +295,7 @@
     sent[...] = total.astype(BF16)
 
 
-def long_kernel(info, x_own, x_got, n_own, n_got, same, other, idx_c, idx_r, w_in, w_out,
+def long_kernel(info, x_own, x_got, n_own, n_got, same, other, idx_c, idx_r, w_in, w_out, after,
                 slope, act, normed, inverse, out_own, out_sent, partial, sent, sender_rows, update):
     half = x_own.shape[1]
     rows = pl.ds(0, x_own.shape[0])
@@ -522,14 +522,15 @@
         in_hbm=(0,),
     )
     same = chips_all_to_all(sent_coarse)
+    rims_got = swap_lat(jnp.concatenate([low, high], 0))
+    we_got = gated(info, we_got, (rims_got,))
     we_again = swap_core(we_got)
-    rims_got = swap_lat(jnp.concatenate([low, high], 0))
 
     got_spec = [whole((4, quarter, full))] * 2
     w_in, w_out, sent_g, sent_wn = call(
         edge_weights_kernel,
         info,
-        (wi_hbm, wo_hbm, pinned(we_got), pinned(we_again), g_hbm, g_hbm, ng_hbm, ni_hbm, no_hbm, rims_got, idx_cf, idx_cl),
+        (wi_hbm, wo_hbm, pinned(we_got), pinned(we_again), g_hbm, g_hbm, ng_hbm, ni_hbm, no_hbm, x_got, idx_cf, idx_cl),
         [whole((3, half, full)), whole((half, full))] + got_spec + [
             fine_other, long_other, whole((nodes, half)),
             block((2, quarter, full), lambda i, s: (0, s[1], 0)), quarter_rows,
@@ -589,11 +590,12 @@
     slope_l, act_l, normed_l, inverse_l, long_out, long_sent, partial_l, partial_l_sent, srow_l = call(
         long_kernel,
         info,
-        (x_hbm, x_got, n_hbm, x_got, same, other, idx_cl, idx_rl, w_in, w_out),
+        (x_hbm, x_got, n_hbm, x_got, same, other, idx_cl, idx_rl, w_in, w_out, g_got),
         [
             long_own(), long_got(), whole((16, half)), block((16, half), lambda i, s: (rows // 16, 0)),
             whole((far_rows, full)), whole((far_rows, full)),
             whole((longs, 3)), whole((3, longs)), win_spec, wout_spec,
+            pl.BlockSpec(memory_space=pl.ANY),
         ],
         forward_outs(longs, 16) + [((longs, full), BF16)],
         [pltpu.VMEM((longs, full), BF16)],
@@ -601,7 +603,8 @@
         moved=6_000_000,
         name="edges_forward_long",
     )
-    wn_got = gated(info, wn_got, (partial_l_sent, partial_f_sent))
+    partial_f_got = swap_lat(partial_f_sent)
+    wn_got = gated(info, wn_got, (partial_l_sent, partial_f_got))
     wn_again = swap_core(wn_got)
     nin, nout = call(
         weights_kernel,
@@ -612,7 +615,6 @@
         moved=3_000_000,
         name="node_weights",
     )
-    partial_f_got = swap_lat(partial_f_sent)
     partial_l_got = swap_lat(partial_l_sent)
 
     edge_out_got = swap_lat(jnp.concatenate([fine_sent, long_sent], 0))

time: 183 us -> 182 us (level)
  starting transfers between devices: 64.9 us -> 68.2 us
  waiting for transfers between devices: 71 us -> 68 us
    ppermute x3, waiting for transfers between devices: 16.6 us -> 7.33 us  [other_neighbour(): return lax.ppermute(value, ('patch', 'lat'), pairs)]
    ppermute x4, waiting for transfers between devices: 3.63 us -> 8.71 us  [shifted(): lax.ppermute(value, 'patch', [(i, (i + steps) % count) for i in range(cou...]
    ppermute x3, starting transfers between devices: 4.52 us -> 6.77 us  [other_neighbour(): return lax.ppermute(value, ('patch', 'lat'), pairs)]
    unnamed x48 -> x50, local copies, waits for them, and re-layouts: 3.69 us -> 3.02 us
  transfers between devices with their start and end apart: 26 -> 26, of which waited for: 15 -> 18; matrix products, arithmetic and copies ran while one was open for 1% -> 1% of each run, Pallas kernels for 12% -> 11%
where the time goes in v5:
time: 182 us
  starting transfers between devices  68.2 us (37%)
  waiting for transfers between devices  68 us (37%)
  Pallas kernels  37.9 us (21%)
  local copies, waits for them, and re-layouts  4.01 us (2%)
  between operations  1.94 us (1%)
    ppermute x10, waiting for transfers between devices, swap_lat(): return lax.ppermute(value, 'lat', [(0, 1), (1, 0)])  39.7 us
    pallas_call x13, Pallas kernels, call(): pl.pallas_call(kernel, grid_spec=pltpu.PrefetchScalarGridSpec(num_scalar_...  33.8 us
    all_to_all x3, starting transfers between devices, chips_all_to_all(): lax.all_to_all(value, 'patch', 0, 0, tiled=True, axis_index_groups=groups)  33.1 us
    ppermute x6, starting transfers between devices, swap_core(): return lax.ppermute(value, 'patch', [(i, i ^ 1) for i in range(count)])  11.4 us
    ppermute x4, starting transfers between devices, shifted(): lax.ppermute(value, 'patch', [(i, (i + steps) % count) for i in range(cou...  10.9 us
    ppermute x4, waiting for transfers between devices, shifted(): lax.ppermute(value, 'patch', [(i, (i + steps) % count) for i in range(cou...  8.71 us
    ppermute x3, waiting for transfers between devices, other_neighbour(): return lax.ppermute(value, ('patch', 'lat'), pairs)  7.33 us
    ppermute x3, starting transfers between devices, other_neighbour(): return lax.ppermute(value, ('patch', 'lat'), pairs)  6.77 us
  transfers between devices with their start and end apart: 26, of which 18 were waited for; matrix products, arithmetic and copies ran while one was open for 1% of the time, Pallas kernels for 11%

profile of v5, /device:TPU:1, one launch (start us, length us, event | category | flops | bytes accessed | tf_op | source)
XLA Modules:
  0.0 181.8 jit_solution(11925447880878203956)
XLA Ops:
  1.3 2.0 %collective-permute-start.6 = (bf16[16,256]{1,0:T(8,128)(2,1)S(1)}, bf16[16,256]{1,0:T(8,128)(2,1)S(1)}, u32[]{:S(2)}, u32[]{:S(2)}) collective-permute-start(bf16[16,256]{1,0:T(8,128)(2,1)S(1)} %slice.78), channel_id=1, source_target_pairs={{0,1},{1,0},{2,3},{3,2},{4,5},{5,4},{6,7},{7,6},{8,9},{9,8},{10,11... | collective-permute-start | bytes 24584 | tf_op jit(solution)/shard_map/ppermute | solution.py:59
  5.3 2.1 %coarse_rows.1 = bf16[64,8,512]{2,1,0:T(8,128)(2,1)} custom-call(s32[2]{0:T(128)S(1)} %pad_add_fusion.2.info, bf16[192,256]{1,0:T(8,128)(2,1)} %n_own.7, bf16[16,256]{1,0:T(8,128)(2,1)S(1)} %collective-permute-done.6.n_got, bf16[32,256]{1,0:T(8,128)(2,1)S(1)} %get-tuple-element.94.after), custom_call_target="tpu_custom_call" | custom-call | bytes 600000 | tf_op jit(solution)/shard_map/coarse_rows/pallas_call | solution.py:96
  7.4 14.0 %all-to-all-start = ((bf16[64,8,512]{2,1,0:T(8,128)(2,1)}), bf16[64,8,512]{2,1,0:T(8,128)(2,1)S(1)}, u32[]{:S(2)}, u32[]{:S(2)}) async-start(bf16[64,8,512]{2,1,0:T(8,128)(2,1)} %coarse_rows.1), calls=%async_computation | async-start | bytes 1048576 | tf_op jit(solution)/shard_map/all_to_all | solution.py:84
  21.4 2.0 %collective-permute-start.4 = (bf16[4,128,512]{2,1,0:T(8,128)(2,1)S(1)}, bf16[4,128,512]{2,1,0:T(8,128)(2,1)S(1)}, u32[]{:S(2)}, u32[]{:S(2)}) collective-permute-start(bf16[4,128,512]{2,1,0:T(8,128)(2,1)S(1)} %get-tuple-element.95), channel_id=1, source_target_pairs={{0,5},{1,4},{2,7},{3,6},{4,1},{5,0},{6,3},{7,2},{8,13},{9,12},{10,... | collective-permute-start | bytes 1572872 | tf_op jit(solution)/shard_map/ppermute | solution.py:78
  23.4 2.6 %collective-permute-start.1 = (bf16[32,256]{1,0:T(8,128)(2,1)S(1)}, bf16[32,256]{1,0:T(8,128)(2,1)S(1)}, u32[]{:S(2)}, u32[]{:S(2)}) collective-permute-start(bf16[32,256]{1,0:T(8,128)(2,1)S(1)} %get-tuple-element.93), channel_id=1, source_target_pairs={{0,2},{2,4},{4,6},{6,8},{8,10},{10,12},{12,14},{14,16},{16,18},{18... | collective-permute-start | bytes 49160 | tf_op jit(solution)/shard_map/ppermute | solution.py:69
  26.9 4.1 %collective-permute-done.2.high = bf16[32,256]{1,0:T(8,128)(2,1)S(1)} collective-permute-done((bf16[32,256]{1,0:T(8,128)(2,1)S(1)}, bf16[32,256]{1,0:T(8,128)(2,1)S(1)}, u32[]{:S(2)}, u32[]{:S(2)}) %collective-permute-start.2) | collective-permute-done | bytes 16416 | tf_op jit(solution)/shard_map/ppermute | solution.py:69
  32.5 1.9 %collective-permute-done.3.rest_0_.rims_got = bf16[64,256]{1,0:T(8,128)(2,1)S(1)} collective-permute-done((bf16[64,256]{1,0:T(8,128)(2,1)S(1)}, bf16[64,256]{1,0:T(8,128)(2,1)S(1)}, u32[]{:S(2)}, u32[]{:S(2)}) %collective-permute-start.3) | collective-permute-done | bytes 32800 | tf_op jit(solution)/shard_map/ppermute | solution.py:59
  34.4 6.3 %collective-permute-done.4.value = bf16[4,128,512]{2,1,0:T(8,128)(2,1)S(1)} collective-permute-done((bf16[4,128,512]{2,1,0:T(8,128)(2,1)S(1)}, bf16[4,128,512]{2,1,0:T(8,128)(2,1)S(1)}, u32[]{:S(2)}, u32[]{:S(2)}) %collective-permute-start.4) | collective-permute-done | bytes 524320 | tf_op jit(solution)/shard_map/ppermute | solution.py:78
  41.2 2.1 %collective-permute-start.5 = (bf16[4,128,512]{2,1,0:T(8,128)(2,1)S(1)}, bf16[4,128,512]{2,1,0:T(8,128)(2,1)}, u32[]{:S(2)}, u32[]{:S(2)}) collective-permute-start(bf16[4,128,512]{2,1,0:T(8,128)(2,1)S(1)} %gate.3.got), channel_id=1, source_target_pairs={{0,2},{2,0},{4,6},{6,4},{8,10},{10,8},{12,14},{14,12},{16,18},{18,... | collective-permute-start | bytes 1572872 | tf_op jit(solution)/shard_map/ppermute | solution.py:64
  45.5 2.6 %edge_weights.1 = (bf16[3,512,512]{2,1,0:T(8,128)(2,1)S(1)}, bf16[512,512]{1,0:T(8,128)(2,1)S(1)}, bf16[960,256]{1,0:T(8,128)(2,1)S(1)}, bf16[3,128,512]{2,1,0:T(8,128)(2,1)S(1)}) custom-call(s32[2]{0:T(128)S(1)} %pad_add_fusion.2.info, bf16[3,256,512]{2,1,0:T(8,128)(2,1)} %wi.4, bf16[256,512]{1,0:T(8,128)(2,1)} %wo.4, bf16[4,128,512]{2,1,0:T(8,128)(2,1)} %copy-done, ...), custom_call_target="tpu_custom_call" | custom-call | bytes 7000000 | tf_op jit(solution)/shard_map/edge_weights/pallas_call | solution.py:96
  48.2 3.3 %collective-permute-start.12 = (bf16[3,128,512]{2,1,0:T(8,128)(2,1)S(1)}, bf16[3,128,512]{2,1,0:T(8,128)(2,1)S(1)}, u32[]{:S(2)}, u32[]{:S(2)}) collective-permute-start(bf16[3,128,512]{2,1,0:T(8,128)(2,1)S(1)} %get-tuple-element.107), channel_id=1, source_target_pairs={{0,5},{1,4},{2,7},{3,6},{4,1},{5,0},{6,3},{7,2},{8,13},{9,12},{10,... | collective-permute-start | bytes 1179656 | tf_op jit(solution)/shard_map/ppermute | solution.py:78
  51.5 4.4 %edges_forward_fine.1 = (f32[576,512]{1,0:T(8,128)S(1)}, bf16[576,512]{1,0:T(8,128)(2,1)S(1)}, f32[576,512]{1,0:T(8,128)S(1)}, f32[576,1]{1,0:T(8,128)S(1)}, bf1...) custom-call(s32[2]{0:T(128)S(1)} %pad_add_fusion.2.info, ...), custom_call_target="tpu_custom_call" | custom-call | flops 1585446912 | bytes 8000000 | tf_op jit(solution)/shard_map/edges_forward_fine/pallas_call | solution.py:96
  56.1 2.9 %collective-permute-done.8.after.ng_got.gf_got.gl_got.g_got = bf16[960,256]{1,0:T(8,128)(2,1)S(1)} collective-permute-done((bf16[960,256]{1,0:T(8,128)(2,1)S(1)}, bf16[960,256]{1,0:T(8,128)(2,1)S(1)}, u32[]{:S(2)}, u32[]{:S(2)}) %collective-permute-start.8) | collective-permute-done | bytes 491552 | tf_op jit(solution)/shard_map/ppermute | solution.py:59
  59.0 3.1 %edges_forward_long.1 = (f32[192,512]{1,0:T(8,128)S(1)}, bf16[192,512]{1,0:T(8,128)(2,1)S(1)}, f32[192,512]{1,0:T(8,128)S(1)}, f32[192,1]{1,0:T(8,128)S(1)}, bf1...) custom-call(s32[2]{0:T(128)S(1)} %pad_add_fusion.2.info, ...), custom_call_target="tpu_custom_call" | custom-call | flops 1283457024 | bytes 6000000 | tf_op jit(solution)/shard_map/edges_forward_long/pallas_call | solution.py:96
  63.8 3.9 %collective-permute-start.13 = (bf16[3,128,512]{2,1,0:T(8,128)(2,1)S(1)}, bf16[3,128,512]{2,1,0:T(8,128)(2,1)S(1)}, u32[]{:S(2)}, u32[]{:S(2)}) collective-permute-start(bf16[3,128,512]{2,1,0:T(8,128)(2,1)S(1)} %gate.4.got), channel_id=1, source_target_pairs={{0,2},{2,0},{4,6},{6,4},{8,10},{10,8},{12,14},{14,12},{16,18},{18,... | collective-permute-start | bytes 1179656 | tf_op jit(solution)/shard_map/ppermute | solution.py:64
  69.0 1.8 %node_weights.1 = (bf16[2,512,512]{2,1,0:T(8,128)(2,1)S(1)}, bf16[512,512]{1,0:T(8,128)(2,1)S(1)}) custom-call(s32[2]{0:T(128)S(1)} %pad_add_fusion.2.info, bf16[2,256,512]{2,1,0:T(8,128)(2,1)} %wi.5, bf16[256,512]{1,0:T(8,128)(2,1)} %wo.5, bf16[3,128,512]{2,1,0:T(8,128)(2,1)S(1)} %gate.4.got, bf16[3,128,512]{2,1,0:T(8,128)(2,1)S(1)} %collective-permute-done.13.again), custom_call_target="tpu_custom_call" | custom-call | bytes 3000000 | tf_op jit(solution)/shard_map/node_weights/pallas_call | solution.py:96
  70.8 8.3 %nodes_and_edges_backward.1 = (bf16[192,256]{1,0:T(8,128)(2,1)}, f32[192,256]{1,0:T(8,128)S(1)}, bf16[1536,256]{1,0:T(8,128)(2,1)S(1)}, bf16[1536,256]{1,0:T(8,1...) custom-call(s32[2]{0:T(128)S(1)} %pad_add_fusion.2.info, ...), custom_call_target="tpu_custom_call" | custom-call | flops 1610612736 | bytes 14000000 | tf_op jit(solution)/shard_map/nodes_and_edges_backward/pallas_call | solution.py:96
  84.2 8.9 %collective-permute-done.20.first = bf16[768,256]{1,0:T(8,128)(2,1)S(1)} collective-permute-done((bf16[768,256]{1,0:T(8,128)(2,1)S(1)}, bf16[768,256]{1,0:T(8,128)(2,1)S(1)}, u32[]{:S(2)}, u32[]{:S(2)}) %collective-permute-start.20) | collective-permute-done | bytes 393248 | tf_op jit(solution)/shard_map/ppermute | solution.py:59
  94.2 2.0 %combine.1 = bf16[64,72,128]{2,1,0:T(8,128)(2,1)} custom-call(s32[2]{0:T(128)S(1)} %pad_add_fusion.2.info, bf16[2304,256]{1,0:T(8,128)(2,1)S(1)} %get-tuple-element.128.keep, bf16[2304,256]{1,0:T(8,128)(2,1)S(1)} %collective-permute-done.18.got, bf16[768,256]{1,0:T(8,128)(2,1)S(1)} %collective-permute-done.20.first, ...), custom_call_target="tpu_custom_call" | custom-call | bytes 4300000 | tf_op jit(solution)/shard_map/combine/pallas_call | solution.py:96
  96.2 10.1 %all-to-all-start.1 = ((bf16[64,72,128]{2,1,0:T(8,128)(2,1)}), bf16[64,72,128]{2,1,0:T(8,128)(2,1)S(1)}, u32[]{:S(2)}, u32[]{:S(2)}) async-start(bf16[64,72,128]{2,1,0:T(8,128)(2,1)} %combine.1), calls=%async_computation.1 | async-start | bytes 2359296 | tf_op jit(solution)/shard_map/all_to_all | solution.py:84
  106.3 2.9 %input_gradients.1 = (bf16[768,256]{1,0:T(8,128)(2,1)S(1)}, bf16[768,256]{1,0:T(8,128)(2,1)S(1)}, f32[256,256]{1,0:T(8,128)S(1)}, bf16[256,256]{1,0:T(8,128)(2,1)S(1)}) custom-call(s32[2]{0:T(128)S(1)} %pad_add_fusion.2.info, bf16[768,512]{1,0:T(8,128)(2,1)} %copy-done.4, bf16[1536,256]{1,0:T(8,128)(2,1)} %gl_own.3, bf16[1536,256]{1,0:T(8,128)(2,1)} %gl_own.3, ...), custom_call_target="tpu_custom_call" | custom-call | flops 805306368 | bytes 5000000 | tf_op jit(solution)/shard_map/input_gradients/pallas_call | solution.py:96
  112.3 3.3 %collective-permute-done.15 = bf16[256,256]{1,0:T(8,128)(2,1)S(1)} collective-permute-done((bf16[256,256]{1,0:T(8,128)(2,1)S(1)}, bf16[256,256]{1,0:T(8,128)(2,1)S(1)}, u32[]{:S(2)}, u32[]{:S(2)}) %collective-permute-start.15) | collective-permute-done | bytes 131104 | tf_op jit(solution)/shard_map/ppermute | solution.py:59
  116.3 5.9 %collective-permute-start.16 = (bf16[32,256]{1,0:T(8,128)(2,1)S(1)}, bf16[32,256]{1,0:T(8,128)(2,1)S(1)}, u32[]{:S(2)}, u32[]{:S(2)}) collective-permute-start(bf16[32,256]{1,0:T(8,128)(2,1)S(1)} %get-tuple-element.145), channel_id=1, source_target_pairs={{0,254},{2,0},{4,2},{6,4},{8,6},{10,8},{12,10},{14,12},{16,14},{18... | collective-permute-start | bytes 49160 | tf_op jit(solution)/shard_map/ppermute | solution.py:69
  122.3 2.3 %collective-permute-start.17 = (bf16[32,256]{1,0:T(8,128)(2,1)S(1)}, bf16[32,256]{1,0:T(8,128)(2,1)S(1)}, u32[]{:S(2)}, u32[]{:S(2)}) collective-permute-start(bf16[32,256]{1,0:T(8,128)(2,1)S(1)} %get-tuple-element.144), channel_id=1, source_target_pairs={{0,2},{2,4},{4,6},{6,8},{8,10},{10,12},{12,14},{14,16},{16,18},{18... | collective-permute-start | bytes 49160 | tf_op jit(solution)/shard_map/ppermute | solution.py:69
  124.6 6.5 %collective-permute-done.9.got = bf16[768,256]{1,0:T(8,128)(2,1)S(1)} collective-permute-done((bf16[768,256]{1,0:T(8,128)(2,1)S(1)}, bf16[768,256]{1,0:T(8,128)(2,1)S(1)}, u32[]{:S(2)}, u32[]{:S(2)}) %collective-permute-start.9) | collective-permute-done | bytes 393248 | tf_op jit(solution)/shard_map/ppermute | solution.py:59
  132.5 3.8 %collective-permute-done.16 = bf16[32,256]{1,0:T(8,128)(2,1)S(1)} collective-permute-done((bf16[32,256]{1,0:T(8,128)(2,1)S(1)}, bf16[32,256]{1,0:T(8,128)(2,1)S(1)}, u32[]{:S(2)}, u32[]{:S(2)}) %collective-permute-start.16) | collective-permute-done | bytes 16416 | tf_op jit(solution)/shard_map/ppermute | solution.py:69
  138.9 8.9 %all-to-all-start.2 = ((bf16[64,56,128]{2,1,0:T(8,128)(2,1)}), bf16[64,56,128]{2,1,0:T(8,128)(2,1)S(1)}, u32[]{:S(2)}, u32[]{:S(2)}) async-start(bf16[64,56,128]{2,1,0:T(8,128)(2,1)} %copy-done.3), calls=%async_computation.2 | async-start | bytes 1835008 | tf_op jit(solution)/shard_map/all_to_all | solution.py:84
  148.5 15.2 %collective-permute-done.14.got = bf16[768,256]{1,0:T(8,128)(2,1)S(1)} collective-permute-done((bf16[768,256]{1,0:T(8,128)(2,1)S(1)}, bf16[768,256]{1,0:T(8,128)(2,1)S(1)}, u32[]{:S(2)}, u32[]{:S(2)}) %collective-permute-start.14) | collective-permute-done | bytes 393248 | tf_op jit(solution)/shard_map/ppermute | solution.py:59
  165.8 6.3 %all-to-all-done.2.value = bf16[64,56,128]{2,1,0:T(8,128)(2,1)S(1)} async-done(((bf16[64,56,128]{2,1,0:T(8,128)(2,1)}), bf16[64,56,128]{2,1,0:T(8,128)(2,1)S(1)}, u32[]{:S(2)}, u32[]{:S(2)}) %all-to-all-start.2) | async-done | bytes 917536 | tf_op jit(solution)/shard_map/all_to_all | solution.py:84
  172.7 4.4 %collective-permute-start.22 = (bf16[2,1792,128]{2,1,0:T(8,128)(2,1)S(1)}, bf16[2,1792,128]{2,1,0:T(8,128)(2,1)S(1)}, u32[]{:S(2)}, u32[]{:S(2)}) collective-permute-start(bf16[2,1792,128]{2,1,0:T(8,128)(2,1)S(1)} %bitcast.15), channel_id=1, source_target_pairs={{0,2},{2,0},{4,6},{6,4},{8,10},{10,8},{12,14},{14,12},{16,18},{18,... | collective-permute-start | bytes 2752520 | tf_op jit(solution)/shard_map/ppermute | solution.py:64
  177.1 2.1 %collective-permute-done.22.other = bf16[2,1792,128]{2,1,0:T(8,128)(2,1)S(1)} collective-permute-done((bf16[2,1792,128]{2,1,0:T(8,128)(2,1)S(1)}, bf16[2,1792,128]{2,1,0:T(8,128)(2,1)S(1)}, u32[]{:S(2)}, u32[]{:S(2)}) %collective-permute-start.22) | collective-permute-done | bytes 917536 | tf_op jit(solution)/shard_map/ppermute | solution.py:64
  179.2 2.5 %results.1 = (f32[3,256,512]{2,1,0:T(8,128)}, f32[256,512]{1,0:T(8,128)}, f32[2,256,512]{2,1,0:T(8,128)}, f32[256,512]{1,0:T(8,128)}) custom-call(s32[2]{0:T(128)S(1)} %pad_add_fusion.2.info, bf16[2,1792,128]{2,1,0:T(8,128)(2,1)S(1)} %bitcast.16, bf16[2,1792,128]{2,1,0:T(8,128)(2,1)S(1)} %collective-permute-done.22.other), custom_call_target="tpu_custom_call" | custom-call | bytes 6000000 | tf_op jit(solution)/shard_map/results/pallas_call | solution.py:761
  (110 shorter events, 27.5 us)
Async XLA Ops:
  1.3 3.9 %collective-permute-start.6 = (bf16[16,256]{1,0:T(8,128)(2,1)S(1)}, bf16[16,256]{1,0:T(8,128)(2,1)S(1)}, u32[]{:S(2)}, u32[]{:S(2)}) collective-permute-start(bf16[16,256]{1,0:T(8,128)(2,1)S(1)} %slice.78), channel_id=1, source_target_pairs={{0,1},{1,0},{2,3},{3,2},{4,5},{5,4},{6,7},{7,6},{8,9},{9,8},{10,11... | collective-permute-start | bytes 24584 | tf_op jit(solution)/shard_map/ppermute | solution.py:59
  7.4 35.9 %copy-start.23 = (s32[12,128]{1,0:T(8,128)S(1)}, s32[12,128]{1,0:T(8,128)}, u32[]{:S(2)}) copy-start(s32[12,128]{1,0:T(8,128)} %param.19) | copy-start | bytes 18436
  7.4 35.9 %copy-start.24 = (s32[12,128]{1,0:T(8,128)S(1)}, s32[12,128]{1,0:T(8,128)}, u32[]{:S(2)}) copy-start(s32[12,128]{1,0:T(8,128)} %param.20) | copy-start | bytes 18436
  7.4 36.8 %all-to-all-start = ((bf16[64,8,512]{2,1,0:T(8,128)(2,1)}), bf16[64,8,512]{2,1,0:T(8,128)(2,1)S(1)}, u32[]{:S(2)}, u32[]{:S(2)}) async-start(bf16[64,8,512]{2,1,0:T(8,128)(2,1)} %coarse_rows.1), calls=%async_computation | async-start | bytes 1048576 | tf_op jit(solution)/shard_map/all_to_all | solution.py:84
  21.4 19.2 %collective-permute-start.4 = (bf16[4,128,512]{2,1,0:T(8,128)(2,1)S(1)}, bf16[4,128,512]{2,1,0:T(8,128)(2,1)S(1)}, u32[]{:S(2)}, u32[]{:S(2)}) collective-permute-start(bf16[4,128,512]{2,1,0:T(8,128)(2,1)S(1)} %get-tuple-element.95), channel_id=1, source_target_pairs={{0,5},{1,4},{2,7},{3,6},{4,1},{5,0},{6,3},{7,2},{8,13},{9,12},{10,... | collective-permute-start | bytes 1572872 | tf_op jit(solution)/shard_map/ppermute | solution.py:78
  23.4 3.5 %collective-permute-start.1 = (bf16[32,256]{1,0:T(8,128)(2,1)S(1)}, bf16[32,256]{1,0:T(8,128)(2,1)S(1)}, u32[]{:S(2)}, u32[]{:S(2)}) collective-permute-start(bf16[32,256]{1,0:T(8,128)(2,1)S(1)} %get-tuple-element.93), channel_id=1, source_target_pairs={{0,2},{2,4},{4,6},{6,8},{8,10},{10,12},{12,14},{14,16},{16,18},{18... | collective-permute-start | bytes 49160 | tf_op jit(solution)/shard_map/ppermute | solution.py:69
  26.0 5.0 %collective-permute-start.2 = (bf16[32,256]{1,0:T(8,128)(2,1)S(1)}, bf16[32,256]{1,0:T(8,128)(2,1)S(1)}, u32[]{:S(2)}, u32[]{:S(2)}) collective-permute-start(bf16[32,256]{1,0:T(8,128)(2,1)S(1)} %get-tuple-element.94.after), channel_id=1, source_target_pairs={{0,254},{2,0},{4,2},{6,4},{8,6},{10,8},{12,10},{14,12},{16,14},{18... | collective-permute-start | bytes 49160 | tf_op jit(solution)/shard_map/ppermute | solution.py:69
  26.9 17.5 %copy-start.15 = (bf16[32,256]{1,0:T(8,128)(2,1)}, bf16[32,256]{1,0:T(8,128)(2,1)S(1)}, u32[]{:S(2)}) copy-start(bf16[32,256]{1,0:T(8,128)(2,1)S(1)} %collective-permute-done.1.low) | copy-start | bytes 49156
  31.0 3.3 %collective-permute-start.3 = (bf16[64,256]{1,0:T(8,128)(2,1)S(1)}, bf16[64,256]{1,0:T(8,128)(2,1)S(1)}, u32[]{:S(2)}, u32[]{:S(2)}) collective-permute-start(bf16[64,256]{1,0:T(8,128)(2,1)S(1)} %pad_maximum_fusion.1), channel_id=1, source_target_pairs={{0,1},{1,0},{2,3},{3,2},{4,5},{5,4},{6,7},{7,6},{8,9},{9,8},{10,11... | collective-permute-start | bytes 98312 | tf_op jit(solution)/shard_map/ppermute | solution.py:59
  31.7 13.0 %collective-permute-start = (bf16[960,256]{1,0:T(8,128)(2,1)S(1)}, bf16[960,256]{1,0:T(8,128)(2,1)S(1)}, u32[]{:S(2)}, u32[]{:S(2)}) collective-permute-start(bf16[960,256]{1,0:T(8,128)(2,1)S(1)} %get-tuple-element.92), channel_id=1, source_target_pairs={{0,1},{1,0},{2,3},{3,2},{4,5},{5,4},{6,7},{7,6},{8,9},{9,8},{10,11... | collective-permute-start | bytes 1474568 | tf_op jit(solution)/shard_map/ppermute | solution.py:59
  41.2 3.8 %collective-permute-start.5 = (bf16[4,128,512]{2,1,0:T(8,128)(2,1)S(1)}, bf16[4,128,512]{2,1,0:T(8,128)(2,1)}, u32[]{:S(2)}, u32[]{:S(2)}) collective-permute-start(bf16[4,128,512]{2,1,0:T(8,128)(2,1)S(1)} %gate.3.got), channel_id=1, source_target_pairs={{0,2},{2,0},{4,6},{6,4},{8,10},{10,8},{12,14},{14,12},{16,18},{18,... | collective-permute-start | bytes 1572872 | tf_op jit(solution)/shard_map/ppermute | solution.py:64
  44.2 14.8 %collective-permute-start.7 = (bf16[64,8,512]{2,1,0:T(8,128)(2,1)S(1)}, bf16[64,8,512]{2,1,0:T(8,128)(2,1)}, u32[]{:S(2)}, u32[]{:S(2)}) collective-permute-start(bf16[64,8,512]{2,1,0:T(8,128)(2,1)S(1)} %all-to-all-done), channel_id=1, source_target_pairs={{0,2},{2,0},{4,6},{6,4},{8,10},{10,8},{12,14},{14,12},{16,18},{18,... | collective-permute-start | bytes 1572872 | tf_op jit(solution)/shard_map/ppermute | solution.py:64
  48.1 10.9 %collective-permute-start.8 = (bf16[960,256]{1,0:T(8,128)(2,1)S(1)}, bf16[960,256]{1,0:T(8,128)(2,1)S(1)}, u32[]{:S(2)}, u32[]{:S(2)}) collective-permute-start(bf16[960,256]{1,0:T(8,128)(2,1)S(1)} %get-tuple-element.99), channel_id=1, source_target_pairs={{0,1},{1,0},{2,3},{3,2},{4,5},{5,4},{6,7},{7,6},{8,9},{9,8},{10,11... | collective-permute-start | bytes 1474568 | tf_op jit(solution)/shard_map/ppermute | solution.py:59
  48.2 15.0 %collective-permute-start.12 = (bf16[3,128,512]{2,1,0:T(8,128)(2,1)S(1)}, bf16[3,128,512]{2,1,0:T(8,128)(2,1)S(1)}, u32[]{:S(2)}, u32[]{:S(2)}) collective-permute-start(bf16[3,128,512]{2,1,0:T(8,128)(2,1)S(1)} %get-tuple-element.107), channel_id=1, source_target_pairs={{0,5},{1,4},{2,7},{3,6},{4,1},{5,0},{6,3},{7,2},{8,13},{9,12},{10,... | collective-permute-start | bytes 1179656 | tf_op jit(solution)/shard_map/ppermute | solution.py:78
  56.0 7.2 %collective-permute-start.10 = (bf16[192,512]{1,0:T(8,128)(2,1)S(1)}, bf16[192,512]{1,0:T(8,128)(2,1)S(1)}, u32[]{:S(2)}, u32[]{:S(2)}) collective-permute-start(bf16[192,512]{1,0:T(8,128)(2,1)S(1)} %get-tuple-element.104), channel_id=1, source_target_pairs={{0,1},{1,0},{2,3},{3,2},{4,5},{5,4},{6,7},{7,6},{8,9},{9,8},{10,11... | collective-permute-start | bytes 589832 | tf_op jit(solution)/shard_map/ppermute | solution.py:59
  63.8 5.2 %collective-permute-start.13 = (bf16[3,128,512]{2,1,0:T(8,128)(2,1)S(1)}, bf16[3,128,512]{2,1,0:T(8,128)(2,1)S(1)}, u32[]{:S(2)}, u32[]{:S(2)}) collective-permute-start(bf16[3,128,512]{2,1,0:T(8,128)(2,1)S(1)} %gate.4.got), channel_id=1, source_target_pairs={{0,2},{2,0},{4,6},{6,4},{8,10},{10,8},{12,14},{14,12},{16,18},{18,... | collective-permute-start | bytes 1179656 | tf_op jit(solution)/shard_map/ppermute | solution.py:64
  67.6 3.2 %collective-permute-start.11 = (bf16[16,512]{1,0:T(8,128)(2,1)S(1)}, bf16[16,512]{1,0:T(8,128)(2,1)S(1)}, u32[]{:S(2)}, u32[]{:S(2)}) collective-permute-start(bf16[16,512]{1,0:T(8,128)(2,1)S(1)} %get-tuple-element.106.rest_0_), channel_id=1, source_target_pairs={{0,1},{1,0},{2,3},{3,2},{4,5},{5,4},{6,7},{7,6},{8,9},{9,8},{10,11... | collective-permute-start | bytes 49160 | tf_op jit(solution)/shard_map/ppermute | solution.py:59
  79.2 15.0 %copy-start.11 = (f32[192,256]{1,0:T(8,128)}, f32[192,256]{1,0:T(8,128)S(1)}, u32[]{:S(2)}) copy-start(f32[192,256]{1,0:T(8,128)S(1)} %get-tuple-element.125) | copy-start | bytes 589828
  79.2 2.7 %collective-permute-start.19 = (bf16[1536,256]{1,0:T(8,128)(2,1)S(1)}, bf16[1536,256]{1,0:T(8,128)(2,1)S(1)}, u32[]{:S(2)}, u32[]{:S(2)}) collective-permute-start(bf16[1536,256]{1,0:T(8,128)(2,1)S(1)} %get-tuple-element.131), channel_id=1, source_target_pairs={{0,2},{2,0},{4,6},{6,4},{8,10},{10,8},{12,14},{14,12},{16,18},{18,... | collective-permute-start | bytes 2359304 | tf_op jit(solution)/shard_map/ppermute | solution.py:64
  80.0 14.1 %collective-permute-start.18 = (bf16[2304,256]{1,0:T(8,128)(2,1)S(1)}, bf16[2304,256]{1,0:T(8,128)(2,1)S(1)}, u32[]{:S(2)}, u32[]{:S(2)}) collective-permute-start(bf16[2304,256]{1,0:T(8,128)(2,1)S(1)} %get-tuple-element.129), channel_id=1, source_target_pairs={{0,2},{2,0},{4,6},{6,4},{8,10},{10,8},{12,14},{14,12},{16,18},{18,... | collective-permute-start | bytes 3538952 | tf_op jit(solution)/shard_map/ppermute | solution.py:64
  82.7 10.4 %collective-permute-start.20 = (bf16[768,256]{1,0:T(8,128)(2,1)S(1)}, bf16[768,256]{1,0:T(8,128)(2,1)S(1)}, u32[]{:S(2)}, u32[]{:S(2)}) collective-permute-start(bf16[768,256]{1,0:T(8,128)(2,1)S(1)} %get-tuple-element.132), channel_id=1, source_target_pairs={{0,1},{1,0},{2,3},{3,2},{4,5},{5,4},{6,7},{7,6},{8,9},{9,8},{10,11... | collective-permute-start | bytes 1179656 | tf_op jit(solution)/shard_map/ppermute | solution.py:59
  82.8 11.4 %collective-permute-start.21 = (bf16[768,256]{1,0:T(8,128)(2,1)S(1)}, bf16[768,256]{1,0:T(8,128)(2,1)S(1)}, u32[]{:S(2)}, u32[]{:S(2)}) collective-permute-start(bf16[768,256]{1,0:T(8,128)(2,1)S(1)} %get-tuple-element.133), channel_id=1, source_target_pairs={{0,5},{1,4},{2,7},{3,6},{4,1},{5,0},{6,3},{7,2},{8,13},{9,12},{10,... | collective-permute-start | bytes 1179656 | tf_op jit(solution)/shard_map/ppermute | solution.py:78
  96.2 40.6 %all-to-all-start.1 = ((bf16[64,72,128]{2,1,0:T(8,128)(2,1)}), bf16[64,72,128]{2,1,0:T(8,128)(2,1)S(1)}, u32[]{:S(2)}, u32[]{:S(2)}) async-start(bf16[64,72,128]{2,1,0:T(8,128)(2,1)} %combine.1), calls=%async_computation.1 | async-start | bytes 2359296 | tf_op jit(solution)/shard_map/all_to_all | solution.py:84
  110.7 20.3 %copy-start.8 = (bf16[576,256]{1,0:T(8,128)(2,1)S(1)}, bf16[576,256]{1,0:T(8,128)(2,1)}, u32[]{:S(2)}) copy-start(bf16[576,256]{1,0:T(8,128)(2,1)} %copy-done.7) | copy-start | bytes 884740
  110.7 4.9 %collective-permute-start.15 = (bf16[256,256]{1,0:T(8,128)(2,1)S(1)}, bf16[256,256]{1,0:T(8,128)(2,1)S(1)}, u32[]{:S(2)}, u32[]{:S(2)}) collective-permute-start(bf16[256,256]{1,0:T(8,128)(2,1)S(1)} %get-tuple-element.127), channel_id=1, source_target_pairs={{0,1},{1,0},{2,3},{3,2},{4,5},{5,4},{6,7},{7,6},{8,9},{9,8},{10,11... | collective-permute-start | bytes 393224 | tf_op jit(solution)/shard_map/ppermute | solution.py:59
  111.6 19.4 %collective-permute-start.9 = (bf16[768,256]{1,0:T(8,128)(2,1)S(1)}, bf16[768,256]{1,0:T(8,128)(2,1)S(1)}, u32[]{:S(2)}, u32[]{:S(2)}) collective-permute-start(bf16[768,256]{1,0:T(8,128)(2,1)S(1)} %pad_maximum_fusion), channel_id=1, source_target_pairs={{0,1},{1,0},{2,3},{3,2},{4,5},{5,4},{6,7},{7,6},{8,9},{9,8},{10,11... | collective-permute-start | bytes 1179656 | tf_op jit(solution)/shard_map/ppermute | solution.py:59
  116.3 19.9 %collective-permute-start.16 = (bf16[32,256]{1,0:T(8,128)(2,1)S(1)}, bf16[32,256]{1,0:T(8,128)(2,1)S(1)}, u32[]{:S(2)}, u32[]{:S(2)}) collective-permute-start(bf16[32,256]{1,0:T(8,128)(2,1)S(1)} %get-tuple-element.145), channel_id=1, source_target_pairs={{0,254},{2,0},{4,2},{6,4},{8,6},{10,8},{12,10},{14,12},{16,14},{18... | collective-permute-start | bytes 49160 | tf_op jit(solution)/shard_map/ppermute | solution.py:69
  122.3 14.0 %collective-permute-start.17 = (bf16[32,256]{1,0:T(8,128)(2,1)S(1)}, bf16[32,256]{1,0:T(8,128)(2,1)S(1)}, u32[]{:S(2)}, u32[]{:S(2)}) collective-permute-start(bf16[32,256]{1,0:T(8,128)(2,1)S(1)} %get-tuple-element.144), channel_id=1, source_target_pairs={{0,2},{2,4},{4,6},{6,8},{8,10},{10,12},{12,14},{14,16},{16,18},{18... | collective-permute-start | bytes 49160 | tf_op jit(solution)/shard_map/ppermute | solution.py:69
  138.9 24.8 %copy-start.2 = (bf16[768,256]{1,0:T(8,128)(2,1)S(1)}, bf16[768,256]{1,0:T(8,128)(2,1)}, u32[]{:S(2)}) copy-start(bf16[768,256]{1,0:T(8,128)(2,1)} %copy-done.1) | copy-start | bytes 1179652
  138.9 33.2 %all-to-all-start.2 = ((bf16[64,56,128]{2,1,0:T(8,128)(2,1)}), bf16[64,56,128]{2,1,0:T(8,128)(2,1)S(1)}, u32[]{:S(2)}, u32[]{:S(2)}) async-start(bf16[64,56,128]{2,1,0:T(8,128)(2,1)} %copy-done.3), calls=%async_computation.2 | async-start | bytes 1835008 | tf_op jit(solution)/shard_map/all_to_all | solution.py:84
  147.9 15.9 %collective-permute-start.14 = (bf16[768,256]{1,0:T(8,128)(2,1)S(1)}, bf16[768,256]{1,0:T(8,128)(2,1)S(1)}, u32[]{:S(2)}, u32[]{:S(2)}) collective-permute-start(bf16[768,256]{1,0:T(8,128)(2,1)S(1)} %copy-done.20), channel_id=1, source_target_pairs={{0,1},{1,0},{2,3},{3,2},{4,5},{5,4},{6,7},{7,6},{8,9},{9,8},{10,11... | collective-permute-start | bytes 1179656 | tf_op jit(solution)/shard_map/ppermute | solution.py:59
  172.7 6.5 %collective-permute-start.22 = (bf16[2,1792,128]{2,1,0:T(8,128)(2,1)S(1)}, bf16[2,1792,128]{2,1,0:T(8,128)(2,1)S(1)}, u32[]{:S(2)}, u32[]{:S(2)}) collective-permute-start(bf16[2,1792,128]{2,1,0:T(8,128)(2,1)S(1)} %bitcast.15), channel_id=1, source_target_pairs={{0,2},{2,0},{4,6},{6,4},{8,10},{10,8},{12,14},{14,12},{16,18},{18,... | collective-permute-start | bytes 2752520 | tf_op jit(solution)/shard_map/ppermute | solution.py:64
  (19 other events, 138.7 us)

commit v6 on v5

--- a/solution.py
+++ b/solution.py
@@ -116,7 +116,7 @@
     return pltpu.with_memory_space_constraint(value, pltpu.HBM)
 
 
-def pack_kernel(info, xf, xl, n, wi, wo, xs, wes, low, high):
+def pack_kernel(info, xf, xl, gf, gl, n, ng, wi, wo, xs, gs, wes, low, high):
     fine = xf.shape[0]
     low[...] = n[:HALO]
     high[...] = n[n.shape[0] - HALO :]
@@ -125,6 +125,9 @@
     xs[:fine] = xf[...]
     xs[fine : fine + xl.shape[0]] = xl[...]
     xs[fine + xl.shape[0] :] = n[...]
+    gs[:fine] = gf[...]
+    gs[fine : fine + gl.shape[0]] = gl[...]
+    gs[fine + gl.shape[0] :] = ng[...]
 
 
 def coarse_kernel(info, n_own, n_got, after, out, staged, sem):
@@ -226,13 +229,9 @@
         copy.wait()
 
 
-def edge_weights_kernel(info, wi, wo, got, again, gf, gl, ng, ni, no, after, idx_f, idx_l, full_in, full_out, gs, wns):
-    fine = gf.shape[0]
+def edge_weights_kernel(info, wi, wo, got, again, ni, no, after, idx_f, idx_l, full_in, full_out, wns):
     wns[:2] = ni[...]
     wns[2] = no[...]
-    gs[:fine] = gf[...]
-    gs[fine : fine + gl.shape[0]] = gl[...]
-    gs[fine + gl.shape[0] :] = ng[...]
     weights_kernel(info, wi, wo, got, again, full_in, full_out)
 
 
@@ -494,15 +493,15 @@
     fine_other = block((fine, half), lambda i, s: (1 - s[0], 0))
     long_other = block((longs, half), lambda i, s: (FINE // longs + 1 - s[0], 0))
     quarter_rows = block((quarter, full), lambda i, s: (s[1], 0))
-    sent_x, sent_we, rim_low, rim_high = call(
+    sent_x, sent_g, sent_we, rim_low, rim_high = call(
         pack_kernel,
         info,
-        (x_hbm, x_hbm, n_hbm, wi_hbm, wo_hbm),
+        (x_hbm, x_hbm, g_hbm, g_hbm, n_hbm, ng_hbm, wi_hbm, wo_hbm),
         [
-            fine_other, long_other, whole((nodes, half)),
+            fine_other, long_other, fine_other, long_other, whole((nodes, half)), whole((nodes, half)),
             block((3, quarter, full), lambda i, s: (0, s[1], 0)), quarter_rows,
         ],
-        [((rows + nodes, half), BF16), ((4, quarter, full), BF16), ((HALO, half), BF16), ((HALO, half), BF16)],
+        [((rows + nodes, half), BF16), ((rows + nodes, half), BF16), ((4, quarter, full), BF16), ((HALO, half), BF16), ((HALO, half), BF16)],
         moved=3_000_000,
         name="pack",
     )
@@ -527,16 +526,15 @@
     we_again = swap_core(we_got)
 
     got_spec = [whole((4, quarter, full))] * 2
-    w_in, w_out, sent_g, sent_wn = call(
+    w_in, w_out, sent_wn = call(
         edge_weights_kernel,
         info,
-        (wi_hbm, wo_hbm, pinned(we_got), pinned(we_again), g_hbm, g_hbm, ng_hbm, ni_hbm, no_hbm, x_got, idx_cf, idx_cl),
+        (wi_hbm, wo_hbm, pinned(we_got), pinned(we_again), ni_hbm, no_hbm, x_got, idx_cf, idx_cl),
         [whole((3, half, full)), whole((half, full))] + got_spec + [
-            fine_other, long_other, whole((nodes, half)),
             block((2, quarter, full), lambda i, s: (0, s[1], 0)), quarter_rows,
             pl.BlockSpec(memory_space=pl.ANY), whole((fine, 2)), whole((longs, 3)),
         ],
-        [((3, full, full), BF16), ((full, full), BF16), ((rows + nodes, half), BF16), ((3, quarter, full), BF16)],
+        [((3, full, full), BF16), ((full, full), BF16), ((3, quarter, full), BF16)],
         moved=7_000_000,
         name="edge_weights",
     )

time: 182 us -> 182 us (level)
    ppermute x3, starting transfers between devices: 6.77 us -> 10.3 us  [other_neighbour(): return lax.ppermute(value, ('patch', 'lat'), pairs)]
    ppermute x6, starting transfers between devices: 11.4 us -> 8.19 us  [swap_core(): return lax.ppermute(value, 'patch', [(i, i ^ 1) for i in range(count)])]
  transfers between devices with their start and end apart: 26 -> 26, of which waited for: 18 -> 16; matrix products, arithmetic and copies ran while one was open for 1% -> 1% of each run, Pallas kernels for 11% -> 12%
where the time goes in v6:
time: 182 us
  starting transfers between devices  68.5 us (38%)
  waiting for transfers between devices  66.7 us (37%)
  Pallas kernels  38.6 us (21%)
  local copies, waits for them, and re-layouts  4.27 us (2%)
  between operations  1.9 us (1%)
    ppermute x10, waiting for transfers between devices, swap_lat(): return lax.ppermute(value, 'lat', [(0, 1), (1, 0)])  38.1 us
    pallas_call x13, Pallas kernels, call(): pl.pallas_call(kernel, grid_spec=pltpu.PrefetchScalarGridSpec(num_scalar_...  34.5 us
    all_to_all x3, starting transfers between devices, chips_all_to_all(): lax.all_to_all(value, 'patch', 0, 0, tiled=True, axis_index_groups=groups)  32.7 us
    ppermute x4, starting transfers between devices, shifted(): lax.ppermute(value, 'patch', [(i, (i + steps) % count) for i in range(cou...  10.4 us
    ppermute x3, starting transfers between devices, other_neighbour(): return lax.ppermute(value, ('patch', 'lat'), pairs)  10.3 us
    ppermute x4, waiting for transfers between devices, shifted(): lax.ppermute(value, 'patch', [(i, (i + steps) % count) for i in range(cou...  8.74 us
    ppermute x6, starting transfers between devices, swap_core(): return lax.ppermute(value, 'patch', [(i, i ^ 1) for i in range(count)])  8.19 us
    ppermute x3, waiting for transfers between devices, other_neighbour(): return lax.ppermute(value, ('patch', 'lat'), pairs)  8.08 us
  transfers between devices with their start and end apart: 26, of which 16 were waited for; matrix products, arithmetic and copies ran while one was open for 1% of the time, Pallas kernels for 12%

profile of v6, /device:TPU:1, one launch (start us, length us, event | category | flops | bytes accessed | tf_op | source)
XLA Modules:
  0.0 181.7 jit_solution(1644509884017583111)
XLA Ops:
  1.3 2.0 %collective-permute-start.6 = (bf16[16,256]{1,0:T(8,128)(2,1)S(1)}, bf16[16,256]{1,0:T(8,128)(2,1)S(1)}, u32[]{:S(2)}, u32[]{:S(2)}) collective-permute-start(bf16[16,256]{1,0:T(8,128)(2,1)S(1)} %slice.78), channel_id=1, source_target_pairs={{0,1},{1,0},{2,3},{3,2},{4,5},{5,4},{6,7},{7,6},{8,9},{9,8},{10,11... | collective-permute-start | bytes 24584 | tf_op jit(solution)/shard_map/ppermute | solution.py:59
  3.4 2.7 %pack.1 = (bf16[960,256]{1,0:T(8,128)(2,1)S(1)}, bf16[960,256]{1,0:T(8,128)(2,1)}, bf16[4,128,512]{2,1,0:T(8,128)(2,1)S(1)}, bf16[32,256]{1,0:T(8,128)(2,1)S(1)}, bf16[32,256]{1,0:T(8,128)(2,1)S(1)}) custom-call(s32[2]{0:T(128)S(1)} %pad_add_fusion.2.info, bf16[1536,256]{1,0:T(8,128)(2,1)} %xl_own.1, bf16[1536,256]{1,0:T(8,128)(2,1)} %xl_own.1, ...), custom_call_target="tpu_custom_call" | custom-call | bytes 3000000 | tf_op jit(solution)/shard_map/pack/pallas_call | solution.py:96
  6.2 2.1 %coarse_rows.1 = bf16[64,8,512]{2,1,0:T(8,128)(2,1)} custom-call(s32[2]{0:T(128)S(1)} %pad_add_fusion.2.info, bf16[192,256]{1,0:T(8,128)(2,1)} %n_own.7, bf16[16,256]{1,0:T(8,128)(2,1)S(1)} %collective-permute-done.6.n_got, bf16[32,256]{1,0:T(8,128)(2,1)S(1)} %get-tuple-element.94.after), custom_call_target="tpu_custom_call" | custom-call | bytes 600000 | tf_op jit(solution)/shard_map/coarse_rows/pallas_call | solution.py:96
  8.3 14.0 %all-to-all-start = ((bf16[64,8,512]{2,1,0:T(8,128)(2,1)}), bf16[64,8,512]{2,1,0:T(8,128)(2,1)S(1)}, u32[]{:S(2)}, u32[]{:S(2)}) async-start(bf16[64,8,512]{2,1,0:T(8,128)(2,1)} %coarse_rows.1), calls=%async_computation | async-start | bytes 1048576 | tf_op jit(solution)/shard_map/all_to_all | solution.py:84
  22.3 2.0 %collective-permute-start.4 = (bf16[4,128,512]{2,1,0:T(8,128)(2,1)S(1)}, bf16[4,128,512]{2,1,0:T(8,128)(2,1)S(1)}, u32[]{:S(2)}, u32[]{:S(2)}) collective-permute-start(bf16[4,128,512]{2,1,0:T(8,128)(2,1)S(1)} %get-tuple-element.95), channel_id=1, source_target_pairs={{0,5},{1,4},{2,7},{3,6},{4,1},{5,0},{6,3},{7,2},{8,13},{9,12},{10,... | collective-permute-start | bytes 1572872 | tf_op jit(solution)/shard_map/ppermute | solution.py:78
  24.2 2.1 %collective-permute-start.1 = (bf16[32,256]{1,0:T(8,128)(2,1)S(1)}, bf16[32,256]{1,0:T(8,128)(2,1)S(1)}, u32[]{:S(2)}, u32[]{:S(2)}) collective-permute-start(bf16[32,256]{1,0:T(8,128)(2,1)S(1)} %get-tuple-element.93), channel_id=1, source_target_pairs={{0,2},{2,4},{4,6},{6,8},{8,10},{10,12},{12,14},{14,16},{16,18},{18... | collective-permute-start | bytes 49160 | tf_op jit(solution)/shard_map/ppermute | solution.py:69
  27.2 4.2 %collective-permute-done.2.high = bf16[32,256]{1,0:T(8,128)(2,1)S(1)} collective-permute-done((bf16[32,256]{1,0:T(8,128)(2,1)S(1)}, bf16[32,256]{1,0:T(8,128)(2,1)S(1)}, u32[]{:S(2)}, u32[]{:S(2)}) %collective-permute-start.2) | collective-permute-done | bytes 16416 | tf_op jit(solution)/shard_map/ppermute | solution.py:69
  34.8 7.0 %collective-permute-done.4.value = bf16[4,128,512]{2,1,0:T(8,128)(2,1)S(1)} collective-permute-done((bf16[4,128,512]{2,1,0:T(8,128)(2,1)S(1)}, bf16[4,128,512]{2,1,0:T(8,128)(2,1)S(1)}, u32[]{:S(2)}, u32[]{:S(2)}) %collective-permute-start.4) | collective-permute-done | bytes 524320 | tf_op jit(solution)/shard_map/ppermute | solution.py:78
  42.4 1.8 collective-permute-start.5
  46.3 2.4 %edge_weights.1 = (bf16[3,512,512]{2,1,0:T(8,128)(2,1)S(1)}, bf16[512,512]{1,0:T(8,128)(2,1)S(1)}, bf16[3,128,512]{2,1,0:T(8,128)(2,1)S(1)}) custom-call(s32[2]{0:T(128)S(1)} %pad_add_fusion.2.info, bf16[3,256,512]{2,1,0:T(8,128)(2,1)} %wi.4, bf16[256,512]{1,0:T(8,128)(2,1)} %wo.4, bf16[4,128,512]{2,1,0:T(8,128)(2,1)} %copy-done, ...), custom_call_target="tpu_custom_call" | custom-call | bytes 7000000 | tf_op jit(solution)/shard_map/edge_weights/pallas_call | solution.py:96
  48.7 6.6 %collective-permute-start.12 = (bf16[3,128,512]{2,1,0:T(8,128)(2,1)S(1)}, bf16[3,128,512]{2,1,0:T(8,128)(2,1)S(1)}, u32[]{:S(2)}, u32[]{:S(2)}) collective-permute-start(bf16[3,128,512]{2,1,0:T(8,128)(2,1)S(1)} %get-tuple-element.107), channel_id=1, source_target_pairs={{0,5},{1,4},{2,7},{3,6},{4,1},{5,0},{6,3},{7,2},{8,13},{9,12},{10,... | collective-permute-start | bytes 1179656 | tf_op jit(solution)/shard_map/ppermute | solution.py:78
  55.3 4.4 %edges_forward_fine.1 = (f32[576,512]{1,0:T(8,128)S(1)}, bf16[576,512]{1,0:T(8,128)(2,1)S(1)}, f32[576,512]{1,0:T(8,128)S(1)}, f32[576,1]{1,0:T(8,128)S(1)}, bf1...) custom-call(s32[2]{0:T(128)S(1)} %pad_add_fusion.2.info, ...), custom_call_target="tpu_custom_call" | custom-call | flops 1585446912 | bytes 8000000 | tf_op jit(solution)/shard_map/edges_forward_fine/pallas_call | solution.py:96
  60.1 3.1 %edges_forward_long.1 = (f32[192,512]{1,0:T(8,128)S(1)}, bf16[192,512]{1,0:T(8,128)(2,1)S(1)}, f32[192,512]{1,0:T(8,128)S(1)}, f32[192,1]{1,0:T(8,128)S(1)}, bf1...) custom-call(s32[2]{0:T(128)S(1)} %pad_add_fusion.2.info, ...), custom_call_target="tpu_custom_call" | custom-call | flops 1283457024 | bytes 6000000 | tf_op jit(solution)/shard_map/edges_forward_long/pallas_call | solution.py:96
  63.2 3.2 %collective-permute-done.10.rest_1_.got = bf16[192,512]{1,0:T(8,128)(2,1)S(1)} collective-permute-done((bf16[192,512]{1,0:T(8,128)(2,1)S(1)}, bf16[192,512]{1,0:T(8,128)(2,1)S(1)}, u32[]{:S(2)}, u32[]{:S(2)}) %collective-permute-start.10) | collective-permute-done | bytes 196640 | tf_op jit(solution)/shard_map/ppermute | solution.py:59
  69.2 1.8 %node_weights.1 = (bf16[2,512,512]{2,1,0:T(8,128)(2,1)S(1)}, bf16[512,512]{1,0:T(8,128)(2,1)S(1)}) custom-call(s32[2]{0:T(128)S(1)} %pad_add_fusion.2.info, bf16[2,256,512]{2,1,0:T(8,128)(2,1)} %wi.5, bf16[256,512]{1,0:T(8,128)(2,1)} %wo.5, bf16[3,128,512]{2,1,0:T(8,128)(2,1)S(1)} %gate.4.got, bf16[3,128,512]{2,1,0:T(8,128)(2,1)S(1)} %collective-permute-done.13.again), custom_call_target="tpu_custom_call" | custom-call | bytes 3000000 | tf_op jit(solution)/shard_map/node_weights/pallas_call | solution.py:96
  71.1 8.3 %nodes_and_edges_backward.1 = (bf16[192,256]{1,0:T(8,128)(2,1)}, f32[192,256]{1,0:T(8,128)S(1)}, bf16[1536,256]{1,0:T(8,128)(2,1)S(1)}, bf16[1536,256]{1,0:T(8,1...) custom-call(s32[2]{0:T(128)S(1)} %pad_add_fusion.2.info, ...), custom_call_target="tpu_custom_call" | custom-call | flops 1610612736 | bytes 14000000 | tf_op jit(solution)/shard_map/nodes_and_edges_backward/pallas_call | solution.py:96
  80.3 1.8 collective-permute-done.19.got
  84.9 8.4 %collective-permute-done.20.first = bf16[768,256]{1,0:T(8,128)(2,1)S(1)} collective-permute-done((bf16[768,256]{1,0:T(8,128)(2,1)S(1)}, bf16[768,256]{1,0:T(8,128)(2,1)S(1)}, u32[]{:S(2)}, u32[]{:S(2)}) %collective-permute-start.20) | collective-permute-done | bytes 393248 | tf_op jit(solution)/shard_map/ppermute | solution.py:59
  94.4 2.0 %combine.1 = bf16[64,72,128]{2,1,0:T(8,128)(2,1)} custom-call(s32[2]{0:T(128)S(1)} %pad_add_fusion.2.info, bf16[2304,256]{1,0:T(8,128)(2,1)S(1)} %get-tuple-element.128.keep, bf16[2304,256]{1,0:T(8,128)(2,1)S(1)} %collective-permute-done.18.got, bf16[768,256]{1,0:T(8,128)(2,1)S(1)} %collective-permute-done.20.first, ...), custom_call_target="tpu_custom_call" | custom-call | bytes 4300000 | tf_op jit(solution)/shard_map/combine/pallas_call | solution.py:96
  96.4 9.7 %all-to-all-start.1 = ((bf16[64,72,128]{2,1,0:T(8,128)(2,1)}), bf16[64,72,128]{2,1,0:T(8,128)(2,1)S(1)}, u32[]{:S(2)}, u32[]{:S(2)}) async-start(bf16[64,72,128]{2,1,0:T(8,128)(2,1)} %combine.1), calls=%async_computation.1 | async-start | bytes 2359296 | tf_op jit(solution)/shard_map/all_to_all | solution.py:84
  106.1 2.9 %input_gradients.1 = (bf16[768,256]{1,0:T(8,128)(2,1)S(1)}, bf16[768,256]{1,0:T(8,128)(2,1)S(1)}, f32[256,256]{1,0:T(8,128)S(1)}, bf16[256,256]{1,0:T(8,128)(2,1)S(1)}) custom-call(s32[2]{0:T(128)S(1)} %pad_add_fusion.2.info, bf16[768,512]{1,0:T(8,128)(2,1)} %copy-done.4, bf16[1536,256]{1,0:T(8,128)(2,1)} %gl_own.3, bf16[1536,256]{1,0:T(8,128)(2,1)} %gl_own.3, ...), custom_call_target="tpu_custom_call" | custom-call | flops 805306368 | bytes 5000000 | tf_op jit(solution)/shard_map/input_gradients/pallas_call | solution.py:96
  112.1 3.4 %collective-permute-done.15 = bf16[256,256]{1,0:T(8,128)(2,1)S(1)} collective-permute-done((bf16[256,256]{1,0:T(8,128)(2,1)S(1)}, bf16[256,256]{1,0:T(8,128)(2,1)S(1)}, u32[]{:S(2)}, u32[]{:S(2)}) %collective-permute-start.15) | collective-permute-done | bytes 131104 | tf_op jit(solution)/shard_map/ppermute | solution.py:59
  116.2 5.5 %collective-permute-start.16 = (bf16[32,256]{1,0:T(8,128)(2,1)S(1)}, bf16[32,256]{1,0:T(8,128)(2,1)S(1)}, u32[]{:S(2)}, u32[]{:S(2)}) collective-permute-start(bf16[32,256]{1,0:T(8,128)(2,1)S(1)} %get-tuple-element.145), channel_id=1, source_target_pairs={{0,254},{2,0},{4,2},{6,4},{8,6},{10,8},{12,10},{14,12},{16,14},{18... | collective-permute-start | bytes 49160 | tf_op jit(solution)/shard_map/ppermute | solution.py:69
  121.7 2.7 %collective-permute-start.17 = (bf16[32,256]{1,0:T(8,128)(2,1)S(1)}, bf16[32,256]{1,0:T(8,128)(2,1)S(1)}, u32[]{:S(2)}, u32[]{:S(2)}) collective-permute-start(bf16[32,256]{1,0:T(8,128)(2,1)S(1)} %get-tuple-element.144), channel_id=1, source_target_pairs={{0,2},{2,4},{4,6},{6,8},{8,10},{10,12},{12,14},{14,16},{16,18},{18... | collective-permute-start | bytes 49160 | tf_op jit(solution)/shard_map/ppermute | solution.py:69
  124.4 6.5 %collective-permute-done.9.got = bf16[768,256]{1,0:T(8,128)(2,1)S(1)} collective-permute-done((bf16[768,256]{1,0:T(8,128)(2,1)S(1)}, bf16[768,256]{1,0:T(8,128)(2,1)S(1)}, u32[]{:S(2)}, u32[]{:S(2)}) %collective-permute-start.9) | collective-permute-done | bytes 393248 | tf_op jit(solution)/shard_map/ppermute | solution.py:59
  132.4 3.6 %collective-permute-done.16 = bf16[32,256]{1,0:T(8,128)(2,1)S(1)} collective-permute-done((bf16[32,256]{1,0:T(8,128)(2,1)S(1)}, bf16[32,256]{1,0:T(8,128)(2,1)S(1)}, u32[]{:S(2)}, u32[]{:S(2)}) %collective-permute-start.16) | collective-permute-done | bytes 16416 | tf_op jit(solution)/shard_map/ppermute | solution.py:69
  138.7 9.0 %all-to-all-start.2 = ((bf16[64,56,128]{2,1,0:T(8,128)(2,1)}), bf16[64,56,128]{2,1,0:T(8,128)(2,1)S(1)}, u32[]{:S(2)}, u32[]{:S(2)}) async-start(bf16[64,56,128]{2,1,0:T(8,128)(2,1)} %copy-done.3), calls=%async_computation.2 | async-start | bytes 1835008 | tf_op jit(solution)/shard_map/all_to_all | solution.py:84
  148.4 15.2 %collective-permute-done.14.got = bf16[768,256]{1,0:T(8,128)(2,1)S(1)} collective-permute-done((bf16[768,256]{1,0:T(8,128)(2,1)S(1)}, bf16[768,256]{1,0:T(8,128)(2,1)S(1)}, u32[]{:S(2)}, u32[]{:S(2)}) %collective-permute-start.14) | collective-permute-done | bytes 393248 | tf_op jit(solution)/shard_map/ppermute | solution.py:59
  165.7 6.3 %all-to-all-done.2.value = bf16[64,56,128]{2,1,0:T(8,128)(2,1)S(1)} async-done(((bf16[64,56,128]{2,1,0:T(8,128)(2,1)}), bf16[64,56,128]{2,1,0:T(8,128)(2,1)S(1)}, u32[]{:S(2)}, u32[]{:S(2)}) %all-to-all-start.2) | async-done | bytes 917536 | tf_op jit(solution)/shard_map/all_to_all | solution.py:84
  172.5 4.4 %collective-permute-start.22 = (bf16[2,1792,128]{2,1,0:T(8,128)(2,1)S(1)}, bf16[2,1792,128]{2,1,0:T(8,128)(2,1)S(1)}, u32[]{:S(2)}, u32[]{:S(2)}) collective-permute-start(bf16[2,1792,128]{2,1,0:T(8,128)(2,1)S(1)} %bitcast.15), channel_id=1, source_target_pairs={{0,2},{2,0},{4,6},{6,4},{8,10},{10,8},{12,14},{14,12},{16,18},{18,... | collective-permute-start | bytes 2752520 | tf_op jit(solution)/shard_map/ppermute | solution.py:64
  176.9 2.1 %collective-permute-done.22.other = bf16[2,1792,128]{2,1,0:T(8,128)(2,1)S(1)} collective-permute-done((bf16[2,1792,128]{2,1,0:T(8,128)(2,1)S(1)}, bf16[2,1792,128]{2,1,0:T(8,128)(2,1)S(1)}, u32[]{:S(2)}, u32[]{:S(2)}) %collective-permute-start.22) | collective-permute-done | bytes 917536 | tf_op jit(solution)/shard_map/ppermute | solution.py:64
  179.0 2.5 %results.1 = (f32[3,256,512]{2,1,0:T(8,128)}, f32[256,512]{1,0:T(8,128)}, f32[2,256,512]{2,1,0:T(8,128)}, f32[256,512]{1,0:T(8,128)}) custom-call(s32[2]{0:T(128)S(1)} %pad_add_fusion.2.info, bf16[2,1792,128]{2,1,0:T(8,128)(2,1)S(1)} %bitcast.16, bf16[2,1792,128]{2,1,0:T(8,128)(2,1)S(1)} %collective-permute-done.22.other), custom_call_target="tpu_custom_call" | custom-call | bytes 6000000 | tf_op jit(solution)/shard_map/results/pallas_call | solution.py:759
  (110 shorter events, 26.0 us)
Async XLA Ops:
  1.3 4.8 %collective-permute-start.6 = (bf16[16,256]{1,0:T(8,128)(2,1)S(1)}, bf16[16,256]{1,0:T(8,128)(2,1)S(1)}, u32[]{:S(2)}, u32[]{:S(2)}) collective-permute-start(bf16[16,256]{1,0:T(8,128)(2,1)S(1)} %slice.78), channel_id=1, source_target_pairs={{0,1},{1,0},{2,3},{3,2},{4,5},{5,4},{6,7},{7,6},{8,9},{9,8},{10,11... | collective-permute-start | bytes 24584 | tf_op jit(solution)/shard_map/ppermute | solution.py:59
  8.2 35.9 %copy-start.23 = (s32[12,128]{1,0:T(8,128)S(1)}, s32[12,128]{1,0:T(8,128)}, u32[]{:S(2)}) copy-start(s32[12,128]{1,0:T(8,128)} %param.19) | copy-start | bytes 18436
  8.2 35.9 %copy-start.24 = (s32[12,128]{1,0:T(8,128)S(1)}, s32[12,128]{1,0:T(8,128)}, u32[]{:S(2)}) copy-start(s32[12,128]{1,0:T(8,128)} %param.20) | copy-start | bytes 18436
  8.3 36.8 %all-to-all-start = ((bf16[64,8,512]{2,1,0:T(8,128)(2,1)}), bf16[64,8,512]{2,1,0:T(8,128)(2,1)S(1)}, u32[]{:S(2)}, u32[]{:S(2)}) async-start(bf16[64,8,512]{2,1,0:T(8,128)(2,1)} %coarse_rows.1), calls=%async_computation | async-start | bytes 1048576 | tf_op jit(solution)/shard_map/all_to_all | solution.py:84
  22.3 19.6 %collective-permute-start.4 = (bf16[4,128,512]{2,1,0:T(8,128)(2,1)S(1)}, bf16[4,128,512]{2,1,0:T(8,128)(2,1)S(1)}, u32[]{:S(2)}, u32[]{:S(2)}) collective-permute-start(bf16[4,128,512]{2,1,0:T(8,128)(2,1)S(1)} %get-tuple-element.95), channel_id=1, source_target_pairs={{0,5},{1,4},{2,7},{3,6},{4,1},{5,0},{6,3},{7,2},{8,13},{9,12},{10,... | collective-permute-start | bytes 1572872 | tf_op jit(solution)/shard_map/ppermute | solution.py:78
  24.2 3.0 %collective-permute-start.1 = (bf16[32,256]{1,0:T(8,128)(2,1)S(1)}, bf16[32,256]{1,0:T(8,128)(2,1)S(1)}, u32[]{:S(2)}, u32[]{:S(2)}) collective-permute-start(bf16[32,256]{1,0:T(8,128)(2,1)S(1)} %get-tuple-element.93), channel_id=1, source_target_pairs={{0,2},{2,4},{4,6},{6,8},{8,10},{10,12},{12,14},{14,16},{16,18},{18... | collective-permute-start | bytes 49160 | tf_op jit(solution)/shard_map/ppermute | solution.py:69
  26.4 5.1 %collective-permute-start.2 = (bf16[32,256]{1,0:T(8,128)(2,1)S(1)}, bf16[32,256]{1,0:T(8,128)(2,1)S(1)}, u32[]{:S(2)}, u32[]{:S(2)}) collective-permute-start(bf16[32,256]{1,0:T(8,128)(2,1)S(1)} %get-tuple-element.94.after), channel_id=1, source_target_pairs={{0,254},{2,0},{4,2},{6,4},{8,6},{10,8},{12,10},{14,12},{16,14},{18... | collective-permute-start | bytes 49160 | tf_op jit(solution)/shard_map/ppermute | solution.py:69
  27.2 18.0 %copy-start.15 = (bf16[32,256]{1,0:T(8,128)(2,1)}, bf16[32,256]{1,0:T(8,128)(2,1)S(1)}, u32[]{:S(2)}) copy-start(bf16[32,256]{1,0:T(8,128)(2,1)S(1)} %collective-permute-done.1.low) | copy-start | bytes 49156
  31.5 3.3 %collective-permute-start.3 = (bf16[64,256]{1,0:T(8,128)(2,1)S(1)}, bf16[64,256]{1,0:T(8,128)(2,1)S(1)}, u32[]{:S(2)}, u32[]{:S(2)}) collective-permute-start(bf16[64,256]{1,0:T(8,128)(2,1)S(1)} %pad_maximum_fusion.1), channel_id=1, source_target_pairs={{0,1},{1,0},{2,3},{3,2},{4,5},{5,4},{6,7},{7,6},{8,9},{9,8},{10,11... | collective-permute-start | bytes 98312 | tf_op jit(solution)/shard_map/ppermute | solution.py:59
  32.0 13.6 %collective-permute-start = (bf16[960,256]{1,0:T(8,128)(2,1)S(1)}, bf16[960,256]{1,0:T(8,128)(2,1)S(1)}, u32[]{:S(2)}, u32[]{:S(2)}) collective-permute-start(bf16[960,256]{1,0:T(8,128)(2,1)S(1)} %get-tuple-element.92), channel_id=1, source_target_pairs={{0,1},{1,0},{2,3},{3,2},{4,5},{5,4},{6,7},{7,6},{8,9},{9,8},{10,11... | collective-permute-start | bytes 1474568 | tf_op jit(solution)/shard_map/ppermute | solution.py:59
  32.9 27.1 %collective-permute-start.8 = (bf16[960,256]{1,0:T(8,128)(2,1)}, bf16[960,256]{1,0:T(8,128)(2,1)S(1)}, u32[]{:S(2)}, u32[]{:S(2)}) collective-permute-start(bf16[960,256]{1,0:T(8,128)(2,1)} %get-tuple-element.99), channel_id=1, source_target_pairs={{0,1},{1,0},{2,3},{3,2},{4,5},{5,4},{6,7},{7,6},{8,9},{9,8},{10,11... | collective-permute-start | bytes 1474568 | tf_op jit(solution)/shard_map/ppermute | solution.py:59
  42.4 4.0 %collective-permute-start.5 = (bf16[4,128,512]{2,1,0:T(8,128)(2,1)S(1)}, bf16[4,128,512]{2,1,0:T(8,128)(2,1)}, u32[]{:S(2)}, u32[]{:S(2)}) collective-permute-start(bf16[4,128,512]{2,1,0:T(8,128)(2,1)S(1)} %gate.3.got), channel_id=1, source_target_pairs={{0,2},{2,0},{4,6},{6,4},{8,10},{10,8},{12,14},{14,12},{16,18},{18,... | collective-permute-start | bytes 1572872 | tf_op jit(solution)/shard_map/ppermute | solution.py:64
  45.0 15.0 %collective-permute-start.7 = (bf16[64,8,512]{2,1,0:T(8,128)(2,1)S(1)}, bf16[64,8,512]{2,1,0:T(8,128)(2,1)}, u32[]{:S(2)}, u32[]{:S(2)}) collective-permute-start(bf16[64,8,512]{2,1,0:T(8,128)(2,1)S(1)} %all-to-all-done), channel_id=1, source_target_pairs={{0,2},{2,0},{4,6},{6,4},{8,10},{10,8},{12,14},{14,12},{16,18},{18,... | collective-permute-start | bytes 1572872 | tf_op jit(solution)/shard_map/ppermute | solution.py:64
  48.7 17.6 %collective-permute-start.12 = (bf16[3,128,512]{2,1,0:T(8,128)(2,1)S(1)}, bf16[3,128,512]{2,1,0:T(8,128)(2,1)S(1)}, u32[]{:S(2)}, u32[]{:S(2)}) collective-permute-start(bf16[3,128,512]{2,1,0:T(8,128)(2,1)S(1)} %get-tuple-element.107), channel_id=1, source_target_pairs={{0,5},{1,4},{2,7},{3,6},{4,1},{5,0},{6,3},{7,2},{8,13},{9,12},{10,... | collective-permute-start | bytes 1179656 | tf_op jit(solution)/shard_map/ppermute | solution.py:78
  59.8 6.6 %collective-permute-start.10 = (bf16[192,512]{1,0:T(8,128)(2,1)S(1)}, bf16[192,512]{1,0:T(8,128)(2,1)S(1)}, u32[]{:S(2)}, u32[]{:S(2)}) collective-permute-start(bf16[192,512]{1,0:T(8,128)(2,1)S(1)} %get-tuple-element.104), channel_id=1, source_target_pairs={{0,1},{1,0},{2,3},{3,2},{4,5},{5,4},{6,7},{7,6},{8,9},{9,8},{10,11... | collective-permute-start | bytes 589832 | tf_op jit(solution)/shard_map/ppermute | solution.py:59
  66.9 2.3 %collective-permute-start.13 = (bf16[3,128,512]{2,1,0:T(8,128)(2,1)S(1)}, bf16[3,128,512]{2,1,0:T(8,128)(2,1)S(1)}, u32[]{:S(2)}, u32[]{:S(2)}) collective-permute-start(bf16[3,128,512]{2,1,0:T(8,128)(2,1)S(1)} %gate.4.got), channel_id=1, source_target_pairs={{0,2},{2,0},{4,6},{6,4},{8,10},{10,8},{12,14},{14,12},{16,18},{18,... | collective-permute-start | bytes 1179656 | tf_op jit(solution)/shard_map/ppermute | solution.py:64
  67.9 3.2 %collective-permute-start.11 = (bf16[16,512]{1,0:T(8,128)(2,1)S(1)}, bf16[16,512]{1,0:T(8,128)(2,1)S(1)}, u32[]{:S(2)}, u32[]{:S(2)}) collective-permute-start(bf16[16,512]{1,0:T(8,128)(2,1)S(1)} %get-tuple-element.106.rest_0_), channel_id=1, source_target_pairs={{0,1},{1,0},{2,3},{3,2},{4,5},{5,4},{6,7},{7,6},{8,9},{9,8},{10,11... | collective-permute-start | bytes 49160 | tf_op jit(solution)/shard_map/ppermute | solution.py:59
  79.4 15.0 %copy-start.11 = (f32[192,256]{1,0:T(8,128)}, f32[192,256]{1,0:T(8,128)S(1)}, u32[]{:S(2)}) copy-start(f32[192,256]{1,0:T(8,128)S(1)} %get-tuple-element.125) | copy-start | bytes 589828
  79.4 2.7 %collective-permute-start.19 = (bf16[1536,256]{1,0:T(8,128)(2,1)S(1)}, bf16[1536,256]{1,0:T(8,128)(2,1)S(1)}, u32[]{:S(2)}, u32[]{:S(2)}) collective-permute-start(bf16[1536,256]{1,0:T(8,128)(2,1)S(1)} %get-tuple-element.131), channel_id=1, source_target_pairs={{0,2},{2,0},{4,6},{6,4},{8,10},{10,8},{12,14},{14,12},{16,18},{18,... | collective-permute-start | bytes 2359304 | tf_op jit(solution)/shard_map/ppermute | solution.py:64
  80.2 14.1 %collective-permute-start.18 = (bf16[2304,256]{1,0:T(8,128)(2,1)S(1)}, bf16[2304,256]{1,0:T(8,128)(2,1)S(1)}, u32[]{:S(2)}, u32[]{:S(2)}) collective-permute-start(bf16[2304,256]{1,0:T(8,128)(2,1)S(1)} %get-tuple-element.129), channel_id=1, source_target_pairs={{0,2},{2,0},{4,6},{6,4},{8,10},{10,8},{12,14},{14,12},{16,18},{18,... | collective-permute-start | bytes 3538952 | tf_op jit(solution)/shard_map/ppermute | solution.py:64
  82.9 10.4 %collective-permute-start.20 = (bf16[768,256]{1,0:T(8,128)(2,1)S(1)}, bf16[768,256]{1,0:T(8,128)(2,1)S(1)}, u32[]{:S(2)}, u32[]{:S(2)}) collective-permute-start(bf16[768,256]{1,0:T(8,128)(2,1)S(1)} %get-tuple-element.132), channel_id=1, source_target_pairs={{0,1},{1,0},{2,3},{3,2},{4,5},{5,4},{6,7},{7,6},{8,9},{9,8},{10,11... | collective-permute-start | bytes 1179656 | tf_op jit(solution)/shard_map/ppermute | solution.py:59
  83.2 11.2 %collective-permute-start.21 = (bf16[768,256]{1,0:T(8,128)(2,1)S(1)}, bf16[768,256]{1,0:T(8,128)(2,1)S(1)}, u32[]{:S(2)}, u32[]{:S(2)}) collective-permute-start(bf16[768,256]{1,0:T(8,128)(2,1)S(1)} %get-tuple-element.133), channel_id=1, source_target_pairs={{0,5},{1,4},{2,7},{3,6},{4,1},{5,0},{6,3},{7,2},{8,13},{9,12},{10,... | collective-permute-start | bytes 1179656 | tf_op jit(solution)/shard_map/ppermute | solution.py:78
  96.4 40.1 %all-to-all-start.1 = ((bf16[64,72,128]{2,1,0:T(8,128)(2,1)}), bf16[64,72,128]{2,1,0:T(8,128)(2,1)S(1)}, u32[]{:S(2)}, u32[]{:S(2)}) async-start(bf16[64,72,128]{2,1,0:T(8,128)(2,1)} %combine.1), calls=%async_computation.1 | async-start | bytes 2359296 | tf_op jit(solution)/shard_map/all_to_all | solution.py:84
  110.5 20.5 %copy-start.8 = (bf16[576,256]{1,0:T(8,128)(2,1)S(1)}, bf16[576,256]{1,0:T(8,128)(2,1)}, u32[]{:S(2)}) copy-start(bf16[576,256]{1,0:T(8,128)(2,1)} %copy-done.7) | copy-start | bytes 884740
  110.5 5.0 %collective-permute-start.15 = (bf16[256,256]{1,0:T(8,128)(2,1)S(1)}, bf16[256,256]{1,0:T(8,128)(2,1)S(1)}, u32[]{:S(2)}, u32[]{:S(2)}) collective-permute-start(bf16[256,256]{1,0:T(8,128)(2,1)S(1)} %get-tuple-element.127), channel_id=1, source_target_pairs={{0,1},{1,0},{2,3},{3,2},{4,5},{5,4},{6,7},{7,6},{8,9},{9,8},{10,11... | collective-permute-start | bytes 393224 | tf_op jit(solution)/shard_map/ppermute | solution.py:59
  111.5 19.4 %collective-permute-start.9 = (bf16[768,256]{1,0:T(8,128)(2,1)S(1)}, bf16[768,256]{1,0:T(8,128)(2,1)S(1)}, u32[]{:S(2)}, u32[]{:S(2)}) collective-permute-start(bf16[768,256]{1,0:T(8,128)(2,1)S(1)} %pad_maximum_fusion), channel_id=1, source_target_pairs={{0,1},{1,0},{2,3},{3,2},{4,5},{5,4},{6,7},{7,6},{8,9},{9,8},{10,11... | collective-permute-start | bytes 1179656 | tf_op jit(solution)/shard_map/ppermute | solution.py:59
  116.2 19.9 %collective-permute-start.16 = (bf16[32,256]{1,0:T(8,128)(2,1)S(1)}, bf16[32,256]{1,0:T(8,128)(2,1)S(1)}, u32[]{:S(2)}, u32[]{:S(2)}) collective-permute-start(bf16[32,256]{1,0:T(8,128)(2,1)S(1)} %get-tuple-element.145), channel_id=1, source_target_pairs={{0,254},{2,0},{4,2},{6,4},{8,6},{10,8},{12,10},{14,12},{16,14},{18... | collective-permute-start | bytes 49160 | tf_op jit(solution)/shard_map/ppermute | solution.py:69
  121.7 14.4 %collective-permute-start.17 = (bf16[32,256]{1,0:T(8,128)(2,1)S(1)}, bf16[32,256]{1,0:T(8,128)(2,1)S(1)}, u32[]{:S(2)}, u32[]{:S(2)}) collective-permute-start(bf16[32,256]{1,0:T(8,128)(2,1)S(1)} %get-tuple-element.144), channel_id=1, source_target_pairs={{0,2},{2,4},{4,6},{6,8},{8,10},{10,12},{12,14},{14,16},{16,18},{18... | collective-permute-start | bytes 49160 | tf_op jit(solution)/shard_map/ppermute | solution.py:69
  138.7 24.9 %copy-start.2 = (bf16[768,256]{1,0:T(8,128)(2,1)S(1)}, bf16[768,256]{1,0:T(8,128)(2,1)}, u32[]{:S(2)}) copy-start(bf16[768,256]{1,0:T(8,128)(2,1)} %copy-done.1) | copy-start | bytes 1179652
  138.7 33.3 %all-to-all-start.2 = ((bf16[64,56,128]{2,1,0:T(8,128)(2,1)}), bf16[64,56,128]{2,1,0:T(8,128)(2,1)S(1)}, u32[]{:S(2)}, u32[]{:S(2)}) async-start(bf16[64,56,128]{2,1,0:T(8,128)(2,1)} %copy-done.3), calls=%async_computation.2 | async-start | bytes 1835008 | tf_op jit(solution)/shard_map/all_to_all | solution.py:84
  147.7 15.9 %collective-permute-start.14 = (bf16[768,256]{1,0:T(8,128)(2,1)S(1)}, bf16[768,256]{1,0:T(8,128)(2,1)S(1)}, u32[]{:S(2)}, u32[]{:S(2)}) collective-permute-start(bf16[768,256]{1,0:T(8,128)(2,1)S(1)} %copy-done.20), channel_id=1, source_target_pairs={{0,1},{1,0},{2,3},{3,2},{4,5},{5,4},{6,7},{7,6},{8,9},{9,8},{10,11... | collective-permute-start | bytes 1179656 | tf_op jit(solution)/shard_map/ppermute | solution.py:59
  172.5 6.5 %collective-permute-start.22 = (bf16[2,1792,128]{2,1,0:T(8,128)(2,1)S(1)}, bf16[2,1792,128]{2,1,0:T(8,128)(2,1)S(1)}, u32[]{:S(2)}, u32[]{:S(2)}) collective-permute-start(bf16[2,1792,128]{2,1,0:T(8,128)(2,1)S(1)} %bitcast.15), channel_id=1, source_target_pairs={{0,2},{2,0},{4,6},{6,4},{8,10},{10,8},{12,14},{14,12},{16,18},{18,... | collective-permute-start | bytes 2752520 | tf_op jit(solution)/shard_map/ppermute | solution.py:64
  (19 other events, 139.3 us)

commit v7 on v6

--- a/solution.py
+++ b/solution.py
@@ -521,7 +521,7 @@
         in_hbm=(0,),
     )
     same = chips_all_to_all(sent_coarse)
-    rims_got = swap_lat(jnp.concatenate([low, high], 0))
+    rims_got = swap_lat(gated(info, jnp.concatenate([low, high], 0), (x_got,)))
     we_got = gated(info, we_got, (rims_got,))
     we_again = swap_core(we_got)
 

time: 182 us -> 181 us (level)
  starting transfers between devices: 68.5 us -> 63.1 us
  waiting for transfers between devices: 66.7 us -> 70.3 us
    ppermute x4, waiting for transfers between devices: 8.74 us -> 19.2 us  [shifted(): lax.ppermute(value, 'patch', [(i, (i + steps) % count) for i in range(cou...]
    ppermute x3, waiting for transfers between devices: 8.08 us -> 1.39 us  [other_neighbour(): return lax.ppermute(value, ('patch', 'lat'), pairs)]
    ppermute x3, starting transfers between devices: 10.3 us -> 5.4 us  [other_neighbour(): return lax.ppermute(value, ('patch', 'lat'), pairs)]
  transfers between devices with their start and end apart: 26 -> 26, of which waited for: 16 -> 17; matrix products, arithmetic and copies ran while one was open for 1% -> 1% of each run, Pallas kernels for 12% -> 12%
where the time goes in v7:
time: 181 us
  waiting for transfers between devices  70.3 us (39%)
  starting transfers between devices  63.1 us (35%)
  Pallas kernels  39.2 us (22%)
  local copies, waits for them, and re-layouts  4.26 us (2%)
  between operations  1.94 us (1%)
    ppermute x10, waiting for transfers between devices, swap_lat(): return lax.ppermute(value, 'lat', [(0, 1), (1, 0)])  37.1 us
    pallas_call x13, Pallas kernels, call(): pl.pallas_call(kernel, grid_spec=pltpu.PrefetchScalarGridSpec(num_scalar_...  34.5 us
    all_to_all x3, starting transfers between devices, chips_all_to_all(): lax.all_to_all(value, 'patch', 0, 0, tiled=True, axis_index_groups=groups)  33.1 us
    ppermute x4, waiting for transfers between devices, shifted(): lax.ppermute(value, 'patch', [(i, (i + steps) % count) for i in range(cou...  19.2 us
    ppermute x4, starting transfers between devices, shifted(): lax.ppermute(value, 'patch', [(i, (i + steps) % count) for i in range(cou...  10.6 us
    ppermute x6, starting transfers between devices, swap_core(): return lax.ppermute(value, 'patch', [(i, i ^ 1) for i in range(count)])  7.34 us
    all_to_all x3, waiting for transfers between devices, chips_all_to_all(): lax.all_to_all(value, 'patch', 0, 0, tiled=True, axis_index_groups=groups)  6.83 us
    ppermute x10, starting transfers between devices, swap_lat(): return lax.ppermute(value, 'lat', [(0, 1), (1, 0)])  6.75 us
  transfers between devices with their start and end apart: 26, of which 17 were waited for; matrix products, arithmetic and copies ran while one was open for 1% of the time, Pallas kernels for 12%

profile of v7, /device:TPU:1, one launch (start us, length us, event | category | flops | bytes accessed | tf_op | source)
XLA Modules:
  0.0 180.6 jit_solution(13901045309722830756)
XLA Ops:
  1.3 2.0 %collective-permute-start.6 = (bf16[16,256]{1,0:T(8,128)(2,1)S(1)}, bf16[16,256]{1,0:T(8,128)(2,1)S(1)}, u32[]{:S(2)}, u32[]{:S(2)}) collective-permute-start(bf16[16,256]{1,0:T(8,128)(2,1)S(1)} %slice.78), channel_id=1, source_target_pairs={{0,1},{1,0},{2,3},{3,2},{4,5},{5,4},{6,7},{7,6},{8,9},{9,8},{10,11... | collective-permute-start | bytes 24584 | tf_op jit(solution)/shard_map/ppermute | solution.py:59
  3.4 2.7 %pack.1 = (bf16[960,256]{1,0:T(8,128)(2,1)S(1)}, bf16[960,256]{1,0:T(8,128)(2,1)}, bf16[4,128,512]{2,1,0:T(8,128)(2,1)S(1)}, bf16[32,256]{1,0:T(8,128)(2,1)S(1)}, bf16[32,256]{1,0:T(8,128)(2,1)S(1)}) custom-call(s32[2]{0:T(128)S(1)} %pad_add_fusion.2.info, bf16[1536,256]{1,0:T(8,128)(2,1)} %xl_own.1, bf16[1536,256]{1,0:T(8,128)(2,1)} %xl_own.1, ...), custom_call_target="tpu_custom_call" | custom-call | bytes 3000000 | tf_op jit(solution)/shard_map/pack/pallas_call | solution.py:96
  6.2 2.1 %coarse_rows.1 = bf16[64,8,512]{2,1,0:T(8,128)(2,1)} custom-call(s32[2]{0:T(128)S(1)} %pad_add_fusion.2.info, bf16[192,256]{1,0:T(8,128)(2,1)} %n_own.7, bf16[16,256]{1,0:T(8,128)(2,1)S(1)} %collective-permute-done.6.n_got, bf16[32,256]{1,0:T(8,128)(2,1)S(1)} %get-tuple-element.94.after), custom_call_target="tpu_custom_call" | custom-call | bytes 600000 | tf_op jit(solution)/shard_map/coarse_rows/pallas_call | solution.py:96
  8.3 14.0 %all-to-all-start = ((bf16[64,8,512]{2,1,0:T(8,128)(2,1)}), bf16[64,8,512]{2,1,0:T(8,128)(2,1)S(1)}, u32[]{:S(2)}, u32[]{:S(2)}) async-start(bf16[64,8,512]{2,1,0:T(8,128)(2,1)} %coarse_rows.1), calls=%async_computation | async-start | bytes 1048576 | tf_op jit(solution)/shard_map/all_to_all | solution.py:84
  22.4 2.8 %collective-permute-start.4 = (bf16[4,128,512]{2,1,0:T(8,128)(2,1)S(1)}, bf16[4,128,512]{2,1,0:T(8,128)(2,1)S(1)}, u32[]{:S(2)}, u32[]{:S(2)}) collective-permute-start(bf16[4,128,512]{2,1,0:T(8,128)(2,1)S(1)} %get-tuple-element.95), channel_id=1, source_target_pairs={{0,5},{1,4},{2,7},{3,6},{4,1},{5,0},{6,3},{7,2},{8,13},{9,12},{10,... | collective-permute-start | bytes 1572872 | tf_op jit(solution)/shard_map/ppermute | solution.py:78
  25.2 2.1 %collective-permute-start.1 = (bf16[32,256]{1,0:T(8,128)(2,1)S(1)}, bf16[32,256]{1,0:T(8,128)(2,1)S(1)}, u32[]{:S(2)}, u32[]{:S(2)}) collective-permute-start(bf16[32,256]{1,0:T(8,128)(2,1)S(1)} %get-tuple-element.93), channel_id=1, source_target_pairs={{0,2},{2,4},{4,6},{6,8},{8,10},{10,12},{12,14},{14,16},{16,18},{18... | collective-permute-start | bytes 49160 | tf_op jit(solution)/shard_map/ppermute | solution.py:69
  27.3 10.6 %collective-permute-done.1.low = bf16[32,256]{1,0:T(8,128)(2,1)S(1)} collective-permute-done((bf16[32,256]{1,0:T(8,128)(2,1)S(1)}, bf16[32,256]{1,0:T(8,128)(2,1)S(1)}, u32[]{:S(2)}, u32[]{:S(2)}) %collective-permute-start.1) | collective-permute-done | bytes 16416 | tf_op jit(solution)/shard_map/ppermute | solution.py:69
  37.9 4.7 %collective-permute-done.2.high = bf16[32,256]{1,0:T(8,128)(2,1)S(1)} collective-permute-done((bf16[32,256]{1,0:T(8,128)(2,1)S(1)}, bf16[32,256]{1,0:T(8,128)(2,1)S(1)}, u32[]{:S(2)}, u32[]{:S(2)}) %collective-permute-start.2) | collective-permute-done | bytes 16416 | tf_op jit(solution)/shard_map/ppermute | solution.py:69
  50.1 2.4 %edge_weights.1 = (bf16[3,512,512]{2,1,0:T(8,128)(2,1)S(1)}, bf16[512,512]{1,0:T(8,128)(2,1)S(1)}, bf16[3,128,512]{2,1,0:T(8,128)(2,1)S(1)}) custom-call(s32[2]{0:T(128)S(1)} %pad_add_fusion.2.info, bf16[3,256,512]{2,1,0:T(8,128)(2,1)} %wi.4, bf16[256,512]{1,0:T(8,128)(2,1)} %wo.4, bf16[4,128,512]{2,1,0:T(8,128)(2,1)} %copy-done, ...), custom_call_target="tpu_custom_call" | custom-call | bytes 7000000 | tf_op jit(solution)/shard_map/edge_weights/pallas_call | solution.py:96
  53.8 4.4 %edges_forward_fine.1 = (f32[576,512]{1,0:T(8,128)S(1)}, bf16[576,512]{1,0:T(8,128)(2,1)S(1)}, f32[576,512]{1,0:T(8,128)S(1)}, f32[576,1]{1,0:T(8,128)S(1)}, bf1...) custom-call(s32[2]{0:T(128)S(1)} %pad_add_fusion.2.info, ...), custom_call_target="tpu_custom_call" | custom-call | flops 1585446912 | bytes 8000000 | tf_op jit(solution)/shard_map/edges_forward_fine/pallas_call | solution.py:96
  58.6 3.1 %edges_forward_long.1 = (f32[192,512]{1,0:T(8,128)S(1)}, bf16[192,512]{1,0:T(8,128)(2,1)S(1)}, f32[192,512]{1,0:T(8,128)S(1)}, f32[192,1]{1,0:T(8,128)S(1)}, bf1...) custom-call(s32[2]{0:T(128)S(1)} %pad_add_fusion.2.info, ...), custom_call_target="tpu_custom_call" | custom-call | flops 1283457024 | bytes 6000000 | tf_op jit(solution)/shard_map/edges_forward_long/pallas_call | solution.py:96
  61.7 2.5 %collective-permute-done.10.rest_1_.got = bf16[192,512]{1,0:T(8,128)(2,1)S(1)} collective-permute-done((bf16[192,512]{1,0:T(8,128)(2,1)S(1)}, bf16[192,512]{1,0:T(8,128)(2,1)S(1)}, u32[]{:S(2)}, u32[]{:S(2)}) %collective-permute-start.10) | collective-permute-done | bytes 196640 | tf_op jit(solution)/shard_map/ppermute | solution.py:59
  67.7 1.8 %node_weights.1 = (bf16[2,512,512]{2,1,0:T(8,128)(2,1)S(1)}, bf16[512,512]{1,0:T(8,128)(2,1)S(1)}) custom-call(s32[2]{0:T(128)S(1)} %pad_add_fusion.2.info, bf16[2,256,512]{2,1,0:T(8,128)(2,1)} %wi.5, bf16[256,512]{1,0:T(8,128)(2,1)} %wo.5, bf16[3,128,512]{2,1,0:T(8,128)(2,1)S(1)} %gate.6.got, bf16[3,128,512]{2,1,0:T(8,128)(2,1)S(1)} %collective-permute-done.13.again), custom_call_target="tpu_custom_call" | custom-call | bytes 3000000 | tf_op jit(solution)/shard_map/node_weights/pallas_call | solution.py:96
  69.5 8.3 %nodes_and_edges_backward.1 = (bf16[192,256]{1,0:T(8,128)(2,1)}, f32[192,256]{1,0:T(8,128)S(1)}, bf16[1536,256]{1,0:T(8,128)(2,1)S(1)}, bf16[1536,256]{1,0:T(8,1...) custom-call(s32[2]{0:T(128)S(1)} %pad_add_fusion.2.info, ...), custom_call_target="tpu_custom_call" | custom-call | flops 1610612736 | bytes 14000000 | tf_op jit(solution)/shard_map/nodes_and_edges_backward/pallas_call | solution.py:96
  78.8 1.8 %collective-permute-done.19.got = bf16[1536,256]{1,0:T(8,128)(2,1)S(1)} collective-permute-done((bf16[1536,256]{1,0:T(8,128)(2,1)S(1)}, bf16[1536,256]{1,0:T(8,128)(2,1)S(1)}, u32[]{:S(2)}, u32[]{:S(2)}) %collective-permute-start.19) | collective-permute-done | bytes 786464 | tf_op jit(solution)/shard_map/ppermute | solution.py:64
  83.0 8.7 %collective-permute-done.20.first = bf16[768,256]{1,0:T(8,128)(2,1)S(1)} collective-permute-done((bf16[768,256]{1,0:T(8,128)(2,1)S(1)}, bf16[768,256]{1,0:T(8,128)(2,1)S(1)}, u32[]{:S(2)}, u32[]{:S(2)}) %collective-permute-start.20) | collective-permute-done | bytes 393248 | tf_op jit(solution)/shard_map/ppermute | solution.py:59
  92.9 2.0 %combine.1 = bf16[64,72,128]{2,1,0:T(8,128)(2,1)} custom-call(s32[2]{0:T(128)S(1)} %pad_add_fusion.2.info, bf16[2304,256]{1,0:T(8,128)(2,1)S(1)} %get-tuple-element.128.keep, bf16[2304,256]{1,0:T(8,128)(2,1)S(1)} %collective-permute-done.18.got, bf16[768,256]{1,0:T(8,128)(2,1)S(1)} %collective-permute-done.20.first, ...), custom_call_target="tpu_custom_call" | custom-call | bytes 4300000 | tf_op jit(solution)/shard_map/combine/pallas_call | solution.py:96
  94.9 10.2 %all-to-all-start.1 = ((bf16[64,72,128]{2,1,0:T(8,128)(2,1)}), bf16[64,72,128]{2,1,0:T(8,128)(2,1)S(1)}, u32[]{:S(2)}, u32[]{:S(2)}) async-start(bf16[64,72,128]{2,1,0:T(8,128)(2,1)} %combine.1), calls=%async_computation.1 | async-start | bytes 2359296 | tf_op jit(solution)/shard_map/all_to_all | solution.py:84
  105.2 2.8 %input_gradients.1 = (bf16[768,256]{1,0:T(8,128)(2,1)S(1)}, bf16[768,256]{1,0:T(8,128)(2,1)S(1)}, f32[256,256]{1,0:T(8,128)S(1)}, bf16[256,256]{1,0:T(8,128)(2,1)S(1)}) custom-call(s32[2]{0:T(128)S(1)} %pad_add_fusion.2.info, bf16[768,512]{1,0:T(8,128)(2,1)} %copy-done.4, bf16[1536,256]{1,0:T(8,128)(2,1)} %gl_own.3, bf16[1536,256]{1,0:T(8,128)(2,1)} %gl_own.3, ...), custom_call_target="tpu_custom_call" | custom-call | flops 805306368 | bytes 5000000 | tf_op jit(solution)/shard_map/input_gradients/pallas_call | solution.py:96
  111.1 3.3 %collective-permute-done.15 = bf16[256,256]{1,0:T(8,128)(2,1)S(1)} collective-permute-done((bf16[256,256]{1,0:T(8,128)(2,1)S(1)}, bf16[256,256]{1,0:T(8,128)(2,1)S(1)}, u32[]{:S(2)}, u32[]{:S(2)}) %collective-permute-start.15) | collective-permute-done | bytes 131104 | tf_op jit(solution)/shard_map/ppermute | solution.py:59
  115.2 6.0 %collective-permute-start.16 = (bf16[32,256]{1,0:T(8,128)(2,1)S(1)}, bf16[32,256]{1,0:T(8,128)(2,1)S(1)}, u32[]{:S(2)}, u32[]{:S(2)}) collective-permute-start(bf16[32,256]{1,0:T(8,128)(2,1)S(1)} %get-tuple-element.145), channel_id=1, source_target_pairs={{0,254},{2,0},{4,2},{6,4},{8,6},{10,8},{12,10},{14,12},{16,14},{18... | collective-permute-start | bytes 49160 | tf_op jit(solution)/shard_map/ppermute | solution.py:69
  121.2 2.4 %collective-permute-start.17 = (bf16[32,256]{1,0:T(8,128)(2,1)S(1)}, bf16[32,256]{1,0:T(8,128)(2,1)S(1)}, u32[]{:S(2)}, u32[]{:S(2)}) collective-permute-start(bf16[32,256]{1,0:T(8,128)(2,1)S(1)} %get-tuple-element.144), channel_id=1, source_target_pairs={{0,2},{2,4},{4,6},{6,8},{8,10},{10,12},{12,14},{14,16},{16,18},{18... | collective-permute-start | bytes 49160 | tf_op jit(solution)/shard_map/ppermute | solution.py:69
  123.6 6.1 %collective-permute-done.9.got = bf16[768,256]{1,0:T(8,128)(2,1)S(1)} collective-permute-done((bf16[768,256]{1,0:T(8,128)(2,1)S(1)}, bf16[768,256]{1,0:T(8,128)(2,1)S(1)}, u32[]{:S(2)}, u32[]{:S(2)}) %collective-permute-start.9) | collective-permute-done | bytes 393248 | tf_op jit(solution)/shard_map/ppermute | solution.py:59
  129.7 1.4 edge_output_rows.1.output
  131.2 3.9 %collective-permute-done.16 = bf16[32,256]{1,0:T(8,128)(2,1)S(1)} collective-permute-done((bf16[32,256]{1,0:T(8,128)(2,1)S(1)}, bf16[32,256]{1,0:T(8,128)(2,1)S(1)}, u32[]{:S(2)}, u32[]{:S(2)}) %collective-permute-start.16) | collective-permute-done | bytes 16416 | tf_op jit(solution)/shard_map/ppermute | solution.py:69
  137.8 8.8 %all-to-all-start.2 = ((bf16[64,56,128]{2,1,0:T(8,128)(2,1)}), bf16[64,56,128]{2,1,0:T(8,128)(2,1)S(1)}, u32[]{:S(2)}, u32[]{:S(2)}) async-start(bf16[64,56,128]{2,1,0:T(8,128)(2,1)} %copy-done.3), calls=%async_computation.2 | async-start | bytes 1835008 | tf_op jit(solution)/shard_map/all_to_all | solution.py:84
  147.3 15.2 %collective-permute-done.14.got = bf16[768,256]{1,0:T(8,128)(2,1)S(1)} collective-permute-done((bf16[768,256]{1,0:T(8,128)(2,1)S(1)}, bf16[768,256]{1,0:T(8,128)(2,1)S(1)}, u32[]{:S(2)}, u32[]{:S(2)}) %collective-permute-start.14) | collective-permute-done | bytes 393248 | tf_op jit(solution)/shard_map/ppermute | solution.py:59
  162.5 1.4 edge_gradient_rows.1.rest_0_
  164.6 6.3 %all-to-all-done.2.value = bf16[64,56,128]{2,1,0:T(8,128)(2,1)S(1)} async-done(((bf16[64,56,128]{2,1,0:T(8,128)(2,1)}), bf16[64,56,128]{2,1,0:T(8,128)(2,1)S(1)}, u32[]{:S(2)}, u32[]{:S(2)}) %all-to-all-start.2) | async-done | bytes 917536 | tf_op jit(solution)/shard_map/all_to_all | solution.py:84
  171.4 4.4 %collective-permute-start.22 = (bf16[2,1792,128]{2,1,0:T(8,128)(2,1)S(1)}, bf16[2,1792,128]{2,1,0:T(8,128)(2,1)S(1)}, u32[]{:S(2)}, u32[]{:S(2)}) collective-permute-start(bf16[2,1792,128]{2,1,0:T(8,128)(2,1)S(1)} %bitcast.15), channel_id=1, source_target_pairs={{0,2},{2,0},{4,6},{6,4},{8,10},{10,8},{12,14},{14,12},{16,18},{18,... | collective-permute-start | bytes 2752520 | tf_op jit(solution)/shard_map/ppermute | solution.py:64
  175.8 2.1 %collective-permute-done.22.other = bf16[2,1792,128]{2,1,0:T(8,128)(2,1)S(1)} collective-permute-done((bf16[2,1792,128]{2,1,0:T(8,128)(2,1)S(1)}, bf16[2,1792,128]{2,1,0:T(8,128)(2,1)S(1)}, u32[]{:S(2)}, u32[]{:S(2)}) %collective-permute-start.22) | collective-permute-done | bytes 917536 | tf_op jit(solution)/shard_map/ppermute | solution.py:64
  177.9 2.5 %results.1 = (f32[3,256,512]{2,1,0:T(8,128)}, f32[256,512]{1,0:T(8,128)}, f32[2,256,512]{2,1,0:T(8,128)}, f32[256,512]{1,0:T(8,128)}) custom-call(s32[2]{0:T(128)S(1)} %pad_add_fusion.2.info, bf16[2,1792,128]{2,1,0:T(8,128)(2,1)S(1)} %bitcast.16, bf16[2,1792,128]{2,1,0:T(8,128)(2,1)S(1)} %collective-permute-done.22.other), custom_call_target="tpu_custom_call" | custom-call | bytes 6000000 | tf_op jit(solution)/shard_map/results/pallas_call | solution.py:759
  (111 shorter events, 25.6 us)
Async XLA Ops:
  1.3 4.8 %collective-permute-start.6 = (bf16[16,256]{1,0:T(8,128)(2,1)S(1)}, bf16[16,256]{1,0:T(8,128)(2,1)S(1)}, u32[]{:S(2)}, u32[]{:S(2)}) collective-permute-start(bf16[16,256]{1,0:T(8,128)(2,1)S(1)} %slice.78), channel_id=1, source_target_pairs={{0,1},{1,0},{2,3},{3,2},{4,5},{5,4},{6,7},{7,6},{8,9},{9,8},{10,11... | collective-permute-start | bytes 24584 | tf_op jit(solution)/shard_map/ppermute | solution.py:59
  8.2 39.9 %copy-start.23 = (s32[12,128]{1,0:T(8,128)S(1)}, s32[12,128]{1,0:T(8,128)}, u32[]{:S(2)}) copy-start(s32[12,128]{1,0:T(8,128)} %param.19) | copy-start | bytes 18436
  8.2 39.9 %copy-start.24 = (s32[12,128]{1,0:T(8,128)S(1)}, s32[12,128]{1,0:T(8,128)}, u32[]{:S(2)}) copy-start(s32[12,128]{1,0:T(8,128)} %param.20) | copy-start | bytes 18436
  8.3 40.1 %all-to-all-start = ((bf16[64,8,512]{2,1,0:T(8,128)(2,1)}), bf16[64,8,512]{2,1,0:T(8,128)(2,1)S(1)}, u32[]{:S(2)}, u32[]{:S(2)}) async-start(bf16[64,8,512]{2,1,0:T(8,128)(2,1)} %coarse_rows.1), calls=%async_computation | async-start | bytes 1048576 | tf_op jit(solution)/shard_map/all_to_all | solution.py:84
  22.3 20.4 %collective-permute-start = (bf16[960,256]{1,0:T(8,128)(2,1)S(1)}, bf16[960,256]{1,0:T(8,128)(2,1)S(1)}, u32[]{:S(2)}, u32[]{:S(2)}) collective-permute-start(bf16[960,256]{1,0:T(8,128)(2,1)S(1)} %get-tuple-element.92), channel_id=1, source_target_pairs={{0,1},{1,0},{2,3},{3,2},{4,5},{5,4},{6,7},{7,6},{8,9},{9,8},{10,11... | collective-permute-start | bytes 1474568 | tf_op jit(solution)/shard_map/ppermute | solution.py:59
  22.4 23.8 %collective-permute-start.4 = (bf16[4,128,512]{2,1,0:T(8,128)(2,1)S(1)}, bf16[4,128,512]{2,1,0:T(8,128)(2,1)S(1)}, u32[]{:S(2)}, u32[]{:S(2)}) collective-permute-start(bf16[4,128,512]{2,1,0:T(8,128)(2,1)S(1)} %get-tuple-element.95), channel_id=1, source_target_pairs={{0,5},{1,4},{2,7},{3,6},{4,1},{5,0},{6,3},{7,2},{8,13},{9,12},{10,... | collective-permute-start | bytes 1572872 | tf_op jit(solution)/shard_map/ppermute | solution.py:78
  25.2 12.7 %collective-permute-start.1 = (bf16[32,256]{1,0:T(8,128)(2,1)S(1)}, bf16[32,256]{1,0:T(8,128)(2,1)S(1)}, u32[]{:S(2)}, u32[]{:S(2)}) collective-permute-start(bf16[32,256]{1,0:T(8,128)(2,1)S(1)} %get-tuple-element.93), channel_id=1, source_target_pairs={{0,2},{2,4},{4,6},{6,8},{8,10},{10,12},{12,14},{14,16},{16,18},{18... | collective-permute-start | bytes 49160 | tf_op jit(solution)/shard_map/ppermute | solution.py:69
  27.3 15.3 %collective-permute-start.2 = (bf16[32,256]{1,0:T(8,128)(2,1)S(1)}, bf16[32,256]{1,0:T(8,128)(2,1)S(1)}, u32[]{:S(2)}, u32[]{:S(2)}) collective-permute-start(bf16[32,256]{1,0:T(8,128)(2,1)S(1)} %get-tuple-element.94.after), channel_id=1, source_target_pairs={{0,254},{2,0},{4,2},{6,4},{8,6},{10,8},{12,10},{14,12},{16,14},{18... | collective-permute-start | bytes 49160 | tf_op jit(solution)/shard_map/ppermute | solution.py:69
  44.0 3.5 %collective-permute-start.3 = (bf16[64,256]{1,0:T(8,128)(2,1)S(1)}, bf16[64,256]{1,0:T(8,128)(2,1)S(1)}, u32[]{:S(2)}, u32[]{:S(2)}) collective-permute-start(bf16[64,256]{1,0:T(8,128)(2,1)S(1)} %gate.4), channel_id=1, source_target_pairs={{0,1},{1,0},{2,3},{3,2},{4,5},{5,4},{6,7},{7,6},{8,9},{9,8},{10,11... | collective-permute-start | bytes 98312 | tf_op jit(solution)/shard_map/ppermute | solution.py:59
  44.3 14.3 %collective-permute-start.8 = (bf16[960,256]{1,0:T(8,128)(2,1)}, bf16[960,256]{1,0:T(8,128)(2,1)S(1)}, u32[]{:S(2)}, u32[]{:S(2)}) collective-permute-start(bf16[960,256]{1,0:T(8,128)(2,1)} %get-tuple-element.99), channel_id=1, source_target_pairs={{0,1},{1,0},{2,3},{3,2},{4,5},{5,4},{6,7},{7,6},{8,9},{9,8},{10,11... | collective-permute-start | bytes 1474568 | tf_op jit(solution)/shard_map/ppermute | solution.py:59
  48.0 2.1 %collective-permute-start.5 = (bf16[4,128,512]{2,1,0:T(8,128)(2,1)S(1)}, bf16[4,128,512]{2,1,0:T(8,128)(2,1)}, u32[]{:S(2)}, u32[]{:S(2)}) collective-permute-start(bf16[4,128,512]{2,1,0:T(8,128)(2,1)S(1)} %gate.5.got), channel_id=1, source_target_pairs={{0,2},{2,0},{4,6},{6,4},{8,10},{10,8},{12,14},{14,12},{16,18},{18,... | collective-permute-start | bytes 1572872 | tf_op jit(solution)/shard_map/ppermute | solution.py:64
  48.3 10.3 %collective-permute-start.7 = (bf16[64,8,512]{2,1,0:T(8,128)(2,1)S(1)}, bf16[64,8,512]{2,1,0:T(8,128)(2,1)}, u32[]{:S(2)}, u32[]{:S(2)}) collective-permute-start(bf16[64,8,512]{2,1,0:T(8,128)(2,1)S(1)} %all-to-all-done), channel_id=1, source_target_pairs={{0,2},{2,0},{4,6},{6,4},{8,10},{10,8},{12,14},{14,12},{16,18},{18,... | collective-permute-start | bytes 1572872 | tf_op jit(solution)/shard_map/ppermute | solution.py:64
  52.5 11.9 %collective-permute-start.12 = (bf16[3,128,512]{2,1,0:T(8,128)(2,1)S(1)}, bf16[3,128,512]{2,1,0:T(8,128)(2,1)S(1)}, u32[]{:S(2)}, u32[]{:S(2)}) collective-permute-start(bf16[3,128,512]{2,1,0:T(8,128)(2,1)S(1)} %get-tuple-element.107), channel_id=1, source_target_pairs={{0,5},{1,4},{2,7},{3,6},{4,1},{5,0},{6,3},{7,2},{8,13},{9,12},{10,... | collective-permute-start | bytes 1179656 | tf_op jit(solution)/shard_map/ppermute | solution.py:78
  58.3 5.9 %collective-permute-start.10 = (bf16[192,512]{1,0:T(8,128)(2,1)S(1)}, bf16[192,512]{1,0:T(8,128)(2,1)S(1)}, u32[]{:S(2)}, u32[]{:S(2)}) collective-permute-start(bf16[192,512]{1,0:T(8,128)(2,1)S(1)} %get-tuple-element.104), channel_id=1, source_target_pairs={{0,1},{1,0},{2,3},{3,2},{4,5},{5,4},{6,7},{7,6},{8,9},{9,8},{10,11... | collective-permute-start | bytes 589832 | tf_op jit(solution)/shard_map/ppermute | solution.py:59
  64.9 2.7 %collective-permute-start.13 = (bf16[3,128,512]{2,1,0:T(8,128)(2,1)S(1)}, bf16[3,128,512]{2,1,0:T(8,128)(2,1)S(1)}, u32[]{:S(2)}, u32[]{:S(2)}) collective-permute-start(bf16[3,128,512]{2,1,0:T(8,128)(2,1)S(1)} %gate.6.got), channel_id=1, source_target_pairs={{0,2},{2,0},{4,6},{6,4},{8,10},{10,8},{12,14},{14,12},{16,18},{18,... | collective-permute-start | bytes 1179656 | tf_op jit(solution)/shard_map/ppermute | solution.py:64
  66.3 3.2 %collective-permute-start.11 = (bf16[16,512]{1,0:T(8,128)(2,1)S(1)}, bf16[16,512]{1,0:T(8,128)(2,1)S(1)}, u32[]{:S(2)}, u32[]{:S(2)}) collective-permute-start(bf16[16,512]{1,0:T(8,128)(2,1)S(1)} %get-tuple-element.106.rest_0_), channel_id=1, source_target_pairs={{0,1},{1,0},{2,3},{3,2},{4,5},{5,4},{6,7},{7,6},{8,9},{9,8},{10,11... | collective-permute-start | bytes 49160 | tf_op jit(solution)/shard_map/ppermute | solution.py:59
  77.9 15.1 %copy-start.10 = (bf16[192,512]{1,0:T(8,128)(2,1)}, bf16[192,512]{1,0:T(8,128)(2,1)S(1)}, u32[]{:S(2)}) copy-start(bf16[192,512]{1,0:T(8,128)(2,1)S(1)} %get-tuple-element.122.recv_sum) | copy-start | bytes 589828
  77.9 15.1 %copy-start.11 = (f32[192,256]{1,0:T(8,128)}, f32[192,256]{1,0:T(8,128)S(1)}, u32[]{:S(2)}) copy-start(f32[192,256]{1,0:T(8,128)S(1)} %get-tuple-element.125) | copy-start | bytes 589828
  77.9 2.7 %collective-permute-start.19 = (bf16[1536,256]{1,0:T(8,128)(2,1)S(1)}, bf16[1536,256]{1,0:T(8,128)(2,1)S(1)}, u32[]{:S(2)}, u32[]{:S(2)}) collective-permute-start(bf16[1536,256]{1,0:T(8,128)(2,1)S(1)} %get-tuple-element.131), channel_id=1, source_target_pairs={{0,2},{2,0},{4,6},{6,4},{8,10},{10,8},{12,14},{14,12},{16,18},{18,... | collective-permute-start | bytes 2359304 | tf_op jit(solution)/shard_map/ppermute | solution.py:64
  78.7 14.2 %collective-permute-start.18 = (bf16[2304,256]{1,0:T(8,128)(2,1)S(1)}, bf16[2304,256]{1,0:T(8,128)(2,1)S(1)}, u32[]{:S(2)}, u32[]{:S(2)}) collective-permute-start(bf16[2304,256]{1,0:T(8,128)(2,1)S(1)} %get-tuple-element.129), channel_id=1, source_target_pairs={{0,2},{2,0},{4,6},{6,4},{8,10},{10,8},{12,14},{14,12},{16,18},{18,... | collective-permute-start | bytes 3538952 | tf_op jit(solution)/shard_map/ppermute | solution.py:64
  81.3 10.4 %collective-permute-start.20 = (bf16[768,256]{1,0:T(8,128)(2,1)S(1)}, bf16[768,256]{1,0:T(8,128)(2,1)S(1)}, u32[]{:S(2)}, u32[]{:S(2)}) collective-permute-start(bf16[768,256]{1,0:T(8,128)(2,1)S(1)} %get-tuple-element.132), channel_id=1, source_target_pairs={{0,1},{1,0},{2,3},{3,2},{4,5},{5,4},{6,7},{7,6},{8,9},{9,8},{10,11... | collective-permute-start | bytes 1179656 | tf_op jit(solution)/shard_map/ppermute | solution.py:59
  81.7 11.2 %collective-permute-start.21 = (bf16[768,256]{1,0:T(8,128)(2,1)S(1)}, bf16[768,256]{1,0:T(8,128)(2,1)S(1)}, u32[]{:S(2)}, u32[]{:S(2)}) collective-permute-start(bf16[768,256]{1,0:T(8,128)(2,1)S(1)} %get-tuple-element.133), channel_id=1, source_target_pairs={{0,5},{1,4},{2,7},{3,6},{4,1},{5,0},{6,3},{7,2},{8,13},{9,12},{10,... | collective-permute-start | bytes 1179656 | tf_op jit(solution)/shard_map/ppermute | solution.py:78
  94.9 40.7 %all-to-all-start.1 = ((bf16[64,72,128]{2,1,0:T(8,128)(2,1)}), bf16[64,72,128]{2,1,0:T(8,128)(2,1)S(1)}, u32[]{:S(2)}, u32[]{:S(2)}) async-start(bf16[64,72,128]{2,1,0:T(8,128)(2,1)} %combine.1), calls=%async_computation.1 | async-start | bytes 2359296 | tf_op jit(solution)/shard_map/all_to_all | solution.py:84
  109.5 20.2 %copy-start.8 = (bf16[576,256]{1,0:T(8,128)(2,1)S(1)}, bf16[576,256]{1,0:T(8,128)(2,1)}, u32[]{:S(2)}) copy-start(bf16[576,256]{1,0:T(8,128)(2,1)} %copy-done.7) | copy-start | bytes 884740
  109.5 4.9 %collective-permute-start.15 = (bf16[256,256]{1,0:T(8,128)(2,1)S(1)}, bf16[256,256]{1,0:T(8,128)(2,1)S(1)}, u32[]{:S(2)}, u32[]{:S(2)}) collective-permute-start(bf16[256,256]{1,0:T(8,128)(2,1)S(1)} %get-tuple-element.127), channel_id=1, source_target_pairs={{0,1},{1,0},{2,3},{3,2},{4,5},{5,4},{6,7},{7,6},{8,9},{9,8},{10,11... | collective-permute-start | bytes 393224 | tf_op jit(solution)/shard_map/ppermute | solution.py:59
  110.4 19.3 %collective-permute-start.9 = (bf16[768,256]{1,0:T(8,128)(2,1)S(1)}, bf16[768,256]{1,0:T(8,128)(2,1)S(1)}, u32[]{:S(2)}, u32[]{:S(2)}) collective-permute-start(bf16[768,256]{1,0:T(8,128)(2,1)S(1)} %pad_maximum_fusion), channel_id=1, source_target_pairs={{0,1},{1,0},{2,3},{3,2},{4,5},{5,4},{6,7},{7,6},{8,9},{9,8},{10,11... | collective-permute-start | bytes 1179656 | tf_op jit(solution)/shard_map/ppermute | solution.py:59
  115.2 19.9 %collective-permute-start.16 = (bf16[32,256]{1,0:T(8,128)(2,1)S(1)}, bf16[32,256]{1,0:T(8,128)(2,1)S(1)}, u32[]{:S(2)}, u32[]{:S(2)}) collective-permute-start(bf16[32,256]{1,0:T(8,128)(2,1)S(1)} %get-tuple-element.145), channel_id=1, source_target_pairs={{0,254},{2,0},{4,2},{6,4},{8,6},{10,8},{12,10},{14,12},{16,14},{18... | collective-permute-start | bytes 49160 | tf_op jit(solution)/shard_map/ppermute | solution.py:69
  121.2 13.9 %collective-permute-start.17 = (bf16[32,256]{1,0:T(8,128)(2,1)S(1)}, bf16[32,256]{1,0:T(8,128)(2,1)S(1)}, u32[]{:S(2)}, u32[]{:S(2)}) collective-permute-start(bf16[32,256]{1,0:T(8,128)(2,1)S(1)} %get-tuple-element.144), channel_id=1, source_target_pairs={{0,2},{2,4},{4,6},{6,8},{8,10},{10,12},{12,14},{14,16},{16,18},{18... | collective-permute-start | bytes 49160 | tf_op jit(solution)/shard_map/ppermute | solution.py:69
  137.8 24.7 %copy-start.2 = (bf16[768,256]{1,0:T(8,128)(2,1)S(1)}, bf16[768,256]{1,0:T(8,128)(2,1)}, u32[]{:S(2)}) copy-start(bf16[768,256]{1,0:T(8,128)(2,1)} %copy-done.1) | copy-start | bytes 1179652
  137.8 33.1 %all-to-all-start.2 = ((bf16[64,56,128]{2,1,0:T(8,128)(2,1)}), bf16[64,56,128]{2,1,0:T(8,128)(2,1)S(1)}, u32[]{:S(2)}, u32[]{:S(2)}) async-start(bf16[64,56,128]{2,1,0:T(8,128)(2,1)} %copy-done.3), calls=%async_computation.2 | async-start | bytes 1835008 | tf_op jit(solution)/shard_map/all_to_all | solution.py:84
  146.6 15.9 %collective-permute-start.14 = (bf16[768,256]{1,0:T(8,128)(2,1)S(1)}, bf16[768,256]{1,0:T(8,128)(2,1)S(1)}, u32[]{:S(2)}, u32[]{:S(2)}) collective-permute-start(bf16[768,256]{1,0:T(8,128)(2,1)S(1)} %copy-done.20), channel_id=1, source_target_pairs={{0,1},{1,0},{2,3},{3,2},{4,5},{5,4},{6,7},{7,6},{8,9},{9,8},{10,11... | collective-permute-start | bytes 1179656 | tf_op jit(solution)/shard_map/ppermute | solution.py:59
  171.4 6.5 %collective-permute-start.22 = (bf16[2,1792,128]{2,1,0:T(8,128)(2,1)S(1)}, bf16[2,1792,128]{2,1,0:T(8,128)(2,1)S(1)}, u32[]{:S(2)}, u32[]{:S(2)}) collective-permute-start(bf16[2,1792,128]{2,1,0:T(8,128)(2,1)S(1)} %bitcast.15), channel_id=1, source_target_pairs={{0,2},{2,0},{4,6},{6,4},{8,10},{10,8},{12,14},{14,12},{16,18},{18,... | collective-permute-start | bytes 2752520 | tf_op jit(solution)/shard_map/ppermute | solution.py:64
  (19 other events, 114.8 us)
